TPU v7x, 256 devices: a whole 4x4x8 slice. The times are simulated.
256 devices in a mesh: vocab: 32 (over y, x, core), rep: 8 (over z).
Axes of the slice: x: 4, y: 4, z: 8, core: 2. Of those that a mesh axis runs over, the one named last changes fastest.
Arguments:
- token_grads: bfloat16 [32768, 16384], P(('vocab', 'rep')), may hold values from -6 to 6
- token_slots: int32 [32768], P(('vocab', 'rep')), may hold values from 0 to 63, as said below
- touched_ids: int32 [16384], P(('vocab', 'rep')), may hold values from 0 to 4095, as said below
- table: float32 [4096, 16384], P('vocab', 'rep'), may hold values from -6 to 6
- first_moment: float32 [4096, 16384], P('vocab', 'rep'), may hold values from -1.75 to 1.75
- second_moment: float32 [4096, 16384], P('vocab', 'rep'), may hold values from 0.01 to 1
Outputs:
- new_table: float32 [4096, 16384], P('vocab', 'rep')
- new_first: float32 [4096, 16384], P('vocab', 'rep')
- new_second: float32 [4096, 16384], P('vocab', 'rep')
- refreshed: bfloat16 [16384, 16384], P(('vocab', 'rep'))
Inputs may be any that keep to these rules, and one draw needn't show every extreme that they name: `touched_ids`: each block of 64 entries is strictly ascending. Owner k holds rows k * 128 to (k + 1) * 128 - 1; at most 4 entries of one block fall in one owner's rows, and in every draw one owner receives exactly 4 from every block. `token_slots`: within each block of 128 tokens every position 0 to 63 is named at least once.
All inputs are finite; a program needn't handle non-finite values.
Results may differ from a plain program's by a relative error of at most 0.001.
Values may be sent and summed in bfloat16 or wider, within the bound.
No kernel may reach another device: no remote copies, remote signals or barrier semaphores. Data moves between devices by JAX's collectives and lax.ppermute only.
A program may use at most 128 MiB of HBM per device.

v0:
```python
import jax
import jax.numpy as jnp
from jax import lax
from jax.sharding import PartitionSpec as P

STEP = 4


decay_first = 0.9
decay_second = 0.95
learn_rate = 0.03
epsilon = 1e-08


def adam_step(table, first_moment, second_moment, gradient):
    new_first = decay_first * first_moment + (1.0 - decay_first) * gradient
    new_second = decay_second * second_moment + (1.0 - decay_second) * gradient * gradient
    scaled_first = new_first / (1.0 - decay_first**STEP)
    scaled_second = new_second / (1.0 - decay_second**STEP)
    new_table = table - learn_rate * scaled_first / (jnp.sqrt(scaled_second) + epsilon)
    return (new_table, new_first, new_second)


def shards(token_grads, token_slots, touched_ids, table, first_moment, second_moment):
    owner_count = lax.axis_size("vocab")
    replica_count = lax.axis_size("rep")
    touched_count = touched_ids.shape[0]
    owned_rows = table.shape[0]
    column_width = table.shape[1]
    full_width = token_grads.shape[1]
    capacity = 2 * touched_count // owner_count
    positions = jnp.arange(touched_count, dtype=jnp.int32)
    membership = (token_slots[None, :] == positions[:, None]).astype(jnp.bfloat16)
    summed = jnp.dot(membership, token_grads, preferred_element_type=jnp.float32)
    owner_of = touched_ids // owned_rows
    owners = jnp.arange(owner_count, dtype=jnp.int32)
    counts = jnp.sum((owner_of[None, :] == owners[:, None]).astype(jnp.int32), axis=1)
    starts = jnp.cumsum(counts) - counts
    offset = jnp.arange(capacity, dtype=jnp.int32)
    filled = offset[None, :] < counts[:, None]
    source = jnp.minimum(starts[:, None] + offset[None, :], touched_count - 1)
    outgoing = jnp.where(filled[:, :, None], jnp.take(summed, source, axis=0), 0.0)
    outgoing = outgoing.reshape(owner_count, capacity, replica_count, column_width)
    local_rows = jnp.where(
        filled, jnp.take(touched_ids, source, axis=0) - owners[:, None] * owned_rows, -1
    )
    row_tags = jnp.broadcast_to(
        local_rows[:, :, None, None], (owner_count, capacity, replica_count, 1)
    )
    arrived, arrived_tags = (
        lax.all_to_all(
            lax.all_to_all(outgoing, "vocab", split_axis=0, concat_axis=0, tiled=True),
            "rep",
            split_axis=2,
            concat_axis=2,
            tiled=True,
        ),
        lax.all_to_all(
            lax.all_to_all(row_tags, "vocab", split_axis=0, concat_axis=0, tiled=True),
            "rep",
            split_axis=2,
            concat_axis=2,
            tiled=True,
        ),
    )
    stacked = arrived.reshape(-1, column_width)
    stacked_tags = arrived_tags.reshape(-1)
    placer = (jnp.arange(owned_rows, dtype=jnp.int32)[:, None] == stacked_tags[None, :]).astype(
        jnp.float32
    )
    gradient = jnp.dot(
        placer, stacked, precision=lax.Precision.HIGHEST, preferred_element_type=jnp.float32
    )
    new_table, new_first, new_second = adam_step(table, first_moment, second_moment, gradient)
    new_half = new_table.astype(jnp.bfloat16)
    wanted = lax.all_gather(touched_ids, "rep", axis=0, tiled=True)
    wanted = wanted.reshape(replica_count, touched_count).T
    initial = jnp.zeros((touched_count, replica_count, column_width), jnp.bfloat16)
    shard_rows = lax.all_gather(new_half, "vocab", axis=0, tiled=True)
    inside = (wanted >= 0) & (wanted < shard_rows.shape[0])
    looked = jnp.take(shard_rows, jnp.clip(wanted, 0, shard_rows.shape[0] - 1), axis=0)
    picked = jnp.where(inside[:, :, None], looked, initial)
    returned = lax.all_to_all(picked, "rep", split_axis=1, concat_axis=1, tiled=True)
    refreshed = returned.reshape(touched_count, full_width)
    return (new_table, new_first, new_second, refreshed)


def solution(mesh):
    return jax.shard_map(
        shards,
        mesh=mesh,
        in_specs=(
            P(("vocab", "rep"), None),
            P(("vocab", "rep")),
            P(("vocab", "rep")),
            P("vocab", "rep"),
            P("vocab", "rep"),
            P("vocab", "rep"),
        ),
        out_specs=(
            P("vocab", "rep"),
            P("vocab", "rep"),
            P("vocab", "rep"),
            P(("vocab", "rep"), None),
        ),
        check_vma=False,
    )
```

profile of v0, /device:TPU:2, one launch (start us, length us, event | category | flops | bytes accessed | tf_op | source)
XLA Modules:
  0.0 556.9 jit_solution(2312549432276390628)
XLA Ops:
  7.2 0.7 and_select_fusion
  7.9 0.1 convert_reduce_fusion
  8.2 0.1 reduce
  8.4 0.1 reshape.218
  8.5 1.2 gather_fusion
  9.9 0.7 broadcast_in_dim.75
  10.7 7.6 %all-to-all-start = ((s32[32,4,8,1]{2,1,3,0:T(4,128)}), s32[32,4,8,1]{2,1,3,0:T(4,128)S(1)}, u32[]{:S(2)}, u32[]{:S(2)}) async-start(s32[32,4,8,1]{2,1,3,0:T(4,128)} %broadcast_in_dim.75), calls=%async_computation | async-start | bytes 131072 | tf_op jit(solution)/shard_map/all_to_all | solution.py:59
  18.4 4.8 fusion.5
  23.2 11.8 %gather_fusion.1 = f32[128,16384]{1,0:T(8,128)} fusion(f32[64,16384]{1,0:T(8,128)} %fusion.5, s32[1024]{0:T(1024)S(1)} %pad_clamp_fusion.1), kind=kCustom, calls=%fused_computation.1 | custom fusion | bytes 16777728 | tf_op jit(solution)/shard_map/jit(_take)/gather | solution.py:42
  35.1 14.1 %copy.48 = f32[16,8,8,2048]{3,2,1,0:T(8,128)} copy(f32[16,8,8,2048]{3,1,2,0:T(8,128)} %bitcast.22) | data formatting | bytes 16777216
  49.1 15.3 %fusion = f32[32,4,8,2048]{3,1,2,0:T(4,128)} fusion(f32[32,4,8,2048]{3,2,1,0:T(8,128)} %bitcast.24, pred[32,4]{1,0:T(8,128)(4,1)S(1)} %get-tuple-element.9, pred[32,4]{1,0:T(8,128)(4,1)S(1)} %get-tuple-element.8), kind=kLoop, calls=%fused_computation.4 | loop fusion | flops 4194304 | bytes 16777472 | tf_op jit(solution)/shard_map/jit(_where)/select_n | solution.py:42
  64.5 7.4 %all-to-all-start.2 = ((f32[32,4,8,2048]{3,1,2,0:T(4,128)}), f32[32,4,8,2048]{3,1,2,0:T(4,128)}, u32[]{:S(2)}, u32[]{:S(2)}) async-start(f32[32,4,8,2048]{3,1,2,0:T(4,128)} %fusion), calls=%async_computation.2 | async-start | bytes 16777216 | tf_op jit(solution)/shard_map/all_to_all | solution.py:52
  72.0 0.7 reshape.251
  72.7 98.9 %all-to-all-done.2 = f32[32,4,8,2048]{3,1,2,0:T(4,128)} async-done(((f32[32,4,8,2048]{3,1,2,0:T(4,128)}), f32[32,4,8,2048]{3,1,2,0:T(4,128)}, u32[]{:S(2)}, u32[]{:S(2)}) %all-to-all-start.2) | async-done | bytes 8388640 | tf_op jit(solution)/shard_map/all_to_all | solution.py:52
  171.5 8.5 %all-to-all-start.1 = ((s32[8,1,128]{2,1,0:T(1,128)}), s32[8,1,128]{2,1,0:T(1,128)S(1)}, u32[]{:S(2)}, u32[]{:S(2)}) async-start(s32[8,1,128]{2,1,0:T(1,128)} %reshape.251), calls=%async_computation.1 | async-start | bytes 8192 | tf_op jit(solution)/shard_map/all_to_all | solution.py:58
  180.0 10.3 %copy.42 = f32[32,4,8,2048]{3,1,0,2:T(4,128)} copy(f32[32,4,8,2048]{3,1,2,0:T(4,128)} %all-to-all-done.2) | data formatting | bytes 16777216 | tf_op jit(solution)/shard_map/all_to_all | solution.py:52
  190.3 7.2 %all-to-all-start.3 = ((f32[32,4,8,2048]{3,1,0,2:T(4,128)}), f32[32,4,8,2048]{3,1,0,2:T(4,128)}, u32[]{:S(2)}, u32[]{:S(2)}) async-start(f32[32,4,8,2048]{3,1,0,2:T(4,128)} %copy.42), calls=%async_computation.3 | async-start | bytes 16777216 | tf_op jit(solution)/shard_map/all_to_all | solution.py:51
  197.5 0.2 all-gather.2.cloned.1.call-start
  197.8 0.5 broadcast.204
  198.3 0.7 reduce.1
  199.1 0.1 eq.45
  199.3 183.8 %all-to-all-done.3 = f32[32,4,8,2048]{3,1,0,2:T(4,128)} async-done(((f32[32,4,8,2048]{3,1,0,2:T(4,128)}), f32[32,4,8,2048]{3,1,0,2:T(4,128)}, u32[]{:S(2)}, u32[]{:S(2)}) %all-to-all-start.3) | async-done | bytes 8388640 | tf_op jit(solution)/shard_map/all_to_all | solution.py:51
  383.0 11.0 %copy.43 = f32[32,4,8,2048]{3,2,1,0:T(8,128)S(1)} copy(f32[32,4,8,2048]{3,1,0,2:T(4,128)} %all-to-all-done.3) | data formatting | bytes 16777216 | tf_op jit(solution)/shard_map/all_to_all | solution.py:51
  394.1 6.0 %fusion.10 = (bf16[128,2048]{1,0:T(8,128)(2,1)}, f32[128,2048]{1,0:T(8,128)}, f32[128,2048]{1,0:T(8,128)}, f32[128,2048]{1,0:T(8,128)}) fusion(f32[128,2048]{1,0:T(8,128)S(1)} %copy-done.1, f32[128,2048]{1,0:T(8,128)S(1)} %copy-done.2, f32[128,2048]{1,0:T(8,128)S(1)} %copy-done.3, f32[1024,2048]{1,0:T(8,128)S(1)} %bitcast.23, s32[1024]{0:T(1024)S(1)} %eq.45), kind=kOutput, calls=%fused_computation.37 | convolution fusion | flops 3224764416 | bytes 15208448 | tf_op jit(solution)/shard_map/dot_general | solution.py:71
  400.2 0.6 dynamic-slice
  401.4 0.2 dynamic-update-slice
  401.7 9.4 %all-reduce = s32[512]{0:T(512)S(1)} all-reduce(s32[512]{0:T(512)S(1)} %dynamic-update-slice), channel_id=1, replica_groups=mesh['vocab'=32,'rep'=8] {'rep'}, use_global_device_ids=true, to_apply=%add | all-reduce | flops 512 | bytes 4096
  411.5 63.5 %all-gather.2.cloned.1.call-done = bf16[4096,2048]{1,0:T(8,128)(2,1)} async-done(((bf16[128,2048]{1,0:T(8,128)(2,1)}), bf16[4096,2048]{1,0:T(8,128)(2,1)}) %all-gather.2.cloned.1.call-update) | async-done | bytes 16777232 | tf_op jit(solution)/shard_map/all_gather | solution.py:79
  474.9 12.3 %gather_fusion.2 = bf16[512,2048]{1,0:T(8,128)(2,1)S(1)} fusion(bf16[4096,2048]{1,0:T(8,128)(2,1)} %all-gather.2.cloned.1.call-done, s32[1024]{0:T(1024)S(1)} %pad_clamp_fusion), kind=kCustom, calls=%fused_computation.2 | custom fusion | bytes 4196352 | tf_op jit(solution)/shard_map/jit(_take)/gather | solution.py:81
  487.3 2.6 fusion.1
  489.9 58.4 %all_to_all.25 = bf16[64,8,2048]{2,0,1:T(8,128)(2,1)S(1)} all-to-all(bf16[64,8,2048]{2,0,1:T(8,128)(2,1)S(1)} %fusion.1), channel_id=1, replica_groups=mesh['vocab'=32,'rep'=8] {'rep'}, dimensions={1} | all-to-all | bytes 4194304 | tf_op jit(solution)/shard_map/all_to_all | solution.py:83
  548.3 1.5 copy.47
  (37 shorter events, 1.2 us)
Async XLA Ops:
  7.2 1.3 copy-start
  8.5 9.9 %copy-start.4 = (s32[128]{0:T(128)S(1)}, s32[128]{0:T(128)}, u32[]{:S(2)}) copy-start(s32[128]{0:T(128)} %param.7) | copy-start | bytes 1540
  10.7 53.8 %all-to-all-start = ((s32[32,4,8,1]{2,1,3,0:T(4,128)}), s32[32,4,8,1]{2,1,3,0:T(4,128)S(1)}, u32[]{:S(2)}, u32[]{:S(2)}) async-start(s32[32,4,8,1]{2,1,3,0:T(4,128)} %broadcast_in_dim.75), calls=%async_computation | async-start | bytes 131072 | tf_op jit(solution)/shard_map/all_to_all | solution.py:59
  64.5 107.1 %all-to-all-start.2 = ((f32[32,4,8,2048]{3,1,2,0:T(4,128)}), f32[32,4,8,2048]{3,1,2,0:T(4,128)}, u32[]{:S(2)}, u32[]{:S(2)}) async-start(f32[32,4,8,2048]{3,1,2,0:T(4,128)} %fusion), calls=%async_computation.2 | async-start | bytes 16777216 | tf_op jit(solution)/shard_map/all_to_all | solution.py:52
  171.5 18.8 %all-to-all-start.1 = ((s32[8,1,128]{2,1,0:T(1,128)}), s32[8,1,128]{2,1,0:T(1,128)S(1)}, u32[]{:S(2)}, u32[]{:S(2)}) async-start(s32[8,1,128]{2,1,0:T(1,128)} %reshape.251), calls=%async_computation.1 | async-start | bytes 8192 | tf_op jit(solution)/shard_map/all_to_all | solution.py:58
  190.3 192.7 %all-to-all-start.3 = ((f32[32,4,8,2048]{3,1,0,2:T(4,128)}), f32[32,4,8,2048]{3,1,0,2:T(4,128)}, u32[]{:S(2)}, u32[]{:S(2)}) async-start(f32[32,4,8,2048]{3,1,0,2:T(4,128)} %copy.42), calls=%async_computation.3 | async-start | bytes 16777216 | tf_op jit(solution)/shard_map/all_to_all | solution.py:51
  197.5 277.4 %all-gather.2.cloned.1.call-start = ((), (), s32[]{:S(2)}) async-start(), calls=%async_computation.5 | async-start | bytes 17301504 | tf_op jit(solution)/shard_map/all_gather | solution.py:79
  199.2 194.9 %copy-start.1 = (f32[128,2048]{1,0:T(8,128)S(1)}, f32[128,2048]{1,0:T(8,128)}, u32[]{:S(2)}) copy-start(f32[128,2048]{1,0:T(8,128)} %param.9) | copy-start | bytes 3145732
  199.2 194.9 %copy-start.2 = (f32[128,2048]{1,0:T(8,128)S(1)}, f32[128,2048]{1,0:T(8,128)}, u32[]{:S(2)}) copy-start(f32[128,2048]{1,0:T(8,128)} %param.10) | copy-start | bytes 3145732
  199.2 194.9 %copy-start.3 = (f32[128,2048]{1,0:T(8,128)S(1)}, f32[128,2048]{1,0:T(8,128)}, u32[]{:S(2)}) copy-start(f32[128,2048]{1,0:T(8,128)} %param.11) | copy-start | bytes 3145732
  394.1 6.1 %copy-start.5 = (u32[256]{0:T(256)S(1)}, u32[256]{0:T(256)}, u32[]{:S(2)}) copy-start(u32[256]{0:T(256)} %constant.97) | copy-start | bytes 3076
Sparse Core Ops, SparseCore 0:
  400.3 74.5 all-gather.1
where the time goes:
time: 567 us; the launch traced here: 557 us
  waiting for transfers between devices  346 us (61%)
  blocking collectives  67.8 us (12%)
  local copies, waits for them, and re-layouts  66.1 us (12%)
  starting transfers between devices  30.9 us (5%)
  other arithmetic  19.9 us (4%)
  between operations  15.1 us (3%)
  matrix products  10.9 us (2%)
    all_to_all x1, waiting for transfers between devices, shards(): lax.all_to_all(lax.all_to_all(outgoing, 'vocab', split_axis=0, concat_axi...  184 us
    all_to_all x1, waiting for transfers between devices, shards(): lax.all_to_all(outgoing, 'vocab', split_axis=0, concat_axis=0, tiled=True)  98.9 us
    all_gather x1, waiting for transfers between devices, shards(): shard_rows = lax.all_gather(new_half, 'vocab', axis=0, tiled=True)  63.5 us
    all_to_all x1, blocking collectives, shards(): lax.all_to_all(picked, 'rep', split_axis=1, concat_axis=1, tiled=True)  58.4 us
    unnamed x18, local copies, waits for them, and re-layouts  15.7 us
    select_n x1, other arithmetic, shards(): jnp.where(filled[:, :, None], jnp.take(summed, source, axis=0), 0.0)  15.3 us
    gather x1, local copies, waits for them, and re-layouts, shards(): jnp.take(shard_rows, jnp.clip(wanted, 0, shard_rows.shape[0] - 1), axis=0)  12.3 us
    gather x1, local copies, waits for them, and re-layouts, shards(): jnp.take(summed, source, axis=0)  11.8 us
  transfers between devices with their start and end apart: 5, of which 3 were waited for; matrix products, arithmetic and copies ran while one was open for 11% of the time, Pallas kernels for 0%

commit v1 on v0

v1 whole, which is shorter than its diff:
```python
import functools
import jax
import jax.numpy as jnp
from jax import lax
from jax.experimental import pallas as pl
from jax.experimental.pallas import tpu as pltpu
from jax.sharding import PartitionSpec as P

STEP = 4
decay_first = 0.9
decay_second = 0.95
learn_rate = 0.03
epsilon = 1e-08

CAP = 4
STEP_COLUMNS = 256
SUB, LANES = 8, 128
f32, bf16, i32 = jnp.float32, jnp.bfloat16, jnp.int32
sds = jax.ShapeDtypeStruct
ANY = pl.BlockSpec(memory_space=pl.ANY)


def iota(shape, dim):
    return lax.broadcasted_iota(i32, shape, dim)


def ones(hit):
    return jnp.where(hit, 1.0, 0.0).astype(bf16)


def whole(shape):
    return pl.BlockSpec(shape, lambda *_: (0,) * len(shape))


def call(body, name, out_shape, grid, in_specs, out_specs, flops, nbytes, aliases=None, scratch=()):
    return pl.pallas_call(
        body,
        out_shape=out_shape,
        grid_spec=pltpu.PrefetchScalarGridSpec(
            num_scalar_prefetch=1,
            grid=grid,
            in_specs=in_specs,
            out_specs=out_specs,
            scratch_shapes=scratch,
        ),
        input_output_aliases=aliases or {},
        compiler_params=pltpu.CompilerParams(vmem_limit_bytes=32 << 20),
        cost_estimate=pl.CostEstimate(flops=flops, bytes_accessed=nbytes, transcendentals=0),
        name=name,
    )


def parts_dot(onehot, values, contract):
    total = None
    for step in range(3):
        part = values.astype(bf16)
        if step < 2:
            values = values - part.astype(f32)
        term = lax.dot_general(onehot, part, ((contract, (0,)), ((), ())), preferred_element_type=f32)
        total = term if total is None else total + term
    return total


def positions(ids_row, owned):
    n = ids_row.shape[1]
    ids = jnp.broadcast_to(ids_row, (n, n))
    at, along = iota((n, n), 0), iota((n, n), 1)
    owner_row = ids // owned
    ids_col = jnp.sum(jnp.where(at == along, ids, 0), axis=1, keepdims=True)
    owner_col = jnp.broadcast_to(ids_col // owned, (n, n))
    same = owner_row == owner_col
    rank_row = jnp.sum(jnp.where(same & (at < along), 1, 0), axis=0, keepdims=True)
    rank_col = jnp.sum(jnp.where(same & (along < at), 1, 0), axis=1, keepdims=True)
    return owner_row[:1] * CAP + rank_row, owner_col[:, :1] * CAP + rank_col


def sums_kernel(reps, me_ref, slots_ref, ids_ref, *refs):
    ins, outs = refs[:reps], refs[reps:]
    n, tokens = ids_ref.shape[1], slots_ref.shape[1]
    wa = ins[0].shape[1]
    member = ones(jnp.broadcast_to(slots_ref[...], (n, tokens)) == iota((n, tokens), 0))
    names = jnp.broadcast_to(ids_ref[...], (SUB, n)).astype(f32)
    for i, o in zip(ins, outs):
        total = jnp.dot(member, i[...], preferred_element_type=f32)
        for g in range(n // SUB):
            o[:, g * wa : (g + 1) * wa] = total[g * SUB : (g + 1) * SUB]
        o[:, n // SUB * wa : n // SUB * wa + LANES] = jnp.zeros((SUB, LANES), f32)
        o[:, n // SUB * wa : n // SUB * wa + n] = names


def tags_of(row_at, ids_row, places_row, owned):
    hit = row_at == places_row
    return jnp.sum(jnp.where(hit, ids_row % owned + 1, 0), axis=1, keepdims=True) - 1


def send_kernel(owned, me_ref, slots_ref, ids_ref, *refs):
    ins, (out_ref, buf, sems) = refs[:-3], refs[-3:]
    half, wb = len(ins) // 2, ins[0].shape[1]
    rows, tokens, n = buf.shape[0], slots_ref.shape[1], ids_ref.shape[1]
    place_row, place_col = positions(ids_ref[...], owned)
    slot = jnp.broadcast_to(slots_ref[...], (n, tokens))
    of_token = jnp.sum(
        jnp.where(slot == iota((n, tokens), 0), place_col, 0), axis=0, keepdims=True
    )
    row = iota((rows, tokens), 0)
    hit = (row // (2 * CAP) * CAP + row % CAP) == of_token
    upper = row // CAP % 2
    member = [ones(hit & (upper == h)) for h in range(2)]
    row = iota((rows, n), 0)
    tag = tags_of(row // (2 * CAP) * CAP + row % CAP, ids_ref[...], place_row, owned)
    copies = []
    for i in range(half + 1):
        at = pl.ds(i * wb, wb if i < half else LANES)
        if i < half:
            buf[:, at] = jnp.dot(member[0], ins[i][...], preferred_element_type=f32) + jnp.dot(
                member[1], ins[half + i][...], preferred_element_type=f32
            )
        else:
            buf[:, at] = jnp.broadcast_to(tag, (rows, LANES)).astype(f32)
        copies.append(pltpu.make_async_copy(buf.at[:, at], out_ref.at[:, at], sems.at[i]))
        copies[-1].start()
    for copy in copies:
        copy.wait()


def route_kernel(owned, wa, me_ref, *refs):
    ins, (out_ref, buf, sems) = refs[:-3], refs[-3:]
    owners = buf.shape[0]
    n = (ins[0].shape[1] - LANES) // wa * SUB
    pairs = len(ins) // 2
    rows = owners * 2 * CAP
    tags = jnp.zeros((rows, LANES), i32)
    copies = []
    for pair in range(pairs):
        hits, blocks, tag = [], [], 0
        for t in range(2):
            x = ins[2 * pair + t]
            ids_row = x[:1, n // SUB * wa : n // SUB * wa + n].astype(i32)
            place_row, _ = positions(ids_row, owned)
            at = iota((rows, n), 0)
            here = jnp.where(at // CAP % 2 == t, at // (2 * CAP) * CAP + at % CAP, -1)
            hits.append(ones(here == place_row))
            tag = tag + tags_of(here, ids_row, place_row, owned) + 1
            blocks.append(x)
        tags = jnp.where(iota((rows, LANES), 1) == pair, tag - 1, tags)
        onehot = jnp.concatenate(hits, axis=1)
        for c in range(wa // STEP_COLUMNS):
            values = jnp.concatenate(
                [
                    x[:, g * wa + c * STEP_COLUMNS : g * wa + (c + 1) * STEP_COLUMNS]
                    for x in blocks
                    for g in range(n // SUB)
                ],
                axis=0,
            )
            start = pair * wa + c * STEP_COLUMNS
            buf[:, :, start : start + STEP_COLUMNS] = parts_dot(onehot, values, (1,)).reshape(
                owners, 2 * CAP, STEP_COLUMNS
            )
        at = pl.ds(pair * wa, wa)
        copies.append(pltpu.make_async_copy(buf.at[:, :, at], out_ref.at[:, :, at], sems.at[pair]))
        copies[-1].start()
    at = pl.ds(pairs * wa, LANES)
    buf[:, :, at] = tags.astype(f32).reshape(owners, 2 * CAP, LANES)
    copies.append(pltpu.make_async_copy(buf.at[:, :, at], out_ref.at[:, :, at], sems.at[pairs]))
    copies[-1].start()
    for copy in copies:
        copy.wait()


def place_kernel(owned, me_ref, tags_ref, in_ref, out_ref, placer):
    rows = in_ref.shape[0]

    @pl.when((pl.program_id(0) == 0) & (pl.program_id(1) == 0))
    def _():
        shape = (rows, owned)
        hit = tags_ref[...][:, :1].astype(i32) == iota(shape, 1)
        upper = iota(shape, 0) // CAP % 2
        for h in range(2):
            placer[:, h * owned : (h + 1) * owned] = ones(hit & (upper == h))

    out_ref[...] = parts_dot(placer[...], in_ref[...], (0,)).reshape(out_ref.shape)


def step(gradient, table_ref, first_ref, second_ref, new_table_ref, new_first_ref, new_second_ref):
    new_first = decay_first * first_ref[...] + (1.0 - decay_first) * gradient
    new_second = decay_second * second_ref[...] + (1.0 - decay_second) * gradient * gradient
    scaled_first = new_first / (1.0 - decay_first**STEP)
    scaled_second = new_second / (1.0 - decay_second**STEP)
    new_table = table_ref[...] - learn_rate * scaled_first / (jnp.sqrt(scaled_second) + epsilon)
    new_table_ref[...] = new_table
    new_first_ref[...] = new_first
    new_second_ref[...] = new_second
    return new_table.astype(bf16)


def adam_a_kernel(pairs, me_ref, tags_ref, *refs):
    ins, out_ref, hits = refs[:pairs], refs[-2], refs[-1]
    rows, owned = hits.shape

    @pl.when(pl.program_id(0) == 0)
    def _():
        tags = tags_ref[...]
        tag = jnp.concatenate([tags[:, :, j : j + 1] for j in range(pairs)], axis=1).reshape(rows, 1)
        hits[...] = ones(tag.astype(i32) == iota((rows, owned), 1))

    values = jnp.concatenate([x[...] for x in ins], axis=1).reshape(rows, -1)
    half = step(parts_dot(hits[...], values, (0,)), *refs[pairs:-2])
    out_ref[...] = (
        jnp.dot(hits[...], half, preferred_element_type=f32).astype(bf16).reshape(out_ref.shape)
    )


def adam_b_kernel(me_ref, grad_ref, *refs):
    refs[-1][...] = step(grad_ref[...], *refs[:3], *refs[-4:-1])


def pick_kernel(owned, me_ref, tags_ref, in_ref, out_ref, picker):
    rows = out_ref.shape[0]

    @pl.when((pl.program_id(0) == 0) & (pl.program_id(1) == 0))
    def _():
        tags = tags_ref[...].reshape(rows // (4 * CAP), 2 * CAP, LANES)
        tags = jnp.concatenate([tags, tags], axis=1).reshape(rows, LANES)
        shape = (rows, owned)
        hit = tags[:, :1].astype(i32) == iota(shape, 1)
        quarter = iota(shape, 0) // CAP % 4
        for h in range(4):
            picker[:, h * owned : (h + 1) * owned] = ones(hit & (quarter == h))

    block = in_ref[...].reshape(4 * owned, in_ref.shape[-1])
    out_ref[...] = jnp.dot(picker[...], block, preferred_element_type=f32).astype(bf16)


def unpad_kernel(owned, reps, me_ref, in_ref, *refs):
    names, outs = refs[:reps], refs[reps:]
    owners = in_ref.shape[0]
    n = outs[0].shape[0]
    for group in range(reps // 4):
        block = in_ref[:, group * 4 * CAP : (group + 1) * 4 * CAP, :].reshape(owners * 4 * CAP, -1)
        for t in range(4):
            s = 4 * group + t
            _, col = positions(names[s][:1, :n].astype(i32), owned)
            at = iota((n, owners * 4 * CAP), 1)
            hit = ((at // (4 * CAP) * CAP + at % CAP) == col) & (at // CAP % 4 == t)
            outs[s][...] = jnp.dot(ones(hit), block, preferred_element_type=f32).astype(bf16)


def final_kernel(owned, reps, width, wa, me_ref, ids_ref, in_ref, *refs):
    ins, out_ref, found, sems, sem_b = refs[:reps], refs[-4], refs[-3], refs[-2], refs[-1]
    r = me_ref[1]
    n = out_ref.shape[0]
    copies = []
    for s in range(reps):
        start = pl.multiple_of((r + s) % reps * width, 128)
        copies.append(pltpu.make_async_copy(ins[s], out_ref.at[:, pl.ds(start, wa)], sems.at[s]))
        copies[-1].start()
    _, col = positions(ids_ref[...], owned)
    wb = width - wa
    rows = in_ref.shape[0]
    at = iota((n, rows), 1)
    hit = (at // (4 * CAP) * CAP + at % CAP) == col
    for h in range(4):
        onehot = ones(hit & (at // CAP % 4 == h))
        for i in range(2):
            q = 2 * h + i
            found[q] = jnp.dot(
                onehot, in_ref[:, i * wb : (i + 1) * wb], preferred_element_type=f32
            ).astype(bf16)
            copies.append(
                pltpu.make_async_copy(found.at[q], out_ref.at[:, pl.ds(q * width + wa, wb)], sem_b.at[q])
            )
            copies[-1].start()
    for copy in copies:
        copy.wait()


def shards(token_grads, token_slots, touched_ids, table, first_moment, second_moment):
    owners, reps = lax.axis_size("vocab"), lax.axis_size("rep")
    tokens, full = token_grads.shape
    touched = touched_ids.shape[0]
    owned, width = table.shape
    wa = width // 2
    wb = width - wa
    cols = STEP_COLUMNS
    half = reps // 2
    rows8, rows16, rows_all = owners * 2 * CAP, owners * 4 * CAP, owners * reps * CAP
    slots = token_slots.reshape(1, tokens)
    ids = touched_ids.reshape(1, touched)
    me = jnp.stack([lax.axis_index("vocab"), lax.axis_index("rep")]).astype(i32)

    def over_vocab(x):
        return lax.all_to_all(x, "vocab", split_axis=0, concat_axis=0, tiled=True)

    def shift(x, s):
        if s == 0:
            return x
        return lax.ppermute(x, "rep", [(i, (i + s) % reps) for i in range(reps)])

    wide_a = touched // SUB * wa + LANES
    sums = call(
        functools.partial(sums_kernel, reps),
        "sums",
        [sds((SUB, wide_a), f32)] * reps,
        (1,),
        [whole((1, tokens)), whole((1, touched))]
        + [
            pl.BlockSpec((tokens, wa), lambda i, me, s=s: (0, (me[1] + s) % reps * (width // wa)))
            for s in range(reps)
        ],
        [whole((SUB, wide_a))] * reps,
        2 * touched * tokens * wa * reps,
        (tokens * 2 + touched * 4) * wa * reps,
    )(me, slots, ids, *[token_grads] * reps)
    group = [shift(x, s) for s, x in enumerate(sums)]

    per = wb // cols
    wide_b = half * wb + LANES
    out_b = call(
        functools.partial(send_kernel, owned),
        "send",
        sds((rows8, wide_b), f32),
        (1,),
        [whole((1, tokens)), whole((1, touched))]
        + [pl.BlockSpec((tokens, wb), lambda i, me, q=q: (0, (q * width + wa) // wb)) for q in range(reps)],
        ANY,
        4 * rows8 * tokens * wb * half,
        (tokens * 4 + rows8 * 4) * wb * half,
        scratch=[pltpu.VMEM((rows8, wide_b), f32), pltpu.SemaphoreType.DMA((half + 1,))],
    )(me, slots, ids, *[token_grads] * reps)
    arrived_b = over_vocab(out_b.reshape(owners, 2 * CAP, -1)).reshape(rows8, -1)
    arrived_b, *group = lax.optimization_barrier((arrived_b, *group))
    tags_b = pl.BlockSpec((rows8, LANES), lambda i, j, me: (0, half * wb // LANES))

    dense = call(
        functools.partial(place_kernel, owned),
        "place",
        sds((2, half, owned, wb), f32),
        (half, per),
        [tags_b, pl.BlockSpec((rows8, cols), lambda i, j, me: (0, i * per + j))],
        pl.BlockSpec((2, 1, owned, cols), lambda i, j, me: (0, i, 0, j)),
        6 * rows8 * 2 * owned * wb * half,
        2 * rows8 * half * wb * 4,
        scratch=[pltpu.VMEM((rows8, 2 * owned), bf16)],
    )(me, arrived_b, arrived_b)
    gradient_b = lax.psum_scatter(
        dense.reshape(reps * owned, wb), "rep", scatter_dimension=0, tiled=True
    )

    steps_a = wa // cols
    wide = half * wa + LANES
    out_a = call(
        functools.partial(route_kernel, owned, wa),
        "route",
        sds((owners, 2 * CAP, wide), f32),
        (1,),
        [whole((SUB, wide_a))] * reps,
        ANY,
        6 * rows_all * 2 * touched * wa,
        (rows_all + reps * touched) * 4 * wa,
        scratch=[pltpu.VMEM((owners, 2 * CAP, wide), f32), pltpu.SemaphoreType.DMA((half + 1,))],
    )(me, *group)
    arrived_a = over_vocab(out_a)

    spec = pl.BlockSpec((owned, cols), lambda i, me: (0, i))
    *news, back_a = call(
        functools.partial(adam_a_kernel, half),
        "adam_a",
        [*(sds((owned, width), f32) for _ in range(3)), sds((owners, reps * CAP, wa), bf16)],
        (steps_a,),
        [pl.BlockSpec((owners, 2 * CAP, LANES), lambda i, me: (0, 0, half * wa // LANES))]
        + [
            pl.BlockSpec((owners, 2 * CAP, cols), lambda i, me, j=j: (0, 0, j * steps_a + i))
            for j in range(half)
        ]
        + [spec, spec, spec],
        [spec, spec, spec, pl.BlockSpec((owners, reps * CAP, cols), lambda i, me: (0, 0, i))],
        8 * rows_all * owned * wa,
        (rows_all * 6 + owned * 24) * wa,
        scratch=[pltpu.VMEM((rows_all, owned), bf16)],
    )(me, *[arrived_a] * (half + 1), table, first_moment, second_moment)
    returned_a = over_vocab(back_a)

    spec_b = pl.BlockSpec((owned, cols), lambda i, me: (0, wa // cols + i))
    spec_g = pl.BlockSpec((owned, cols), lambda i, me: (0, i))
    *news, half_b = call(
        adam_b_kernel,
        "adam_b",
        [*(sds((owned, width), f32) for _ in range(3)), sds((owned, wb), bf16)],
        (per,),
        [spec_g, spec_b, spec_b, spec_b, ANY, ANY, ANY],
        [spec_b, spec_b, spec_b, spec_g],
        20 * owned * wb,
        30 * owned * wb,
        aliases={5: 0, 6: 1, 7: 2},
    )(me, gradient_b, table, first_moment, second_moment, *news)
    rows_b = lax.all_gather(half_b, "rep", axis=0, tiled=True)

    mine_a = call(
        functools.partial(unpad_kernel, owned, reps),
        "unpad",
        [sds((touched, wa), bf16)] * reps,
        (steps_a,),
        [pl.BlockSpec((owners, reps * CAP, cols), lambda i, me: (0, 0, i))]
        + [pl.BlockSpec((SUB, LANES), lambda i, me: (0, touched // SUB * wa // LANES))] * reps,
        [pl.BlockSpec((touched, cols), lambda i, me: (0, i))] * reps,
        2 * reps * touched * rows16 * wa,
        (rows_all + reps * touched) * 2 * wa,
    )(me, returned_a, *group)
    home_a = [shift(x, (reps - s) % reps) for s, x in enumerate(mine_a)]

    back_b = call(
        functools.partial(pick_kernel, owned),
        "pick",
        sds((rows16, 2 * wb), bf16),
        (2, per),
        [
            tags_b,
            pl.BlockSpec((4, 1, owned, cols), lambda i, j, me: (0, i, 0, j)),
        ],
        pl.BlockSpec((rows16, cols), lambda i, j, me: (0, i * per + j)),
        4 * rows16 * 4 * owned * wb,
        (8 * owned + 2 * rows16) * wb * 2,
        scratch=[pltpu.VMEM((rows16, 4 * owned), bf16)],
    )(me, arrived_b, rows_b.reshape(4, 2, owned, wb))
    returned_b = over_vocab(back_b.reshape(owners, 4 * CAP, -1)).reshape(rows16, -1)

    refreshed = call(
        functools.partial(final_kernel, owned, reps, width, wa),
        "final",
        sds((touched, full), bf16),
        (1,),
        [whole((1, touched)), whole((rows16, 2 * wb))] + [ANY] * reps,
        ANY,
        16 * touched * rows16 * wb,
        touched * full * 4,
        scratch=[
            pltpu.VMEM((reps, touched, wb), bf16),
            pltpu.SemaphoreType.DMA((reps,)),
            pltpu.SemaphoreType.DMA((reps,)),
        ],
    )(me, ids, returned_b, *home_a)
    return (*news, refreshed)


def solution(mesh):
    return jax.shard_map(
        shards,
        mesh=mesh,
        in_specs=(
            P(("vocab", "rep"), None),
            P(("vocab", "rep")),
            P(("vocab", "rep")),
            P("vocab", "rep"),
            P("vocab", "rep"),
            P("vocab", "rep"),
        ),
        out_specs=(
            P("vocab", "rep"),
            P("vocab", "rep"),
            P("vocab", "rep"),
            P(("vocab", "rep"), None),
        ),
        check_vma=False,
    )
```

time: 567 us -> 282 us (0.50); the launches traced: 557 us -> 281 us
  waiting for transfers between devices: 346 us -> 88.8 us
  local copies, waits for them, and re-layouts: 66.1 us -> 22.5 us
  Pallas kernels: 0 us -> 40.2 us
  starting transfers between devices: 30.9 us -> 56.2 us
  other arithmetic: 19.9 us -> 0.08 us
  matrix products: 10.9 us -> 0 us
  blocking collectives: 67.8 us -> 59 us
    all_to_all x4 -> x3, waiting for transfers between devices: 283 us -> 0.01 us  [over_vocab(): return lax.all_to_all(x, 'vocab', split_axis=0, concat_axis=0, tiled=True)]
    ppermute x0 -> x14, waiting for transfers between devices: none -> 55.2 us  [shift(): return lax.ppermute(x, 'rep', [(i, (i + s) % reps) for i in range(reps)])]
    pallas_call x0 -> x9, Pallas kernels: none -> 40.2 us  [the longest x1 11.3 us: shards(): call(functools.partial(place_kernel, owned), 'place', sds((2, half, owned...]
    ppermute x0 -> x14, starting transfers between devices: none -> 35.7 us  [shift(): return lax.ppermute(x, 'rep', [(i, (i + s) % reps) for i in range(reps)])]
    all_gather x1, waiting for transfers between devices: 63.5 us -> 33.6 us  [shards(): rows_b = lax.all_gather(half_b, 'rep', axis=0, tiled=True)]
    gather x4 -> x0, local copies, waits for them, and re-layouts: 25.5 us -> none  [the longest x1 12.3 us: shards(): jnp.take(shard_rows, jnp.clip(wanted, 0, shard_rows.shape[0] - 1), axis=0)]
    all_to_all x5 -> x0, local copies, waits for them, and re-layouts: 22.1 us -> none  [the longest x1 11 us: shards(): lax.all_to_all(lax.all_to_all(outgoing, 'vocab', split_axis=0, concat_axi...]
    select_n x6 -> x0, other arithmetic: 18.8 us -> none  [the longest x1 15.3 us: shards(): jnp.where(filled[:, :, None], jnp.take(summed, source, axis=0), 0.0)]
  transfers between devices with their start and end apart: 5 -> 19, of which waited for: 3 -> 10; matrix products, arithmetic and copies ran while one was open for 11% -> 0% of each run, Pallas kernels for 0% -> 7%
where the time goes in v1:
time: 282 us; the launch traced here: 281 us
  waiting for transfers between devices  88.8 us (31%)
  blocking collectives  59 us (21%)
  starting transfers between devices  56.2 us (20%)
  Pallas kernels  40.2 us (14%)
  local copies, waits for them, and re-layouts  22.5 us (8%)
  between operations  14.3 us (5%)
    all_to_all x1, blocking collectives, over_vocab(): return lax.all_to_all(x, 'vocab', split_axis=0, concat_axis=0, tiled=True)  59 us
    ppermute x14, waiting for transfers between devices, shift(): return lax.ppermute(x, 'rep', [(i, (i + s) % reps) for i in range(reps)])  55.2 us
    ppermute x14, starting transfers between devices, shift(): return lax.ppermute(x, 'rep', [(i, (i + s) % reps) for i in range(reps)])  35.7 us
    all_gather x1, waiting for transfers between devices, shards(): rows_b = lax.all_gather(half_b, 'rep', axis=0, tiled=True)  33.6 us
    unnamed x64, local copies, waits for them, and re-layouts  22.5 us
    all_to_all x3, starting transfers between devices, over_vocab(): return lax.all_to_all(x, 'vocab', split_axis=0, concat_axis=0, tiled=True)  20.4 us
    pallas_call x1, Pallas kernels, shards(): call(functools.partial(place_kernel, owned), 'place', sds((2, half, owned...  11.3 us
    pallas_call x1, Pallas kernels, shards(): call(functools.partial(adam_a_kernel, half), 'adam_a', [*(sds((owned, wid...  6.65 us
  transfers between devices with their start and end apart: 19, of which 10 were waited for; matrix products, arithmetic and copies ran while one was open for 0% of the time, Pallas kernels for 7%

profile of v1, /device:TPU:2, one launch (start us, length us, event | category | flops | bytes accessed | tf_op | source)
XLA Modules:
  0.0 281.1 jit_solution(9897899638314723575)
XLA Ops:
  7.2 2.2 copy-done
  10.7 2.8 %send.1 = f32[256,4224]{1,0:T(8,128)S(1)} custom-call(s32[2]{0:T(128)S(1)} %pad_add_fusion.me_ref, s32[1,128]{1,0:T(1,128)S(1)} %bitcast.18, s32[1,64]{1,0:T(1,128)S(1)} %bitcast.15, bf16[128,16384]{1,0:T(8,128)(2,1)S(1)} %copy-done, bf16[128,16384]{1,0:T(8,128)(2,1)S(1)} %copy-done, bf16[128,16384]{1,0:T(8,128)(2,1)S(1)} %copy-done, ...), custom_call_target="tpu_custom_call" | custom-call | flops 536870912 | bytes 6291456 | tf_op jit(solution)/shard_map/send/pallas_call | solution.py:319
  13.6 2.1 copy-done.2
  15.7 7.8 %all-to-all-start = ((f32[32,8,4224]{2,1,0:T(8,128)}), f32[32,8,4224]{2,1,0:T(8,128)}, u32[]{:S(2)}, u32[]{:S(2)}) async-start(f32[32,8,4224]{2,1,0:T(8,128)} %bitcast.10), calls=%async_computation | async-start | bytes 8650752 | tf_op jit(solution)/shard_map/all_to_all | solution.py:293
  23.5 2.2 copy-done.1
  28.7 3.3 %collective-permute-start.1 = (f32[8,8320]{1,0:T(8,128)S(1)}, f32[8,8320]{1,0:T(8,128)S(1)}, u32[]{:S(2)}, u32[]{:S(2)}) collective-permute-start(f32[8,8320]{1,0:T(8,128)S(1)} %get-tuple-element.39), channel_id=1, source_target_pairs={{0,2},{1,3},{2,4},{3,5},{4,6},{5,7},{6,0},{7,1},{8,10},{9,11},{10,... | collective-permute-start | bytes 798728 | tf_op jit(solution)/shard_map/ppermute | solution.py:298
  32.0 4.0 %collective-permute-start.2 = (f32[8,8320]{1,0:T(8,128)S(1)}, f32[8,8320]{1,0:T(8,128)S(1)}, u32[]{:S(2)}, u32[]{:S(2)}) collective-permute-start(f32[8,8320]{1,0:T(8,128)S(1)} %get-tuple-element.40), channel_id=1, source_target_pairs={{0,3},{1,4},{2,5},{3,6},{4,7},{5,0},{6,1},{7,2},{8,11},{9,12},{10,... | collective-permute-start | bytes 798728 | tf_op jit(solution)/shard_map/ppermute | solution.py:298
  36.6 4.9 %collective-permute-start.4 = (f32[8,8320]{1,0:T(8,128)S(1)}, f32[8,8320]{1,0:T(8,128)S(1)}, u32[]{:S(2)}, u32[]{:S(2)}) collective-permute-start(f32[8,8320]{1,0:T(8,128)S(1)} %get-tuple-element.42), channel_id=1, source_target_pairs={{0,5},{1,6},{2,7},{3,0},{4,1},{5,2},{6,3},{7,4},{8,13},{9,14},{10,... | collective-permute-start | bytes 798728 | tf_op jit(solution)/shard_map/ppermute | solution.py:298
  41.5 6.2 %collective-permute-start.5 = (f32[8,8320]{1,0:T(8,128)S(1)}, f32[8,8320]{1,0:T(8,128)S(1)}, u32[]{:S(2)}, u32[]{:S(2)}) collective-permute-start(f32[8,8320]{1,0:T(8,128)S(1)} %get-tuple-element.43), channel_id=1, source_target_pairs={{0,6},{1,7},{2,0},{3,1},{4,2},{5,3},{6,4},{7,5},{8,14},{9,15},{10,... | collective-permute-start | bytes 798728 | tf_op jit(solution)/shard_map/ppermute | solution.py:298
  47.7 6.2 %collective-permute-done.1.refs_2_ = f32[8,8320]{1,0:T(8,128)S(1)} collective-permute-done((f32[8,8320]{1,0:T(8,128)S(1)}, f32[8,8320]{1,0:T(8,128)S(1)}, u32[]{:S(2)}, u32[]{:S(2)}) %collective-permute-start.1) | collective-permute-done | bytes 266272 | tf_op jit(solution)/shard_map/ppermute | solution.py:298
  53.9 2.8 collective-permute-start.6
  56.7 17.0 %collective-permute-done.2.refs_3_ = f32[8,8320]{1,0:T(8,128)S(1)} collective-permute-done((f32[8,8320]{1,0:T(8,128)S(1)}, f32[8,8320]{1,0:T(8,128)S(1)}, u32[]{:S(2)}, u32[]{:S(2)}) %collective-permute-start.2) | collective-permute-done | bytes 266272 | tf_op jit(solution)/shard_map/ppermute | solution.py:298
  73.7 7.0 %collective-permute-done.5.refs_6_ = f32[8,8320]{1,0:T(8,128)S(1)} collective-permute-done((f32[8,8320]{1,0:T(8,128)S(1)}, f32[8,8320]{1,0:T(8,128)S(1)}, u32[]{:S(2)}, u32[]{:S(2)}) %collective-permute-start.5) | collective-permute-done | bytes 266272 | tf_op jit(solution)/shard_map/ppermute | solution.py:298
  80.7 3.3 %collective-permute-done.6.refs_7_ = f32[8,8320]{1,0:T(8,128)S(1)} collective-permute-done((f32[8,8320]{1,0:T(8,128)S(1)}, f32[8,8320]{1,0:T(8,128)S(1)}, u32[]{:S(2)}, u32[]{:S(2)}) %collective-permute-start.6) | collective-permute-done | bytes 266272 | tf_op jit(solution)/shard_map/ppermute | solution.py:298
  84.1 11.3 %place.1 = f32[2,4,128,1024]{3,2,1,0:T(8,128)S(1)} custom-call(s32[2]{0:T(128)S(1)} %pad_add_fusion.me_ref, f32[256,4224]{1,0:T(8,128)} %bitcast.5.tags_ref.in_ref, f32[256,4224]{1,0:T(8,128)} %bitcast.5.tags_ref.in_ref), custom_call_target="tpu_custom_call" | custom-call | flops 1610612736 | bytes 8388608 | tf_op jit(solution)/shard_map/place/pallas_call | solution.py:335
  97.6 4.0 %route.1 = f32[32,8,4224]{2,1,0:T(8,128)S(1)} custom-call(s32[2]{0:T(128)S(1)} %pad_add_fusion.me_ref, f32[8,8320]{1,0:T(8,128)S(1)} %get-tuple-element.46.refs_0_, f32[8,8320]{1,0:T(8,128)S(1)} %collective-permute-done.refs_1_, f32[8,8320]{1,0:T(8,128)S(1)} %collective-permute-done.1.refs_2_, f32[8,8320]{1,0:T(8,128)S(1)} %collective-permute-done.2.refs_3_, ...), custom_call_target="tpu_custom_call" | custom-call | flops 805306368 | bytes 6291456 | tf_op jit(solution)/shard_map/route/pallas_call | solution.py:352
  101.7 59.0 %all_to_all.20.tags_ref.refs_0_.refs_1_.refs_2_.refs_3_ = f32[32,8,4224]{2,1,0:T(8,128)S(1)} all-to-all(f32[32,8,4224]{2,1,0:T(8,128)S(1)} %route.1), channel_id=1, replica_groups=mesh['vocab'=32,'rep'=8] {'vocab'}, dimensions={0} | all-to-all | bytes 8650752 | tf_op jit(solution)/shard_map/all_to_all | solution.py:293
  160.7 6.7 %adam_a.1 = (f32[128,2048]{1,0:T(8,128)}, f32[128,2048]{1,0:T(8,128)}, f32[128,2048]{1,0:T(8,128)}, bf16[32,32,1024]{2,1,0:T(8,128)(2,1)S(1)}) custom-call(s32[2]{0:T(128)S(1)} %pad_add_fusion.me_ref, f32[32,8,4224]{2,1,0:T(8,128)S(1)} %all_to_all.20.tags_ref.refs_0_.refs_1_.refs_2_.refs_3_, ...), custom_call_target="tpu_custom_call" | custom-call | flops 1073741824 | bytes 9437184 | tf_op jit(solution)/shard_map/adam_a/pallas_call | solution.py:366
  169.7 2.5 adam_b.1
  172.9 5.2 %all-to-all-start.3 = ((bf16[32,32,1024]{2,1,0:T(8,128)(2,1)}), bf16[32,32,1024]{2,1,0:T(8,128)(2,1)S(1)}, u32[]{:S(2)}, u32[]{:S(2)}) async-start(bf16[32,32,1024]{2,1,0:T(8,128)(2,1)} %copy-done.10), calls=%async_computation.4 | async-start | bytes 4194304 | tf_op jit(solution)/shard_map/all_to_all | solution.py:293
  178.1 33.6 %all-gather.2.cloned.1.call-done = bf16[1024,1024]{1,0:T(8,128)(2,1)} async-done(((bf16[128,1024]{1,0:T(8,128)(2,1)}), bf16[1024,1024]{1,0:T(8,128)(2,1)}) %all-gather.2.cloned.1.call-update) | async-done | bytes 2097168 | tf_op jit(solution)/shard_map/all_gather | solution.py:397
  213.2 4.6 %pick.1 = bf16[512,2048]{1,0:T(8,128)(2,1)S(1)} custom-call(s32[2]{0:T(128)S(1)} %pad_add_fusion.me_ref, f32[256,4224]{1,0:T(8,128)} %bitcast.5.tags_ref.in_ref, bf16[4,2,128,1024]{3,2,1,0:T(8,128)(2,1)S(1)} %bitcast.14), custom_call_target="tpu_custom_call" | custom-call | flops 1073741824 | bytes 4194304 | tf_op jit(solution)/shard_map/pick/pallas_call | solution.py:412
  220.5 7.4 %all-to-all-start.2 = ((bf16[32,16,2048]{2,1,0:T(8,128)(2,1)}), bf16[32,16,2048]{2,1,0:T(8,128)(2,1)S(1)}, u32[]{:S(2)}, u32[]{:S(2)}) async-start(bf16[32,16,2048]{2,1,0:T(8,128)(2,1)} %bitcast.13), calls=%async_computation.3 | async-start | bytes 4194304 | tf_op jit(solution)/shard_map/all_to_all | solution.py:293
  233.4 4.2 %unpad.1 = (bf16[64,1024]{1,0:T(8,128)(2,1)S(1)}, bf16[64,1024]{1,0:T(8,128)(2,1)S(1)}, bf16[64,1024]{1,0:T(8,128)(2,1)S(1)}, bf16[64,1024]{1,0:T(8,128)(2,1)S(1...) custom-call(s32[2]{0:T(128)S(1)} %pad_add_fusion.me_ref, ...), custom_call_target="tpu_custom_call" | custom-call | flops 536870912 | bytes 3145728 | tf_op jit(solution)/shard_map/unpad/pallas_call | solution.py:399
  237.6 3.0 %collective-permute-start.10 = (bf16[64,1024]{1,0:T(8,128)(2,1)S(1)}, bf16[64,1024]{1,0:T(8,128)(2,1)S(1)}, u32[]{:S(2)}, u32[]{:S(2)}) collective-permute-start(bf16[64,1024]{1,0:T(8,128)(2,1)S(1)} %get-tuple-element.66), channel_id=1, source_target_pairs={{0,4},{1,5},{2,6},{3,7},{4,0},{5,1},{6,2},{7,3},{8,12},{9,13},{10,... | collective-permute-start | bytes 393224 | tf_op jit(solution)/shard_map/ppermute | solution.py:298
  240.6 2.1 collective-permute-start.11
  245.3 2.6 collective-permute-start.7
  247.9 3.8 %collective-permute-done.10.refs_4_ = bf16[64,1024]{1,0:T(8,128)(2,1)S(1)} collective-permute-done((bf16[64,1024]{1,0:T(8,128)(2,1)S(1)}, bf16[64,1024]{1,0:T(8,128)(2,1)S(1)}, u32[]{:S(2)}, u32[]{:S(2)}) %collective-permute-start.10) | collective-permute-done | bytes 131104 | tf_op jit(solution)/shard_map/ppermute | solution.py:298
  253.3 7.3 %collective-permute-done.11.refs_5_ = bf16[64,1024]{1,0:T(8,128)(2,1)S(1)} collective-permute-done((bf16[64,1024]{1,0:T(8,128)(2,1)S(1)}, bf16[64,1024]{1,0:T(8,128)(2,1)S(1)}, u32[]{:S(2)}, u32[]{:S(2)}) %collective-permute-start.11) | collective-permute-done | bytes 131104 | tf_op jit(solution)/shard_map/ppermute | solution.py:298
  261.1 4.4 %collective-permute-done.13.refs_7_ = bf16[64,1024]{1,0:T(8,128)(2,1)S(1)} collective-permute-done((bf16[64,1024]{1,0:T(8,128)(2,1)S(1)}, bf16[64,1024]{1,0:T(8,128)(2,1)S(1)}, u32[]{:S(2)}, u32[]{:S(2)}) %collective-permute-start.13) | collective-permute-done | bytes 131104 | tf_op jit(solution)/shard_map/ppermute | solution.py:298
  265.6 5.6 %collective-permute-done.9.refs_3_ = bf16[64,1024]{1,0:T(8,128)(2,1)S(1)} collective-permute-done((bf16[64,1024]{1,0:T(8,128)(2,1)S(1)}, bf16[64,1024]{1,0:T(8,128)(2,1)S(1)}, u32[]{:S(2)}, u32[]{:S(2)}) %collective-permute-start.9) | collective-permute-done | bytes 131104 | tf_op jit(solution)/shard_map/ppermute | solution.py:298
  271.2 3.1 %final.1 = bf16[64,16384]{1,0:T(8,128)(2,1)} custom-call(s32[2]{0:T(128)S(1)} %pad_add_fusion.me_ref, s32[1,64]{1,0:T(1,128)S(1)} %bitcast.17, bf16[512,2048]{1,0:T(8,128)(2,1)S(1)} %bitcast.12, bf16[64,1024]{1,0:T(8,128)(2,1)S(1)} %get-tuple-element.62.refs_0_, bf16[64,1024]{1,0:T(8,128)(2,1)S(1)} %collective-permute-done.7.refs_1_, ...), custom_call_target="tpu_custom_call" | custom-call | flops 536870912 | bytes 4194304 | tf_op jit(solution)/shard_map/final/pallas_call | solution.py:428
  (83 shorter events, 24.6 us)
Async XLA Ops:
  15.7 68.4 %all-to-all-start = ((f32[32,8,4224]{2,1,0:T(8,128)}), f32[32,8,4224]{2,1,0:T(8,128)}, u32[]{:S(2)}, u32[]{:S(2)}) async-start(f32[32,8,4224]{2,1,0:T(8,128)} %bitcast.10), calls=%async_computation | async-start | bytes 8650752 | tf_op jit(solution)/shard_map/all_to_all | solution.py:293
  23.5 145.2 %reduce-scatter.2.cloned.1.call-start = ((), (), s32[]{:S(2)}) async-start(), calls=%async_computation.5 | async-start | bytes 4718592 | tf_op jit(solution)/shard_map/reduce_scatter | solution.py:346
  26.7 14.8 %collective-permute-start = (f32[8,8320]{1,0:T(8,128)S(1)}, f32[8,8320]{1,0:T(8,128)S(1)}, u32[]{:S(2)}, u32[]{:S(2)}) collective-permute-start(f32[8,8320]{1,0:T(8,128)S(1)} %get-tuple-element.38), channel_id=1, source_target_pairs={{0,1},{1,2},{2,3},{3,4},{4,5},{5,6},{6,7},{7,0},{8,9},{9,10},{10,1... | collective-permute-start | bytes 798728 | tf_op jit(solution)/shard_map/ppermute | solution.py:298
  28.7 25.2 %collective-permute-start.1 = (f32[8,8320]{1,0:T(8,128)S(1)}, f32[8,8320]{1,0:T(8,128)S(1)}, u32[]{:S(2)}, u32[]{:S(2)}) collective-permute-start(f32[8,8320]{1,0:T(8,128)S(1)} %get-tuple-element.39), channel_id=1, source_target_pairs={{0,2},{1,3},{2,4},{3,5},{4,6},{5,7},{6,0},{7,1},{8,10},{9,11},{10,... | collective-permute-start | bytes 798728 | tf_op jit(solution)/shard_map/ppermute | solution.py:298
  32.0 41.7 %collective-permute-start.2 = (f32[8,8320]{1,0:T(8,128)S(1)}, f32[8,8320]{1,0:T(8,128)S(1)}, u32[]{:S(2)}, u32[]{:S(2)}) collective-permute-start(f32[8,8320]{1,0:T(8,128)S(1)} %get-tuple-element.40), channel_id=1, source_target_pairs={{0,3},{1,4},{2,5},{3,6},{4,7},{5,0},{6,1},{7,2},{8,11},{9,12},{10,... | collective-permute-start | bytes 798728 | tf_op jit(solution)/shard_map/ppermute | solution.py:298
  36.0 37.7 %collective-permute-start.3 = (f32[8,8320]{1,0:T(8,128)S(1)}, f32[8,8320]{1,0:T(8,128)S(1)}, u32[]{:S(2)}, u32[]{:S(2)}) collective-permute-start(f32[8,8320]{1,0:T(8,128)S(1)} %get-tuple-element.41), channel_id=1, source_target_pairs={{0,4},{1,5},{2,6},{3,7},{4,0},{5,1},{6,2},{7,3},{8,12},{9,13},{10,... | collective-permute-start | bytes 798728 | tf_op jit(solution)/shard_map/ppermute | solution.py:298
  36.6 37.2 %collective-permute-start.4 = (f32[8,8320]{1,0:T(8,128)S(1)}, f32[8,8320]{1,0:T(8,128)S(1)}, u32[]{:S(2)}, u32[]{:S(2)}) collective-permute-start(f32[8,8320]{1,0:T(8,128)S(1)} %get-tuple-element.42), channel_id=1, source_target_pairs={{0,5},{1,6},{2,7},{3,0},{4,1},{5,2},{6,3},{7,4},{8,13},{9,14},{10,... | collective-permute-start | bytes 798728 | tf_op jit(solution)/shard_map/ppermute | solution.py:298
  41.5 56.0 %copy-start.12 = (f32[8,8320]{1,0:T(8,128)}, f32[8,8320]{1,0:T(8,128)S(1)}, u32[]{:S(2)}) copy-start(f32[8,8320]{1,0:T(8,128)S(1)} %collective-permute-done.refs_1_) | copy-start | bytes 798724
  41.5 39.2 %collective-permute-start.5 = (f32[8,8320]{1,0:T(8,128)S(1)}, f32[8,8320]{1,0:T(8,128)S(1)}, u32[]{:S(2)}, u32[]{:S(2)}) collective-permute-start(f32[8,8320]{1,0:T(8,128)S(1)} %get-tuple-element.43), channel_id=1, source_target_pairs={{0,6},{1,7},{2,0},{3,1},{4,2},{5,3},{6,4},{7,5},{8,14},{9,15},{10,... | collective-permute-start | bytes 798728 | tf_op jit(solution)/shard_map/ppermute | solution.py:298
  53.9 43.6 %copy-start.14 = (f32[8,8320]{1,0:T(8,128)}, f32[8,8320]{1,0:T(8,128)S(1)}, u32[]{:S(2)}) copy-start(f32[8,8320]{1,0:T(8,128)S(1)} %collective-permute-done.1.refs_2_) | copy-start | bytes 798724
  53.9 30.2 %collective-permute-start.6 = (f32[8,8320]{1,0:T(8,128)S(1)}, f32[8,8320]{1,0:T(8,128)S(1)}, u32[]{:S(2)}, u32[]{:S(2)}) collective-permute-start(f32[8,8320]{1,0:T(8,128)S(1)} %get-tuple-element.44), channel_id=1, source_target_pairs={{0,7},{1,0},{2,1},{3,2},{4,3},{5,4},{6,5},{7,6},{8,15},{9,8},{10,9... | collective-permute-start | bytes 798728 | tf_op jit(solution)/shard_map/ppermute | solution.py:298
  73.7 23.8 %copy-start.16 = (f32[8,8320]{1,0:T(8,128)}, f32[8,8320]{1,0:T(8,128)S(1)}, u32[]{:S(2)}) copy-start(f32[8,8320]{1,0:T(8,128)S(1)} %collective-permute-done.2.refs_3_) | copy-start | bytes 798724
  73.7 23.8 %copy-start.18 = (f32[8,8320]{1,0:T(8,128)}, f32[8,8320]{1,0:T(8,128)S(1)}, u32[]{:S(2)}) copy-start(f32[8,8320]{1,0:T(8,128)S(1)} %collective-permute-done.3.refs_4_) | copy-start | bytes 798724
  73.7 23.8 %copy-start.20 = (f32[8,8320]{1,0:T(8,128)}, f32[8,8320]{1,0:T(8,128)S(1)}, u32[]{:S(2)}) copy-start(f32[8,8320]{1,0:T(8,128)S(1)} %collective-permute-done.4.refs_5_) | copy-start | bytes 798724
  80.7 16.8 %copy-start.22 = (f32[8,8320]{1,0:T(8,128)}, f32[8,8320]{1,0:T(8,128)S(1)}, u32[]{:S(2)}) copy-start(f32[8,8320]{1,0:T(8,128)S(1)} %collective-permute-done.5.refs_6_) | copy-start | bytes 798724
  84.1 13.5 %copy-start.24 = (f32[8,8320]{1,0:T(8,128)}, f32[8,8320]{1,0:T(8,128)S(1)}, u32[]{:S(2)}) copy-start(f32[8,8320]{1,0:T(8,128)S(1)} %collective-permute-done.6.refs_7_) | copy-start | bytes 798724
  97.5 114.2 %all-gather.2.cloned.1.call-start = ((), (), s32[]{:S(2)}) async-start(), calls=%async_computation.6 | async-start | bytes 2359296 | tf_op jit(solution)/shard_map/all_gather | solution.py:397
  101.6 59.0 %copy-start.7 = (f32[128,2048]{1,0:T(8,128)S(1)}, f32[128,2048]{1,0:T(8,128)}, u32[]{:S(2)}) copy-start(f32[128,2048]{1,0:T(8,128)} %refs_0_.5) | copy-start | bytes 3145732
  101.6 59.0 %copy-start.8 = (f32[128,2048]{1,0:T(8,128)S(1)}, f32[128,2048]{1,0:T(8,128)}, u32[]{:S(2)}) copy-start(f32[128,2048]{1,0:T(8,128)} %refs_1_.5) | copy-start | bytes 3145732
  101.6 59.0 %copy-start.9 = (f32[128,2048]{1,0:T(8,128)S(1)}, f32[128,2048]{1,0:T(8,128)}, u32[]{:S(2)}) copy-start(f32[128,2048]{1,0:T(8,128)} %refs_2_.5) | copy-start | bytes 3145732
  172.9 46.3 %all-to-all-start.3 = ((bf16[32,32,1024]{2,1,0:T(8,128)(2,1)}), bf16[32,32,1024]{2,1,0:T(8,128)(2,1)S(1)}, u32[]{:S(2)}, u32[]{:S(2)}) async-start(bf16[32,32,1024]{2,1,0:T(8,128)(2,1)} %copy-done.10), calls=%async_computation.4 | async-start | bytes 4194304 | tf_op jit(solution)/shard_map/all_to_all | solution.py:293
  219.2 8.8 %copy-start.13 = (f32[8,8320]{1,0:T(8,128)S(1)}, f32[8,8320]{1,0:T(8,128)}, u32[]{:S(2)}) copy-start(f32[8,8320]{1,0:T(8,128)} %copy-done.12) | copy-start | bytes 798724
  219.2 8.8 %copy-start.15 = (f32[8,8320]{1,0:T(8,128)S(1)}, f32[8,8320]{1,0:T(8,128)}, u32[]{:S(2)}) copy-start(f32[8,8320]{1,0:T(8,128)} %copy-done.14) | copy-start | bytes 798724
  219.2 8.8 %copy-start.17 = (f32[8,8320]{1,0:T(8,128)S(1)}, f32[8,8320]{1,0:T(8,128)}, u32[]{:S(2)}) copy-start(f32[8,8320]{1,0:T(8,128)} %copy-done.16) | copy-start | bytes 798724
  220.5 50.7 %all-to-all-start.2 = ((bf16[32,16,2048]{2,1,0:T(8,128)(2,1)}), bf16[32,16,2048]{2,1,0:T(8,128)(2,1)S(1)}, u32[]{:S(2)}, u32[]{:S(2)}) async-start(bf16[32,16,2048]{2,1,0:T(8,128)(2,1)} %bitcast.13), calls=%async_computation.3 | async-start | bytes 4194304 | tf_op jit(solution)/shard_map/all_to_all | solution.py:293
  237.6 14.1 %collective-permute-start.10 = (bf16[64,1024]{1,0:T(8,128)(2,1)S(1)}, bf16[64,1024]{1,0:T(8,128)(2,1)S(1)}, u32[]{:S(2)}, u32[]{:S(2)}) collective-permute-start(bf16[64,1024]{1,0:T(8,128)(2,1)S(1)} %get-tuple-element.66), channel_id=1, source_target_pairs={{0,4},{1,5},{2,6},{3,7},{4,0},{5,1},{6,2},{7,3},{8,12},{9,13},{10,... | collective-permute-start | bytes 393224 | tf_op jit(solution)/shard_map/ppermute | solution.py:298
  240.6 20.0 %collective-permute-start.11 = (bf16[64,1024]{1,0:T(8,128)(2,1)S(1)}, bf16[64,1024]{1,0:T(8,128)(2,1)S(1)}, u32[]{:S(2)}, u32[]{:S(2)}) collective-permute-start(bf16[64,1024]{1,0:T(8,128)(2,1)S(1)} %get-tuple-element.67), channel_id=1, source_target_pairs={{0,3},{1,4},{2,5},{3,6},{4,7},{5,0},{6,1},{7,2},{8,11},{9,12},{10,... | collective-permute-start | bytes 393224 | tf_op jit(solution)/shard_map/ppermute | solution.py:298
  242.7 18.4 %collective-permute-start.12 = (bf16[64,1024]{1,0:T(8,128)(2,1)S(1)}, bf16[64,1024]{1,0:T(8,128)(2,1)S(1)}, u32[]{:S(2)}, u32[]{:S(2)}) collective-permute-start(bf16[64,1024]{1,0:T(8,128)(2,1)S(1)} %get-tuple-element.68), channel_id=1, source_target_pairs={{0,2},{1,3},{2,4},{3,5},{4,6},{5,7},{6,0},{7,1},{8,10},{9,11},{10,... | collective-permute-start | bytes 393224 | tf_op jit(solution)/shard_map/ppermute | solution.py:298
  244.6 20.9 %collective-permute-start.13 = (bf16[64,1024]{1,0:T(8,128)(2,1)S(1)}, bf16[64,1024]{1,0:T(8,128)(2,1)S(1)}, u32[]{:S(2)}, u32[]{:S(2)}) collective-permute-start(bf16[64,1024]{1,0:T(8,128)(2,1)S(1)} %get-tuple-element.69), channel_id=1, source_target_pairs={{0,1},{1,2},{2,3},{3,4},{4,5},{5,6},{6,7},{7,0},{8,9},{9,10},{10,1... | collective-permute-start | bytes 393224 | tf_op jit(solution)/shard_map/ppermute | solution.py:298
  245.3 20.3 %collective-permute-start.7 = (bf16[64,1024]{1,0:T(8,128)(2,1)S(1)}, bf16[64,1024]{1,0:T(8,128)(2,1)S(1)}, u32[]{:S(2)}, u32[]{:S(2)}) collective-permute-start(bf16[64,1024]{1,0:T(8,128)(2,1)S(1)} %get-tuple-element.63), channel_id=1, source_target_pairs={{0,7},{1,0},{2,1},{3,2},{4,3},{5,4},{6,5},{7,6},{8,15},{9,8},{10,9... | collective-permute-start | bytes 393224 | tf_op jit(solution)/shard_map/ppermute | solution.py:298
  251.7 13.9 %collective-permute-start.8 = (bf16[64,1024]{1,0:T(8,128)(2,1)S(1)}, bf16[64,1024]{1,0:T(8,128)(2,1)S(1)}, u32[]{:S(2)}, u32[]{:S(2)}) collective-permute-start(bf16[64,1024]{1,0:T(8,128)(2,1)S(1)} %get-tuple-element.64), channel_id=1, source_target_pairs={{0,6},{1,7},{2,0},{3,1},{4,2},{5,3},{6,4},{7,5},{8,14},{9,15},{10,... | collective-permute-start | bytes 393224 | tf_op jit(solution)/shard_map/ppermute | solution.py:298
  260.6 10.6 %collective-permute-start.9 = (bf16[64,1024]{1,0:T(8,128)(2,1)S(1)}, bf16[64,1024]{1,0:T(8,128)(2,1)S(1)}, u32[]{:S(2)}, u32[]{:S(2)}) collective-permute-start(bf16[64,1024]{1,0:T(8,128)(2,1)S(1)} %get-tuple-element.65), channel_id=1, source_target_pairs={{0,5},{1,6},{2,7},{3,0},{4,1},{5,2},{6,3},{7,4},{8,13},{9,14},{10,... | collective-permute-start | bytes 393224 | tf_op jit(solution)/shard_map/ppermute | solution.py:298
  (19 other events, 38.2 us)
Sparse Core Ops, SparseCore 0:
  97.6 54.9 reduce-scatter.1
  173.0 38.5 all-gather.1

commit v2 on v0

v2 whole, which is shorter than its diff:
```python
import functools
import math
import jax
import jax.numpy as jnp
from jax import lax
from jax.experimental import pallas as pl
from jax.experimental.pallas import tpu as pltpu
from jax.sharding import PartitionSpec as P

STEP = 4
decay_first = 0.9
decay_second = 0.95
learn_rate = 0.03
epsilon = 1e-08

CAP = 4
QUAD = 4
SUB, LANES = 16, 128
PART_A, COLS, COLS_B = 1152, 384, 128
SOON = (1, 7)
TOP = 32000.0
PER_OCTAVE = 64.0 / math.log(2.0)
f32, bf16, i32, i16 = jnp.float32, jnp.bfloat16, jnp.int32, jnp.int16
sds = jax.ShapeDtypeStruct
ANY = pl.BlockSpec(memory_space=pl.ANY)


def iota(shape, dim):
    return lax.broadcasted_iota(i32, shape, dim)


def ones(hit):
    return jnp.where(hit, 1.0, 0.0).astype(bf16)


def whole(shape):
    return pl.BlockSpec(shape, lambda *_: (0,) * len(shape))


def call(body, name, out_shape, grid, in_specs, out_specs, flops, nbytes, aliases=None, scratch=(), room=24):
    return pl.pallas_call(
        body,
        out_shape=out_shape,
        grid_spec=pltpu.PrefetchScalarGridSpec(
            num_scalar_prefetch=1,
            grid=grid,
            in_specs=in_specs,
            out_specs=out_specs,
            scratch_shapes=scratch,
        ),
        input_output_aliases=aliases or {},
        compiler_params=pltpu.CompilerParams(vmem_limit_bytes=room << 20),
        cost_estimate=pl.CostEstimate(flops=flops, bytes_accessed=nbytes, transcendentals=0),
        name=name,
    )


def to_i16(values):
    return values.astype(i32).astype(i16)


def to_f32(codes):
    return codes.astype(i32).astype(f32)


def encode(values):
    most = jnp.max(jnp.abs(values), axis=1, keepdims=True)
    level = jnp.ceil(jnp.log(jnp.maximum(most, 1e-30)) * PER_OCTAVE)
    return to_i16(jnp.round(values * (jnp.exp(level * (-1.0 / PER_OCTAVE)) * TOP))), level


def decode(codes, level):
    return to_f32(codes) * (jnp.exp(to_f32(level) * (1.0 / PER_OCTAVE)) * (1.0 / TOP))


def halves_dot(onehot, values):
    upper = values.astype(bf16)
    lower = (values - upper.astype(f32)).astype(bf16)
    return jnp.dot(onehot, upper, preferred_element_type=f32) + jnp.dot(
        onehot, lower, preferred_element_type=f32
    )


def codes_dot(onehot, codes):
    upper = jnp.floor(codes * (1.0 / 256.0))
    lower = codes - upper * 256.0
    return 256.0 * jnp.dot(onehot, upper.astype(bf16), preferred_element_type=f32) + jnp.dot(
        onehot, lower.astype(bf16), preferred_element_type=f32
    )


def positions(ids_row, owned):
    n = ids_row.shape[1]
    ids = jnp.broadcast_to(ids_row, (n, n))
    at, along = iota((n, n), 0), iota((n, n), 1)
    owner_row = ids // owned
    ids_col = jnp.sum(jnp.where(at == along, ids, 0), axis=1, keepdims=True)
    owner_col = jnp.broadcast_to(ids_col // owned, (n, n))
    same = owner_row == owner_col
    rank_row = jnp.sum(jnp.where(same & (at < along), 1, 0), axis=0, keepdims=True)
    rank_col = jnp.sum(jnp.where(same & (along < at), 1, 0), axis=1, keepdims=True)
    return owner_row[:1] * CAP + rank_row, owner_col[:, :1] * CAP + rank_col, ids_col


def place_of(at):
    return at // (QUAD * CAP) * CAP + at % CAP


def which(at):
    return at // CAP % QUAD


def load_columns(source, buf, sems, firsts):
    width = buf.shape[2]
    copies = [
        pltpu.make_async_copy(source.at[:, pl.ds(first, width)], buf.at[j], sems.at[j])
        for j, first in enumerate(firsts)
    ]
    for copy in copies:
        copy.start()
    return copies


def sums_kernel(width, me_ref, slots_ref, ids_ref, grads_ref, *refs):
    outs, (buf, sems) = refs[:-2], refs[-2:]
    reps, n, tokens, wa = len(outs), ids_ref.shape[1], slots_ref.shape[1], buf.shape[2]
    copies = load_columns(
        grads_ref,
        buf,
        sems,
        [pl.multiple_of((me_ref[1] + s) % reps * width, LANES) for s in range(reps)],
    )
    member = ones(jnp.broadcast_to(slots_ref[...], (n, tokens)) == iota((n, tokens), 0))
    lane = iota((SUB, LANES), 1)
    names = jnp.concatenate([jnp.broadcast_to(ids_ref[...], (SUB, n)), jnp.zeros((SUB, LANES - n), i32)], axis=1)
    for s in range(reps):
        copies[s].wait()
        codes, level = encode(jnp.dot(member, buf[s], preferred_element_type=f32))
        tile = names.astype(f32)
        for g in range(n // SUB):
            outs[s][:, g * wa : (g + 1) * wa] = codes[g * SUB : (g + 1) * SUB]
            tile = jnp.where(lane == n + g, level[g * SUB : (g + 1) * SUB], tile)
        outs[s][:, n // SUB * wa :] = to_i16(tile)


def send_kernel(width, wa, owned, me_ref, slots_ref, ids_ref, after_ref, grads_ref, out_ref, buf, made, sems, out_sems):
    reps, tokens, wb = buf.shape
    n, rows = ids_ref.shape[1], made.shape[0]
    copies = load_columns(
        grads_ref,
        buf,
        sems,
        [s * width + wa for s in range(reps)],
    )
    place_row, place_col, _ = positions(ids_ref[...], owned)
    slot = jnp.broadcast_to(slots_ref[...], (n, tokens))
    of_token = jnp.sum(
        jnp.where(slot == iota((n, tokens), 0), place_col, 0), axis=0, keepdims=True
    )
    at = iota((rows, tokens), 0)
    hit = place_of(at) == of_token
    member = jnp.concatenate([ones(hit & (which(at) == h)) for h in range(QUAD)], axis=1)
    local = ids_ref[...] % owned + 1
    held = jnp.sum(jnp.where(place_of(iota((rows, n), 0)) == place_row, local, 0), axis=1, keepdims=True)
    lane = iota((rows, LANES), 1)
    tile = jnp.where(lane == 2, held, 0).astype(f32)
    for copy in copies:
        copy.wait()
    sent = []
    for i in range(3):
        if i < 2:
            block = jnp.concatenate([buf[2 * h + i] for h in range(QUAD)], axis=0)
            codes, level = encode(jnp.dot(member, block, preferred_element_type=f32))
            tile = jnp.where(lane == i, level, tile)
            cut = pl.ds(i * wb, wb)
            made[:, cut] = codes
        else:
            cut = pl.ds(2 * wb, LANES)
            made[:, cut] = to_i16(tile)
        sent.append(pltpu.make_async_copy(made.at[:, cut], out_ref.at[:, cut], out_sems.at[i]))
        sent[-1].start()
    for copy in sent:
        copy.wait()


def route_kernel(owned, wa, me_ref, *refs):
    ins, (out_ref, made, sems) = refs[:-3], refs[-3:]
    rows = made.shape[0]
    groups = (ins[0].shape[1] - LANES) // wa
    n = groups * SUB
    lane = iota((rows, LANES), 1)
    tile = jnp.zeros((rows, LANES), f32)
    hits = []
    for j in range(len(ins) // QUAD):
        hot, extra = [], []
        for t in range(QUAD):
            last = ins[QUAD * j + t][:, groups * wa :].astype(i32)
            place_row, _, ids_col = positions(last[:1, :n], owned)
            at = iota((rows, n), 0)
            hot.append(ones((place_of(at) == place_row) & (which(at) == t)))
            level = jnp.concatenate([last[:, n + g : n + g + 1] for g in range(groups)], axis=0)
            pair = iota((n, LANES), 1)
            extra.append(
                jnp.where(pair == 2 * j, level, jnp.where(pair == 2 * j + 1, ids_col % owned + 1, 0)).astype(f32)
            )
        hits.append(jnp.concatenate(hot, axis=1))
        tile = tile + codes_dot(hits[j], jnp.concatenate(extra, axis=0))
    made[:, 2 * wa :] = to_i16(tile)
    sent = [pltpu.make_async_copy(made.at[:, pl.ds(2 * wa, LANES)], out_ref.at[:, pl.ds(2 * wa, LANES)], sems.at[0])]
    sent[-1].start()
    for c in range(wa // COLS):
        for j in range(len(hits)):
            codes = jnp.concatenate(
                [
                    to_f32(x[:, g * wa + c * COLS : g * wa + (c + 1) * COLS])
                    for x in ins[QUAD * j : QUAD * (j + 1)]
                    for g in range(groups)
                ],
                axis=0,
            )
            first = (2 * c + j) * COLS
            made[:, first : first + COLS] = to_i16(codes_dot(hits[j], codes))
        cut = pl.ds(2 * c * COLS, 2 * COLS)
        sent.append(pltpu.make_async_copy(made.at[:, cut], out_ref.at[:, cut], sems.at[c + 1]))
        sent[-1].start()
    for copy in sent:
        copy.wait()


def place_kernel(owned, wb, me_ref, in_ref, out_ref, made, sems):
    rows = in_ref.shape[0]
    tile = in_ref[:, 2 * wb :]
    held = tile[:, 2:3].astype(i32)
    shape = (rows, owned)
    hit = jnp.where(held == iota(shape, 1) + 1, 1.0, 0.0).T
    quarter = which(iota((owned, rows), 1))
    placer = jnp.concatenate(
        [jnp.where(quarter == h, hit, 0.0).astype(bf16) for h in range(QUAD)], axis=0
    )
    sent = []
    for i in range(2):
        values = decode(in_ref[:, i * wb : (i + 1) * wb], tile[:, i : i + 1])
        made[i] = halves_dot(placer, values)
        for h in range(QUAD):
            q = 2 * h + i
            sent.append(
                pltpu.make_async_copy(
                    made.at[i, pl.ds(h * owned, owned)], out_ref.at[pl.ds(q * owned, owned)], sems.at[q]
                )
            )
            sent[-1].start()
    for copy in sent:
        copy.wait()


def step(gradient, table_ref, first_ref, second_ref, new_table_ref, new_first_ref, new_second_ref):
    new_first = decay_first * first_ref[...] + (1.0 - decay_first) * gradient
    new_second = decay_second * second_ref[...] + (1.0 - decay_second) * gradient * gradient
    scaled_first = new_first / (1.0 - decay_first**STEP)
    scaled_second = new_second / (1.0 - decay_second**STEP)
    new_table = table_ref[...] - learn_rate * scaled_first / (jnp.sqrt(scaled_second) + epsilon)
    new_table_ref[...] = new_table
    new_first_ref[...] = new_first
    new_second_ref[...] = new_second
    return new_table.astype(bf16)


def adam_a_kernel(me_ref, tile_ref, in_ref, *refs):
    out_ref, hits, turned = refs[-3:]
    rows, owned = hits.shape[1:]
    tile = tile_ref[...]

    @pl.when(pl.program_id(0) == 0)
    def _():
        for j in range(2):
            held = tile[:, 2 * j + 1 : 2 * j + 2].astype(i32)
            hit = jnp.where(held == iota((rows, owned), 1) + 1, 1.0, 0.0)
            hits[j] = hit.astype(bf16)
            turned[j] = hit.T.astype(bf16)

    cols = in_ref.shape[1] // 2
    gradient = None
    for j in range(2):
        values = decode(in_ref[:, j * cols : (j + 1) * cols], tile[:, 2 * j : 2 * j + 1])
        term = halves_dot(turned[j], values)
        gradient = term if gradient is None else gradient + term
    half = step(gradient, *refs[:6])
    for j in range(2):
        out_ref[:, j * cols : (j + 1) * cols] = jnp.dot(
            hits[j], half, preferred_element_type=f32
        ).astype(bf16)


def adam_b_kernel(me_ref, grad_ref, *refs):
    refs[-1][...] = step(grad_ref[...], *refs[:3], *refs[-4:-1])


def pick_kernel(owned, wb, me_ref, tile_ref, in_ref, out_ref, made, sems):
    rows = made.shape[0]
    shape = (rows, owned)
    hit = tile_ref[...][:, 2:3].astype(i32) == iota(shape, 1) + 1
    quarter = which(iota(shape, 0))
    picker = jnp.concatenate([ones(hit & (quarter == h)) for h in range(QUAD)], axis=1)
    sent = []
    for i in range(2):
        block = jnp.concatenate(
            [in_ref[(2 * h + i) * owned : (2 * h + i + 1) * owned] for h in range(QUAD)], axis=0
        )
        cut = pl.ds(i * wb, wb)
        made[:, cut] = jnp.dot(picker, block, preferred_element_type=f32).astype(bf16)
        sent.append(pltpu.make_async_copy(made.at[:, cut], out_ref.at[:, cut], sems.at[i]))
        sent[-1].start()
    for copy in sent:
        copy.wait()


def unpad_kernel(owned, me_ref, in_ref, *refs):
    names, outs = refs[: len(refs) // 2], refs[len(refs) // 2 :]
    rows = in_ref.shape[0]
    n, wa = outs[0].shape
    for j in range(len(outs) // QUAD):
        finder = []
        for t in range(QUAD):
            _, col, _ = positions(names[QUAD * j + t][:1, :n].astype(i32), owned)
            at = iota((n, rows), 1)
            finder.append(ones((place_of(at) == col) & (which(at) == t)))
        finder = jnp.concatenate(finder, axis=0)
        for c in range(wa // COLS):
            first = (2 * c + j) * COLS
            found = jnp.dot(
                finder, in_ref[:, first : first + COLS], preferred_element_type=f32
            ).astype(bf16)
            for t in range(QUAD):
                outs[QUAD * j + t][:, c * COLS : (c + 1) * COLS] = found[t * n : (t + 1) * n]


def final_kernel(owned, reps, width, wa, me_ref, ids_ref, in_ref, *refs):
    ins, out_ref, found, sems, sem_b = refs[:reps], refs[-4], refs[-3], refs[-2], refs[-1]
    r = me_ref[1]
    wb = width - wa
    n, rows = out_ref.shape[0], in_ref.shape[0]
    copies = []
    for s in range(reps):
        start = pl.multiple_of((r + s) % reps * width, LANES)
        copies.append(pltpu.make_async_copy(ins[s], out_ref.at[:, pl.ds(start, wa)], sems.at[s]))
        copies[-1].start()
    _, col, _ = positions(ids_ref[...], owned)
    at = iota((n, rows), 1)
    hit = place_of(at) == col
    finder = jnp.concatenate([ones(hit & (which(at) == h)) for h in range(QUAD)], axis=0)
    for i in range(2):
        rows_b = jnp.dot(
            finder, in_ref[:, i * wb : (i + 1) * wb], preferred_element_type=f32
        ).astype(bf16)
        for h in range(QUAD):
            s = 2 * h + i
            found[s] = rows_b[h * n : (h + 1) * n]
            cut = pl.ds(s * width + wa, wb)
            copies.append(pltpu.make_async_copy(found.at[s], out_ref.at[:, cut], sem_b.at[s]))
            copies[-1].start()
    for copy in copies:
        copy.wait()


def shards(token_grads, token_slots, touched_ids, table, first_moment, second_moment):
    owners, reps = lax.axis_size("vocab"), lax.axis_size("rep")
    tokens, full = token_grads.shape
    touched = touched_ids.shape[0]
    owned, width = table.shape
    wa = PART_A
    wb = width - wa
    rows = owners * QUAD * CAP
    slots = token_slots.reshape(1, tokens)
    ids = touched_ids.reshape(1, touched)
    me = jnp.stack([lax.axis_index("vocab"), lax.axis_index("rep")]).astype(i32)
    dma = pltpu.SemaphoreType.DMA

    def over_vocab(x):
        x = x.reshape(owners, QUAD * CAP, -1)
        return lax.all_to_all(x, "vocab", split_axis=0, concat_axis=0, tiled=True).reshape(rows, -1)

    def shift(x, s):
        if s == 0:
            return x
        return lax.ppermute(x, "rep", [(i, (i + s) % reps) for i in range(reps)])

    def together(*lists):
        done = lax.optimization_barrier(tuple(x for many in lists for x in many))
        starts = [sum(map(len, lists[:j])) for j in range(len(lists))]
        return [done[first : first + len(many)] for first, many in zip(starts, lists)]

    wide = touched // SUB * wa + LANES
    sums = call(
        functools.partial(sums_kernel, width),
        "sums",
        [sds((SUB, wide), i16)] * reps,
        (1,),
        [whole((1, tokens)), whole((1, touched)), ANY],
        [whole((SUB, wide))] * reps,
        2 * touched * tokens * wa * reps,
        (tokens + touched) * 2 * wa * reps,
        scratch=[pltpu.VMEM((reps, tokens, wa), bf16), dma((reps,))],
    )(me, slots, ids, token_grads)
    group = [shift(x, s) for s, x in enumerate(sums)]

    out_b = call(
        functools.partial(send_kernel, width, wa, owned),
        "send",
        sds((rows, 2 * wb + LANES), i16),
        (1,),
        [whole((1, tokens)), whole((1, touched)), ANY, ANY],
        ANY,
        16 * rows * tokens * wb,
        (tokens * reps + rows * 2) * 2 * wb,
        scratch=[
            pltpu.VMEM((reps, tokens, wb), bf16),
            pltpu.VMEM((rows, 2 * wb + LANES), i16),
            dma((reps,)),
            dma((3,)),
        ],
    )(me, slots, ids, sums[0], token_grads)
    arrived_b = over_vocab(out_b)
    tile_b = pl.BlockSpec((rows, LANES), lambda i, me: (0, 2 * wb // LANES))

    dense = call(
        functools.partial(place_kernel, owned, wb),
        "place",
        sds((reps * owned, wb), f32),
        (1,),
        [whole((rows, 2 * wb + LANES))],
        ANY,
        8 * rows * QUAD * owned * wb,
        (rows + owned * reps) * 4 * wb,
        scratch=[pltpu.VMEM((2, QUAD * owned, wb), f32), dma((reps,))],
    )(me, arrived_b)
    group, (dense,) = together(group, [dense])
    gradient_b = lax.psum_scatter(dense, "rep", scatter_dimension=0, tiled=True)

    steps_a = wa // COLS
    wide_a = 2 * wa + LANES
    out_a = call(
        functools.partial(route_kernel, owned, wa),
        "route",
        sds((rows, wide_a), i16),
        (1,),
        [whole((SUB, wide))] * reps,
        ANY,
        8 * rows * QUAD * touched * wa,
        (rows * 2 + reps * touched) * 2 * wa,
        scratch=[pltpu.VMEM((rows, wide_a), i16), dma((steps_a + 1,))],
    )(me, *group)
    arrived_a = over_vocab(out_a)

    spec = pl.BlockSpec((owned, COLS), lambda i, me: (0, i))
    pair = pl.BlockSpec((rows, 2 * COLS), lambda i, me: (0, i))
    *news, back_a = call(
        adam_a_kernel,
        "adam_a",
        [*(sds((owned, width), f32) for _ in range(3)), sds((rows, 2 * wa), bf16)],
        (steps_a,),
        [pl.BlockSpec((rows, LANES), lambda i, me: (0, 2 * wa // LANES)), pair, spec, spec, spec],
        [spec, spec, spec, pair],
        12 * rows * owned * wa,
        (rows * 8 + owned * 24) * wa,
        scratch=[pltpu.VMEM((2, rows, owned), bf16), pltpu.VMEM((2, owned, rows), bf16)],
    )(me, arrived_a, arrived_a, table, first_moment, second_moment)
    spec_b = pl.BlockSpec((owned, COLS_B), lambda i, me: (0, wa // COLS_B + i))
    spec_h = pl.BlockSpec((owned, COLS_B), lambda i, me: (0, i))
    *news, half_b = call(
        adam_b_kernel,
        "adam_b",
        [*(sds((owned, width), f32) for _ in range(3)), sds((owned, wb), bf16)],
        (wb // COLS_B,),
        [spec_h, spec_b, spec_b, spec_b, ANY, ANY, ANY],
        [spec_b, spec_b, spec_b, spec_h],
        20 * owned * wb,
        30 * owned * wb,
        aliases={5 + j: j for j in range(3)},
    )(me, gradient_b, table, first_moment, second_moment, *news)
    rows_b = lax.all_gather(half_b, "rep", axis=0, tiled=True)

    returned_a = over_vocab(back_a)

    mine_a = call(
        functools.partial(unpad_kernel, owned),
        "unpad",
        [sds((touched, wa), bf16)] * reps,
        (1,),
        [whole((rows, 2 * wa))]
        + [pl.BlockSpec((SUB, LANES), lambda i, me: (0, touched // SUB * wa // LANES))] * reps,
        [whole((touched, wa))] * reps,
        2 * reps * touched * rows * wa,
        (rows * 2 + reps * touched) * 2 * wa,
    )(me, returned_a, *group)
    home_a = [shift(x, (reps - s) % reps) for s, x in enumerate(mine_a)]
    first, (rows_b,) = together([home_a[s] for s in SOON], [rows_b])
    for s, x in zip(SOON, first):
        home_a[s] = x
    back_b = call(
        functools.partial(pick_kernel, owned, wb),
        "pick",
        sds((rows, 2 * wb), bf16),
        (1,),
        [tile_b, whole((reps * owned, wb))],
        ANY,
        4 * rows * QUAD * owned * wb,
        (reps * owned + 2 * rows) * wb * 2,
        scratch=[pltpu.VMEM((rows, 2 * wb), bf16), dma((2,))],
    )(me, arrived_b, rows_b)
    returned_b = over_vocab(back_b)

    refreshed = call(
        functools.partial(final_kernel, owned, reps, width, wa),
        "final",
        sds((touched, full), bf16),
        (1,),
        [whole((1, touched)), whole((rows, 2 * wb))] + [whole((touched, wa))] * reps,
        ANY,
        16 * touched * rows * wb,
        touched * full * 4,
        scratch=[pltpu.VMEM((reps, touched, wb), bf16), dma((reps,)), dma((reps,))],
    )(me, ids, returned_b, *home_a)
    return (*news, refreshed)


def solution(mesh):
    return jax.shard_map(
        shards,
        mesh=mesh,
        in_specs=(
            P(("vocab", "rep"), None),
            P(("vocab", "rep")),
            P(("vocab", "rep")),
            P("vocab", "rep"),
            P("vocab", "rep"),
            P("vocab", "rep"),
        ),
        out_specs=(
            P("vocab", "rep"),
            P("vocab", "rep"),
            P("vocab", "rep"),
            P(("vocab", "rep"), None),
        ),
        check_vma=False,
    )
```

time: 567 us -> 223 us (0.39); the launches traced: 557 us -> 220 us
  waiting for transfers between devices: 346 us -> 33.8 us
  local copies, waits for them, and re-layouts: 66.1 us -> 15.6 us
  Pallas kernels: 0 us -> 33.6 us
  other arithmetic: 19.9 us -> 0.08 us
  starting transfers between devices: 30.9 us -> 47.2 us
  matrix products: 10.9 us -> 0 us
  blocking collectives: 67.8 us -> 75.8 us
    all_to_all x4 -> x2, waiting for transfers between devices: 283 us -> 4.29 us  [over_vocab(): lax.all_to_all(x, 'vocab', split_axis=0, concat_axis=0, tiled=True)]
    all_gather x1, waiting for transfers between devices: 63.5 us -> 0.01 us  [shards(): rows_b = lax.all_gather(half_b, 'rep', axis=0, tiled=True)]
    ppermute x0 -> x14, starting transfers between devices: none -> 34.2 us  [shift(): return lax.ppermute(x, 'rep', [(i, (i + s) % reps) for i in range(reps)])]
    pallas_call x0 -> x9, Pallas kernels: none -> 33.6 us  [the longest x1 6.15 us: shards(): call(adam_a_kernel, 'adam_a', [*(sds((owned, width), f32) for _ in range(...]
    ppermute x0 -> x14, waiting for transfers between devices: none -> 29.5 us  [shift(): return lax.ppermute(x, 'rep', [(i, (i + s) % reps) for i in range(reps)])]
    gather x4 -> x0, local copies, waits for them, and re-layouts: 25.5 us -> none  [the longest x1 12.3 us: shards(): jnp.take(shard_rows, jnp.clip(wanted, 0, shard_rows.shape[0] - 1), axis=0)]
    all_to_all x5 -> x0, local copies, waits for them, and re-layouts: 22.1 us -> none  [the longest x1 11 us: shards(): lax.all_to_all(lax.all_to_all(outgoing, 'vocab', split_axis=0, concat_axi...]
    select_n x6 -> x0, other arithmetic: 18.8 us -> none  [the longest x1 15.3 us: shards(): jnp.where(filled[:, :, None], jnp.take(summed, source, axis=0), 0.0)]
  transfers between devices with their start and end apart: 5 -> 18, of which waited for: 3 -> 9; matrix products, arithmetic and copies ran while one was open for 11% -> 0% of each run, Pallas kernels for 0% -> 8%
where the time goes in v2:
time: 223 us; the launch traced here: 220 us
  blocking collectives  75.8 us (34%)
  starting transfers between devices  47.2 us (21%)
  waiting for transfers between devices  33.8 us (15%)
  Pallas kernels  33.6 us (15%)
  local copies, waits for them, and re-layouts  15.6 us (7%)
  between operations  14.4 us (6%)
    all_to_all x2, blocking collectives, over_vocab(): lax.all_to_all(x, 'vocab', split_axis=0, concat_axis=0, tiled=True)  75.8 us
    ppermute x14, starting transfers between devices, shift(): return lax.ppermute(x, 'rep', [(i, (i + s) % reps) for i in range(reps)])  34.2 us
    ppermute x14, waiting for transfers between devices, shift(): return lax.ppermute(x, 'rep', [(i, (i + s) % reps) for i in range(reps)])  29.5 us
    unnamed x60, local copies, waits for them, and re-layouts  15.6 us
    all_to_all x2, starting transfers between devices, over_vocab(): lax.all_to_all(x, 'vocab', split_axis=0, concat_axis=0, tiled=True)  12.8 us
    pallas_call x1, Pallas kernels, shards(): call(adam_a_kernel, 'adam_a', [*(sds((owned, width), f32) for _ in range(...  6.15 us
    pallas_call x1, Pallas kernels, shards(): call(functools.partial(place_kernel, owned, wb), 'place', sds((reps * own...  5.63 us
  transfers between devices with their start and end apart: 18, of which 9 were waited for; matrix products, arithmetic and copies ran while one was open for 0% of the time, Pallas kernels for 8%

profile of v2, /device:TPU:2, one launch (start us, length us, event | category | flops | bytes accessed | tf_op | source)
XLA Modules:
  0.0 220.5 jit_solution(16661742041119967411)
XLA Ops:
  7.3 2.2 copy-done
  10.8 3.8 %sums.1 = (s16[16,4736]{1,0:T(8,128)(2,1)S(1)}, s16[16,4736]{1,0:T(8,128)(2,1)S(1)}, s16[16,4736]{1,0:T(8,128)(2,1)S(1)}, s16[16,4736]{1,0:T(8,128)(2,1)}, s16[1...) custom-call(s32[2]{0:T(128)S(1)} %pad_add_fusion.me_ref, ...), custom_call_target="tpu_custom_call" | custom-call | flops 150994944 | bytes 3538944 | tf_op jit(solution)/shard_map/sums/pallas_call | solution.py:393
  14.6 3.4 %send.1 = s16[512,1920]{1,0:T(8,128)(2,1)S(1)} custom-call(s32[2]{0:T(128)S(1)} %pad_add_fusion.me_ref, s32[1,128]{1,0:T(1,128)S(1)} %bitcast.26, s32[1,64]{1,0:T(1,128)S(1)} %bitcast.23, s16[16,4736]{1,0:T(8,128)(2,1)S(1)} %get-tuple-element.49.after_ref.refs_0_, bf16[128,16384]{1,0:T(8,128)(2,1)S(1)} %copy-done), custom_call_target="tpu_custom_call" | custom-call | flops 939524096 | bytes 3670016 | tf_op jit(solution)/shard_map/send/pallas_call | solution.py:406
  19.3 7.6 %all-to-all-start = ((s16[32,16,1920]{2,1,0:T(8,128)(2,1)}), s16[32,16,1920]{2,1,0:T(8,128)(2,1)S(1)}, u32[]{:S(2)}, u32[]{:S(2)}) async-start(s16[32,16,1920]{2,1,0:T(8,128)(2,1)} %bitcast.17), calls=%async_computation | async-start | bytes 3932160 | tf_op jit(solution)/shard_map/all_to_all | solution.py:380
  27.0 2.0 collective-permute-start
  29.0 3.3 %collective-permute-start.1 = (s16[16,4736]{1,0:T(8,128)(2,1)S(1)}, s16[16,4736]{1,0:T(8,128)(2,1)S(1)}, u32[]{:S(2)}, u32[]{:S(2)}) collective-permute-start(s16[16,4736]{1,0:T(8,128)(2,1)S(1)} %get-tuple-element.42), channel_id=1, source_target_pairs={{0,2},{1,3},{2,4},{3,5},{4,6},{5,7},{6,0},{7,1},{8,10},{9,11},{10,... | collective-permute-start | bytes 454664 | tf_op jit(solution)/shard_map/ppermute | solution.py:385
  32.2 4.0 %collective-permute-start.2 = (s16[16,4736]{1,0:T(8,128)(2,1)}, s16[16,4736]{1,0:T(8,128)(2,1)S(1)}, u32[]{:S(2)}, u32[]{:S(2)}) collective-permute-start(s16[16,4736]{1,0:T(8,128)(2,1)} %get-tuple-element.43), channel_id=1, source_target_pairs={{0,3},{1,4},{2,5},{3,6},{4,7},{5,0},{6,1},{7,2},{8,11},{9,12},{10,... | collective-permute-start | bytes 454664 | tf_op jit(solution)/shard_map/ppermute | solution.py:385
  36.8 4.9 %collective-permute-start.4 = (s16[16,4736]{1,0:T(8,128)(2,1)}, s16[16,4736]{1,0:T(8,128)(2,1)S(1)}, u32[]{:S(2)}, u32[]{:S(2)}) collective-permute-start(s16[16,4736]{1,0:T(8,128)(2,1)} %get-tuple-element.45), channel_id=1, source_target_pairs={{0,5},{1,6},{2,7},{3,0},{4,1},{5,2},{6,3},{7,4},{8,13},{9,14},{10,... | collective-permute-start | bytes 454664 | tf_op jit(solution)/shard_map/ppermute | solution.py:385
  41.8 2.7 %collective-permute-start.5 = (s16[16,4736]{1,0:T(8,128)(2,1)}, s16[16,4736]{1,0:T(8,128)(2,1)S(1)}, u32[]{:S(2)}, u32[]{:S(2)}) collective-permute-start(s16[16,4736]{1,0:T(8,128)(2,1)} %get-tuple-element.46), channel_id=1, source_target_pairs={{0,6},{1,7},{2,0},{3,1},{4,2},{5,3},{6,4},{7,5},{8,14},{9,15},{10,... | collective-permute-start | bytes 454664 | tf_op jit(solution)/shard_map/ppermute | solution.py:385
  44.4 2.4 %collective-permute-done.1.refs_2_ = s16[16,4736]{1,0:T(8,128)(2,1)S(1)} collective-permute-done((s16[16,4736]{1,0:T(8,128)(2,1)S(1)}, s16[16,4736]{1,0:T(8,128)(2,1)S(1)}, u32[]{:S(2)}, u32[]{:S(2)}) %collective-permute-start.1) | collective-permute-done | bytes 151584 | tf_op jit(solution)/shard_map/ppermute | solution.py:385
  46.9 2.2 collective-permute-start.6
  49.0 4.3 %all-to-all-done = s16[32,16,1920]{2,1,0:T(8,128)(2,1)S(1)} async-done(((s16[32,16,1920]{2,1,0:T(8,128)(2,1)}), s16[32,16,1920]{2,1,0:T(8,128)(2,1)S(1)}, u32[]{:S(2)}, u32[]{:S(2)}) %all-to-all-start) | async-done | bytes 1966112 | tf_op jit(solution)/shard_map/all_to_all | solution.py:380
  53.3 5.6 %place.1 = f32[1024,896]{1,0:T(8,128)S(1)} custom-call(s32[2]{0:T(128)S(1)} %pad_add_fusion.me_ref, s16[512,1920]{1,0:T(8,128)(2,1)S(1)} %bitcast.15), custom_call_target="tpu_custom_call" | custom-call | flops 1879048192 | bytes 5505024 | tf_op jit(solution)/shard_map/place/pallas_call | solution.py:425
  59.0 1.8 copy-done.8
  60.8 3.2 %collective-permute-done.5.refs_6_ = s16[16,4736]{1,0:T(8,128)(2,1)S(1)} collective-permute-done((s16[16,4736]{1,0:T(8,128)(2,1)}, s16[16,4736]{1,0:T(8,128)(2,1)S(1)}, u32[]{:S(2)}, u32[]{:S(2)}) %collective-permute-start.5) | collective-permute-done | bytes 151584 | tf_op jit(solution)/shard_map/ppermute | solution.py:385
  65.1 4.2 %route.1 = s16[512,2432]{1,0:T(8,128)(2,1)S(1)} custom-call(s32[2]{0:T(128)S(1)} %pad_add_fusion.me_ref, s16[16,4736]{1,0:T(8,128)(2,1)S(1)} %get-tuple-element.49.after_ref.refs_0_, s16[16,4736]{1,0:T(8,128)(2,1)S(1)} %collective-permute-done.refs_1_, s16[16,4736]{1,0:T(8,128)(2,1)S(1)} %collective-permute-done.1.refs_2_, ...), custom_call_target="tpu_custom_call" | custom-call | flops 1207959552 | bytes 3538944 | tf_op jit(solution)/shard_map/route/pallas_call | solution.py:441
  69.4 39.0 %all_to_all.20 = s16[32,16,2432]{2,1,0:T(8,128)(2,1)S(1)} all-to-all(s16[32,16,2432]{2,1,0:T(8,128)(2,1)S(1)} %bitcast.20), channel_id=1, replica_groups=mesh['vocab'=32,'rep'=8] {'vocab'}, dimensions={0} | all-to-all | bytes 4980736 | tf_op jit(solution)/shard_map/all_to_all | solution.py:380
  108.4 6.1 %adam_a.1 = (f32[128,2048]{1,0:T(8,128)}, f32[128,2048]{1,0:T(8,128)}, f32[128,2048]{1,0:T(8,128)}, bf16[512,2304]{1,0:T(8,128)(2,1)S(1)}) custom-call(s32[2]{0:T(128)S(1)} %pad_add_fusion.me_ref, s16[512,2432]{1,0:T(8,128)(2,1)S(1)} %bitcast.12, s16[512,2432]{1,0:T(8,128)(2,1)S(1)} %bitcast.13, f32[128,2048]{1,0:T(8,128)S(1)} %copy-done.3, ...), custom_call_target="tpu_custom_call" | custom-call | flops 905969664 | bytes 8257536 | tf_op jit(solution)/shard_map/adam_a/pallas_call | solution.py:456
  119.5 3.6 %adam_b.1 = (f32[128,2048]{1,0:T(8,128)}, f32[128,2048]{1,0:T(8,128)}, f32[128,2048]{1,0:T(8,128)}, bf16[128,896]{1,0:T(8,128)(2,1)}) custom-call(s32[2]{0:T(128)S(1)} %pad_add_fusion.me_ref, f32[128,896]{1,0:T(8,128)S(1)} %copy-done.11, f32[128,2048]{1,0:T(8,128)S(1)} %copy-done.3, ...), custom_call_target="tpu_custom_call", output_to_operand_aliasing={{0}: (5, {}), {1}: (6, {}), {2}: (7, {})} | custom-call | flops 2293760 | bytes 3440640 | tf_op jit(solution)/shard_map/adam_b/pallas_call | solution.py:469
  123.2 36.8 %all_to_all.21 = bf16[32,16,2304]{2,1,0:T(8,128)(2,1)S(1)} all-to-all(bf16[32,16,2304]{2,1,0:T(8,128)(2,1)} %bitcast.21), channel_id=1, replica_groups=mesh['vocab'=32,'rep'=8] {'vocab'}, dimensions={0} | all-to-all | bytes 4718592 | tf_op jit(solution)/shard_map/all_to_all | solution.py:380
  160.0 2.4 %unpad.1 = (bf16[64,1152]{1,0:T(8,128)(2,1)S(1)}, bf16[64,1152]{1,0:T(8,128)(2,1)S(1)}, bf16[64,1152]{1,0:T(8,128)(2,1)}, bf16[64,1152]{1,0:T(8,128)(2,1)}, bf16...) custom-call(s32[2]{0:T(128)S(1)} %pad_add_fusion.me_ref, ...), custom_call_target="tpu_custom_call" | custom-call | flops 603979776 | bytes 3538944 | tf_op jit(solution)/shard_map/unpad/pallas_call | solution.py:484
  166.1 4.5 %collective-permute-done.7.refs_1_ = bf16[64,1152]{1,0:T(8,128)(2,1)S(1)} collective-permute-done((bf16[64,1152]{1,0:T(8,128)(2,1)S(1)}, bf16[64,1152]{1,0:T(8,128)(2,1)S(1)}, u32[]{:S(2)}, u32[]{:S(2)}) %collective-permute-start.7) | collective-permute-done | bytes 147488 | tf_op jit(solution)/shard_map/ppermute | solution.py:385
  170.5 1.8 collective-permute-done.8.refs_7_
  173.8 2.2 pick.1
  177.2 5.1 %all-to-all-start.3 = ((bf16[32,16,1792]{2,1,0:T(8,128)(2,1)}), bf16[32,16,1792]{2,1,0:T(8,128)(2,1)S(1)}, u32[]{:S(2)}, u32[]{:S(2)}) async-start(bf16[32,16,1792]{2,1,0:T(8,128)(2,1)} %bitcast.19), calls=%async_computation.4 | async-start | bytes 3670016 | tf_op jit(solution)/shard_map/all_to_all | solution.py:380
  183.3 3.6 %collective-permute-start.10 = (bf16[64,1152]{1,0:T(8,128)(2,1)}, bf16[64,1152]{1,0:T(8,128)(2,1)S(1)}, u32[]{:S(2)}, u32[]{:S(2)}) collective-permute-start(bf16[64,1152]{1,0:T(8,128)(2,1)} %get-tuple-element.71), channel_id=1, source_target_pairs={{0,5},{1,6},{2,7},{3,0},{4,1},{5,2},{6,3},{7,4},{8,13},{9,14},{10,... | collective-permute-start | bytes 442376 | tf_op jit(solution)/shard_map/ppermute | solution.py:385
  186.9 1.7 collective-permute-start.11
  188.6 2.3 %collective-permute-start.12 = (bf16[64,1152]{1,0:T(8,128)(2,1)S(1)}, bf16[64,1152]{1,0:T(8,128)(2,1)S(1)}, u32[]{:S(2)}, u32[]{:S(2)}) collective-permute-start(bf16[64,1152]{1,0:T(8,128)(2,1)S(1)} %copy-done.29), channel_id=1, source_target_pairs={{0,3},{1,4},{2,5},{3,6},{4,7},{5,0},{6,1},{7,2},{8,11},{9,12},{10,... | collective-permute-start | bytes 442376 | tf_op jit(solution)/shard_map/ppermute | solution.py:385
  191.0 3.6 %collective-permute-start.13 = (bf16[64,1152]{1,0:T(8,128)(2,1)S(1)}, bf16[64,1152]{1,0:T(8,128)(2,1)S(1)}, u32[]{:S(2)}, u32[]{:S(2)}) collective-permute-start(bf16[64,1152]{1,0:T(8,128)(2,1)S(1)} %copy-done.27), channel_id=1, source_target_pairs={{0,2},{1,3},{2,4},{3,5},{4,6},{5,7},{6,0},{7,1},{8,10},{9,11},{10,... | collective-permute-start | bytes 442376 | tf_op jit(solution)/shard_map/ppermute | solution.py:385
  194.6 6.1 %collective-permute-done.10.refs_3_ = bf16[64,1152]{1,0:T(8,128)(2,1)S(1)} collective-permute-done((bf16[64,1152]{1,0:T(8,128)(2,1)}, bf16[64,1152]{1,0:T(8,128)(2,1)S(1)}, u32[]{:S(2)}, u32[]{:S(2)}) %collective-permute-start.10) | collective-permute-done | bytes 147488 | tf_op jit(solution)/shard_map/ppermute | solution.py:385
  201.8 9.5 %collective-permute-done.12.refs_5_ = bf16[64,1152]{1,0:T(8,128)(2,1)S(1)} collective-permute-done((bf16[64,1152]{1,0:T(8,128)(2,1)S(1)}, bf16[64,1152]{1,0:T(8,128)(2,1)S(1)}, u32[]{:S(2)}, u32[]{:S(2)}) %collective-permute-start.12) | collective-permute-done | bytes 147488 | tf_op jit(solution)/shard_map/ppermute | solution.py:385
  211.4 2.2 %final.1 = bf16[64,16384]{1,0:T(8,128)(2,1)} custom-call(s32[2]{0:T(128)S(1)} %pad_add_fusion.me_ref, s32[1,64]{1,0:T(1,128)S(1)} %bitcast.24, bf16[512,1792]{1,0:T(8,128)(2,1)S(1)} %bitcast.18, bf16[64,1152]{1,0:T(8,128)(2,1)S(1)} %get-tuple-element.68.refs_0_, bf16[64,1152]{1,0:T(8,128)(2,1)S(1)} %collective-permute-done.7.refs_1_, ...), custom_call_target="tpu_custom_call" | custom-call | flops 469762048 | bytes 4194304 | tf_op jit(solution)/shard_map/final/pallas_call | solution.py:512
  (78 shorter events, 17.9 us)
Async XLA Ops:
  7.2 7.5 %copy-start.25 = (s32[128]{0:T(128)S(1)}, s32[128]{0:T(128)}, u32[]{:S(2)}) copy-start(s32[128]{0:T(128)} %param.7) | copy-start | bytes 1540
  19.3 34.0 %all-to-all-start = ((s16[32,16,1920]{2,1,0:T(8,128)(2,1)}), s16[32,16,1920]{2,1,0:T(8,128)(2,1)S(1)}, u32[]{:S(2)}, u32[]{:S(2)}) async-start(s16[32,16,1920]{2,1,0:T(8,128)(2,1)} %bitcast.17), calls=%async_computation | async-start | bytes 3932160 | tf_op jit(solution)/shard_map/all_to_all | solution.py:380
  26.9 89.1 %reduce-scatter.2.cloned.1.call-start = ((), (), s32[]{:S(2)}) async-start(), calls=%async_computation.5 | async-start | bytes 4128768 | tf_op jit(solution)/shard_map/reduce_scatter | solution.py:437
  27.0 14.8 %collective-permute-start = (s16[16,4736]{1,0:T(8,128)(2,1)S(1)}, s16[16,4736]{1,0:T(8,128)(2,1)S(1)}, u32[]{:S(2)}, u32[]{:S(2)}) collective-permute-start(s16[16,4736]{1,0:T(8,128)(2,1)S(1)} %get-tuple-element.41), channel_id=1, source_target_pairs={{0,1},{1,2},{2,3},{3,4},{4,5},{5,6},{6,7},{7,0},{8,9},{9,10},{10,1... | collective-permute-start | bytes 454664 | tf_op jit(solution)/shard_map/ppermute | solution.py:385
  29.0 17.9 %collective-permute-start.1 = (s16[16,4736]{1,0:T(8,128)(2,1)S(1)}, s16[16,4736]{1,0:T(8,128)(2,1)S(1)}, u32[]{:S(2)}, u32[]{:S(2)}) collective-permute-start(s16[16,4736]{1,0:T(8,128)(2,1)S(1)} %get-tuple-element.42), channel_id=1, source_target_pairs={{0,2},{1,3},{2,4},{3,5},{4,6},{5,7},{6,0},{7,1},{8,10},{9,11},{10,... | collective-permute-start | bytes 454664 | tf_op jit(solution)/shard_map/ppermute | solution.py:385
  32.2 28.5 %collective-permute-start.2 = (s16[16,4736]{1,0:T(8,128)(2,1)}, s16[16,4736]{1,0:T(8,128)(2,1)S(1)}, u32[]{:S(2)}, u32[]{:S(2)}) collective-permute-start(s16[16,4736]{1,0:T(8,128)(2,1)} %get-tuple-element.43), channel_id=1, source_target_pairs={{0,3},{1,4},{2,5},{3,6},{4,7},{5,0},{6,1},{7,2},{8,11},{9,12},{10,... | collective-permute-start | bytes 454664 | tf_op jit(solution)/shard_map/ppermute | solution.py:385
  36.3 24.5 %collective-permute-start.3 = (s16[16,4736]{1,0:T(8,128)(2,1)}, s16[16,4736]{1,0:T(8,128)(2,1)S(1)}, u32[]{:S(2)}, u32[]{:S(2)}) collective-permute-start(s16[16,4736]{1,0:T(8,128)(2,1)} %get-tuple-element.44), channel_id=1, source_target_pairs={{0,4},{1,5},{2,6},{3,7},{4,0},{5,1},{6,2},{7,3},{8,12},{9,13},{10,... | collective-permute-start | bytes 454664 | tf_op jit(solution)/shard_map/ppermute | solution.py:385
  36.8 23.9 %collective-permute-start.4 = (s16[16,4736]{1,0:T(8,128)(2,1)}, s16[16,4736]{1,0:T(8,128)(2,1)S(1)}, u32[]{:S(2)}, u32[]{:S(2)}) collective-permute-start(s16[16,4736]{1,0:T(8,128)(2,1)} %get-tuple-element.45), channel_id=1, source_target_pairs={{0,5},{1,6},{2,7},{3,0},{4,1},{5,2},{6,3},{7,4},{8,13},{9,14},{10,... | collective-permute-start | bytes 454664 | tf_op jit(solution)/shard_map/ppermute | solution.py:385
  41.8 22.2 %collective-permute-start.5 = (s16[16,4736]{1,0:T(8,128)(2,1)}, s16[16,4736]{1,0:T(8,128)(2,1)S(1)}, u32[]{:S(2)}, u32[]{:S(2)}) collective-permute-start(s16[16,4736]{1,0:T(8,128)(2,1)} %get-tuple-element.46), channel_id=1, source_target_pairs={{0,6},{1,7},{2,0},{3,1},{4,2},{5,3},{6,4},{7,5},{8,14},{9,15},{10,... | collective-permute-start | bytes 454664 | tf_op jit(solution)/shard_map/ppermute | solution.py:385
  46.9 18.0 %collective-permute-start.6 = (s16[16,4736]{1,0:T(8,128)(2,1)S(1)}, s16[16,4736]{1,0:T(8,128)(2,1)S(1)}, u32[]{:S(2)}, u32[]{:S(2)}) collective-permute-start(s16[16,4736]{1,0:T(8,128)(2,1)S(1)} %get-tuple-element.47), channel_id=1, source_target_pairs={{0,7},{1,0},{2,1},{3,2},{4,3},{5,4},{6,5},{7,6},{8,15},{9,8},{10,9... | collective-permute-start | bytes 454664 | tf_op jit(solution)/shard_map/ppermute | solution.py:385
  60.7 8.6 %copy-start.12 = (s16[16,4736]{1,0:T(8,128)(2,1)}, s16[16,4736]{1,0:T(8,128)(2,1)S(1)}, u32[]{:S(2)}) copy-start(s16[16,4736]{1,0:T(8,128)(2,1)S(1)} %collective-permute-done.2.refs_3_) | copy-start | bytes 454660
  60.7 8.6 %copy-start.14 = (s16[16,4736]{1,0:T(8,128)(2,1)}, s16[16,4736]{1,0:T(8,128)(2,1)S(1)}, u32[]{:S(2)}) copy-start(s16[16,4736]{1,0:T(8,128)(2,1)S(1)} %collective-permute-done.3.refs_4_) | copy-start | bytes 454660
  60.8 8.6 %copy-start.16 = (s16[16,4736]{1,0:T(8,128)(2,1)}, s16[16,4736]{1,0:T(8,128)(2,1)S(1)}, u32[]{:S(2)}) copy-start(s16[16,4736]{1,0:T(8,128)(2,1)S(1)} %collective-permute-done.4.refs_5_) | copy-start | bytes 454660
  64.9 107.4 %all-gather.2.cloned.1.call-start = ((), (), s32[]{:S(2)}) async-start(), calls=%async_computation.6 | async-start | bytes 2064384 | tf_op jit(solution)/shard_map/all_gather | solution.py:480
  69.4 39.0 %copy-start.3 = (f32[128,2048]{1,0:T(8,128)S(1)}, f32[128,2048]{1,0:T(8,128)}, u32[]{:S(2)}) copy-start(f32[128,2048]{1,0:T(8,128)} %refs_0_.3) | copy-start | bytes 3145732
  69.4 39.0 %copy-start.4 = (f32[128,2048]{1,0:T(8,128)S(1)}, f32[128,2048]{1,0:T(8,128)}, u32[]{:S(2)}) copy-start(f32[128,2048]{1,0:T(8,128)} %refs_1_.3) | copy-start | bytes 3145732
  69.4 39.0 %copy-start.6 = (f32[128,2048]{1,0:T(8,128)S(1)}, f32[128,2048]{1,0:T(8,128)}, u32[]{:S(2)}) copy-start(f32[128,2048]{1,0:T(8,128)} %refs_2_.3) | copy-start | bytes 3145732
  123.1 36.8 %copy-start.13 = (s16[16,4736]{1,0:T(8,128)(2,1)S(1)}, s16[16,4736]{1,0:T(8,128)(2,1)}, u32[]{:S(2)}) copy-start(s16[16,4736]{1,0:T(8,128)(2,1)} %copy-done.12) | copy-start | bytes 454660
  123.1 36.8 %copy-start.15 = (s16[16,4736]{1,0:T(8,128)(2,1)S(1)}, s16[16,4736]{1,0:T(8,128)(2,1)}, u32[]{:S(2)}) copy-start(s16[16,4736]{1,0:T(8,128)(2,1)} %copy-done.14) | copy-start | bytes 454660
  123.2 36.8 %copy-start.17 = (s16[16,4736]{1,0:T(8,128)(2,1)S(1)}, s16[16,4736]{1,0:T(8,128)(2,1)}, u32[]{:S(2)}) copy-start(s16[16,4736]{1,0:T(8,128)(2,1)} %copy-done.16) | copy-start | bytes 454660
  123.2 36.8 %copy-start.19 = (s16[16,4736]{1,0:T(8,128)(2,1)S(1)}, s16[16,4736]{1,0:T(8,128)(2,1)}, u32[]{:S(2)}) copy-start(s16[16,4736]{1,0:T(8,128)(2,1)} %copy-done.18) | copy-start | bytes 454660
  123.2 36.8 %copy-start.21 = (s16[16,4736]{1,0:T(8,128)(2,1)S(1)}, s16[16,4736]{1,0:T(8,128)(2,1)}, u32[]{:S(2)}) copy-start(s16[16,4736]{1,0:T(8,128)(2,1)} %copy-done.20) | copy-start | bytes 454660
  163.7 6.8 %collective-permute-start.7 = (bf16[64,1152]{1,0:T(8,128)(2,1)S(1)}, bf16[64,1152]{1,0:T(8,128)(2,1)S(1)}, u32[]{:S(2)}, u32[]{:S(2)}) collective-permute-start(bf16[64,1152]{1,0:T(8,128)(2,1)S(1)} %get-tuple-element.64), channel_id=1, source_target_pairs={{0,7},{1,0},{2,1},{3,2},{4,3},{5,4},{6,5},{7,6},{8,15},{9,8},{10,9... | collective-permute-start | bytes 442376 | tf_op jit(solution)/shard_map/ppermute | solution.py:385
  165.2 7.1 %collective-permute-start.8 = (bf16[64,1152]{1,0:T(8,128)(2,1)S(1)}, bf16[64,1152]{1,0:T(8,128)(2,1)S(1)}, u32[]{:S(2)}, u32[]{:S(2)}) collective-permute-start(bf16[64,1152]{1,0:T(8,128)(2,1)S(1)} %get-tuple-element.65), channel_id=1, source_target_pairs={{0,1},{1,2},{2,3},{3,4},{4,5},{5,6},{6,7},{7,0},{8,9},{9,10},{10,1... | collective-permute-start | bytes 442376 | tf_op jit(solution)/shard_map/ppermute | solution.py:385
  177.2 11.4 %copy-start.29 = (bf16[64,1152]{1,0:T(8,128)(2,1)S(1)}, bf16[64,1152]{1,0:T(8,128)(2,1)}, u32[]{:S(2)}) copy-start(bf16[64,1152]{1,0:T(8,128)(2,1)} %copy-done.28) | copy-start | bytes 442372
  177.2 13.8 %copy-start.27 = (bf16[64,1152]{1,0:T(8,128)(2,1)S(1)}, bf16[64,1152]{1,0:T(8,128)(2,1)}, u32[]{:S(2)}) copy-start(bf16[64,1152]{1,0:T(8,128)(2,1)} %copy-done.26) | copy-start | bytes 442372
  177.2 34.2 %all-to-all-start.3 = ((bf16[32,16,1792]{2,1,0:T(8,128)(2,1)}), bf16[32,16,1792]{2,1,0:T(8,128)(2,1)S(1)}, u32[]{:S(2)}, u32[]{:S(2)}) async-start(bf16[32,16,1792]{2,1,0:T(8,128)(2,1)} %bitcast.19), calls=%async_computation.4 | async-start | bytes 3670016 | tf_op jit(solution)/shard_map/all_to_all | solution.py:380
  182.4 12.2 %collective-permute-start.9 = (bf16[64,1152]{1,0:T(8,128)(2,1)}, bf16[64,1152]{1,0:T(8,128)(2,1)S(1)}, u32[]{:S(2)}, u32[]{:S(2)}) collective-permute-start(bf16[64,1152]{1,0:T(8,128)(2,1)} %get-tuple-element.70), channel_id=1, source_target_pairs={{0,6},{1,7},{2,0},{3,1},{4,2},{5,3},{6,4},{7,5},{8,14},{9,15},{10,... | collective-permute-start | bytes 442376 | tf_op jit(solution)/shard_map/ppermute | solution.py:385
  183.3 17.4 %collective-permute-start.10 = (bf16[64,1152]{1,0:T(8,128)(2,1)}, bf16[64,1152]{1,0:T(8,128)(2,1)S(1)}, u32[]{:S(2)}, u32[]{:S(2)}) collective-permute-start(bf16[64,1152]{1,0:T(8,128)(2,1)} %get-tuple-element.71), channel_id=1, source_target_pairs={{0,5},{1,6},{2,7},{3,0},{4,1},{5,2},{6,3},{7,4},{8,13},{9,14},{10,... | collective-permute-start | bytes 442376 | tf_op jit(solution)/shard_map/ppermute | solution.py:385
  186.9 14.9 %collective-permute-start.11 = (bf16[64,1152]{1,0:T(8,128)(2,1)}, bf16[64,1152]{1,0:T(8,128)(2,1)S(1)}, u32[]{:S(2)}, u32[]{:S(2)}) collective-permute-start(bf16[64,1152]{1,0:T(8,128)(2,1)} %get-tuple-element.72), channel_id=1, source_target_pairs={{0,4},{1,5},{2,6},{3,7},{4,0},{5,1},{6,2},{7,3},{8,12},{9,13},{10,... | collective-permute-start | bytes 442376 | tf_op jit(solution)/shard_map/ppermute | solution.py:385
  188.6 22.7 %collective-permute-start.12 = (bf16[64,1152]{1,0:T(8,128)(2,1)S(1)}, bf16[64,1152]{1,0:T(8,128)(2,1)S(1)}, u32[]{:S(2)}, u32[]{:S(2)}) collective-permute-start(bf16[64,1152]{1,0:T(8,128)(2,1)S(1)} %copy-done.29), channel_id=1, source_target_pairs={{0,3},{1,4},{2,5},{3,6},{4,7},{5,0},{6,1},{7,2},{8,11},{9,12},{10,... | collective-permute-start | bytes 442376 | tf_op jit(solution)/shard_map/ppermute | solution.py:385
  191.0 20.4 %collective-permute-start.13 = (bf16[64,1152]{1,0:T(8,128)(2,1)S(1)}, bf16[64,1152]{1,0:T(8,128)(2,1)S(1)}, u32[]{:S(2)}, u32[]{:S(2)}) collective-permute-start(bf16[64,1152]{1,0:T(8,128)(2,1)S(1)} %copy-done.27), channel_id=1, source_target_pairs={{0,2},{1,3},{2,4},{3,5},{4,6},{5,7},{6,0},{7,1},{8,10},{9,11},{10,... | collective-permute-start | bytes 442376 | tf_op jit(solution)/shard_map/ppermute | solution.py:385
  (16 other events, 32.9 us)
Sparse Core Ops, SparseCore 0:
  65.0 50.0 reduce-scatter.1
  123.3 38.1 all-gather.1

commit v3 on v2

--- a/solution.py
+++ b/solution.py
@@ -16,7 +16,8 @@
 CAP = 4
 QUAD = 4
 SUB, LANES = 16, 128
-PART_A, COLS, COLS_B = 1152, 384, 128
+PART_A, COLS = 1152, 384
+ORDER = (3, 5, 2, 6, 4, 1, 7)
 SOON = (1, 7)
 TOP = 32000.0
 PER_OCTAVE = 64.0 / math.log(2.0)
@@ -340,9 +341,9 @@
     wb = width - wa
     n, rows = out_ref.shape[0], in_ref.shape[0]
     copies = []
-    for s in range(reps):
+    for x, s in zip(ins, (*ORDER, 0)):
         start = pl.multiple_of((r + s) % reps * width, LANES)
-        copies.append(pltpu.make_async_copy(ins[s], out_ref.at[:, pl.ds(start, wa)], sems.at[s]))
+        copies.append(pltpu.make_async_copy(x, out_ref.at[:, pl.ds(start, wa)], sems.at[s]))
         copies[-1].start()
     _, col, _ = positions(ids_ref[...], owned)
     at = iota((n, rows), 1)
@@ -400,8 +401,11 @@
         2 * touched * tokens * wa * reps,
         (tokens + touched) * 2 * wa * reps,
         scratch=[pltpu.VMEM((reps, tokens, wa), bf16), dma((reps,))],
+        room=56,
     )(me, slots, ids, token_grads)
-    group = [shift(x, s) for s, x in enumerate(sums)]
+    group = list(sums)
+    for s in ORDER:
+        group[s] = shift(sums[s], s)
 
     out_b = call(
         functools.partial(send_kernel, width, wa, owned),
@@ -418,6 +422,7 @@
             dma((reps,)),
             dma((3,)),
         ],
+        room=56,
     )(me, slots, ids, sums[0], token_grads)
     arrived_b = over_vocab(out_b)
     tile_b = pl.BlockSpec((rows, LANES), lambda i, me: (0, 2 * wb // LANES))
@@ -432,8 +437,11 @@
         8 * rows * QUAD * owned * wb,
         (rows + owned * reps) * 4 * wb,
         scratch=[pltpu.VMEM((2, QUAD * owned, wb), f32), dma((reps,))],
+        room=56,
     )(me, arrived_b)
-    group, (dense,) = together(group, [dense])
+    far, (dense,) = together([group[s] for s in ORDER], [dense])
+    for s, x in zip(ORDER, far):
+        group[s] = x
     gradient_b = lax.psum_scatter(dense, "rep", scatter_dimension=0, tiled=True)
 
     steps_a = wa // COLS
@@ -464,18 +472,19 @@
         (rows * 8 + owned * 24) * wa,
         scratch=[pltpu.VMEM((2, rows, owned), bf16), pltpu.VMEM((2, owned, rows), bf16)],
     )(me, arrived_a, arrived_a, table, first_moment, second_moment)
-    spec_b = pl.BlockSpec((owned, COLS_B), lambda i, me: (0, wa // COLS_B + i))
-    spec_h = pl.BlockSpec((owned, COLS_B), lambda i, me: (0, i))
+    spec_b = pl.BlockSpec((pl.Element(owned), pl.Element(wb)), lambda i, me: (0, wa))
+    spec_h = whole((owned, wb))
     *news, half_b = call(
         adam_b_kernel,
         "adam_b",
         [*(sds((owned, width), f32) for _ in range(3)), sds((owned, wb), bf16)],
-        (wb // COLS_B,),
+        (1,),
         [spec_h, spec_b, spec_b, spec_b, ANY, ANY, ANY],
         [spec_b, spec_b, spec_b, spec_h],
         20 * owned * wb,
         30 * owned * wb,
         aliases={5 + j: j for j in range(3)},
+        room=56,
     )(me, gradient_b, table, first_moment, second_moment, *news)
     rows_b = lax.all_gather(half_b, "rep", axis=0, tiled=True)
 
@@ -492,7 +501,9 @@
         2 * reps * touched * rows * wa,
         (rows * 2 + reps * touched) * 2 * wa,
     )(me, returned_a, *group)
-    home_a = [shift(x, (reps - s) % reps) for s, x in enumerate(mine_a)]
+    home_a = list(mine_a)
+    for s in ORDER:
+        home_a[s] = shift(mine_a[s], reps - s)
     first, (rows_b,) = together([home_a[s] for s in SOON], [rows_b])
     for s, x in zip(SOON, first):
         home_a[s] = x
@@ -519,7 +530,7 @@
         16 * touched * rows * wb,
         touched * full * 4,
         scratch=[pltpu.VMEM((reps, touched, wb), bf16), dma((reps,)), dma((reps,))],
-    )(me, ids, returned_b, *home_a)
+    )(me, ids, returned_b, *[home_a[s] for s in (*ORDER, 0)])
     return (*news, refreshed)
 
 

time: 223 us -> 216 us (0.969)
  local copies, waits for them, and re-layouts: 15.6 us -> 6.88 us
  waiting for transfers between devices: 33.8 us -> 29 us
  Pallas kernels: 33.6 us -> 38.1 us
  starting transfers between devices: 47.2 us -> 50.3 us
    unnamed x60 -> x62, local copies, waits for them, and re-layouts: 15.6 us -> 6.88 us
    ppermute x14, starting transfers between devices: 34.2 us -> 37.2 us  [shift(): return lax.ppermute(x, 'rep', [(i, (i + s) % reps) for i in range(reps)])]
    all_to_all x2, waiting for transfers between devices: 4.29 us -> 1.8 us  [over_vocab(): lax.all_to_all(x, 'vocab', split_axis=0, concat_axis=0, tiled=True)]
    ppermute x14, waiting for transfers between devices: 29.5 us -> 27.1 us  [shift(): return lax.ppermute(x, 'rep', [(i, (i + s) % reps) for i in range(reps)])]
  transfers between devices with their start and end apart: 18 -> 18, of which waited for: 9 -> 8; matrix products, arithmetic and copies ran while one was open for 0% -> 0% of each run, Pallas kernels for 8% -> 9%
where the time goes in v3:
time: 216 us; the launch traced here: 215 us
  blocking collectives  75.5 us (35%)
  starting transfers between devices  50.3 us (23%)
  Pallas kernels  38.1 us (18%)
  waiting for transfers between devices  29 us (13%)
  between operations  14.4 us (7%)
  local copies, waits for them, and re-layouts  6.88 us (3%)
    all_to_all x2, blocking collectives, over_vocab(): lax.all_to_all(x, 'vocab', split_axis=0, concat_axis=0, tiled=True)  75.5 us
    ppermute x14, starting transfers between devices, shift(): return lax.ppermute(x, 'rep', [(i, (i + s) % reps) for i in range(reps)])  37.2 us
    ppermute x14, waiting for transfers between devices, shift(): return lax.ppermute(x, 'rep', [(i, (i + s) % reps) for i in range(reps)])  27.1 us
    all_to_all x2, starting transfers between devices, over_vocab(): lax.all_to_all(x, 'vocab', split_axis=0, concat_axis=0, tiled=True)  12.9 us
    unnamed x62, local copies, waits for them, and re-layouts  6.88 us
    pallas_call x1, Pallas kernels, shards(): call(functools.partial(place_kernel, owned, wb), 'place', sds((reps * own...  6.15 us
    pallas_call x1, Pallas kernels, shards(): call(adam_a_kernel, 'adam_a', [*(sds((owned, width), f32) for _ in range(...  6.14 us
    pallas_call x1, Pallas kernels, shards(): call(functools.partial(sums_kernel, width), 'sums', [sds((SUB, wide), i16...  5.55 us
  transfers between devices with their start and end apart: 18, of which 8 were waited for; matrix products, arithmetic and copies ran while one was open for 0% of the time, Pallas kernels for 9%

profile of v3, /device:TPU:2, one launch (start us, length us, event | category | flops | bytes accessed | tf_op | source)
XLA Modules:
  0.0 214.8 jit_solution(17305683717942346399)
XLA Ops:
  7.8 5.5 %sums.1 = (s16[16,4736]{1,0:T(8,128)(2,1)}, s16[16,4736]{1,0:T(8,128)(2,1)}, s16[16,4736]{1,0:T(8,128)(2,1)}, s16[16,4736]{1,0:T(8,128)(2,1)}, s16[16,4736]{1,0:...) custom-call(s32[2]{0:T(128)} %pad_add_fusion.me_ref, s32[1,128]{1,0:T(1,128)} %bitcast.25, ...), custom_call_target="tpu_custom_call" | custom-call | flops 150994944 | bytes 3538944 | tf_op jit(solution)/shard_map/sums/pallas_call | solution.py:394
  13.3 5.5 %send.1 = s16[512,1920]{1,0:T(8,128)(2,1)} custom-call(s32[2]{0:T(128)} %pad_add_fusion.me_ref, s32[1,128]{1,0:T(1,128)} %bitcast.26, s32[1,64]{1,0:T(1,128)} %bitcast.22, s16[16,4736]{1,0:T(8,128)(2,1)} %get-tuple-element.46.after_ref.refs_0_, bf16[128,16384]{1,0:T(8,128)(2,1)} %grads_ref.3), custom_call_target="tpu_custom_call" | custom-call | flops 939524096 | bytes 3670016 | tf_op jit(solution)/shard_map/send/pallas_call | solution.py:410
  18.9 7.8 %all-to-all-start = ((s16[32,16,1920]{2,1,0:T(8,128)(2,1)}), s16[32,16,1920]{2,1,0:T(8,128)(2,1)S(1)}, u32[]{:S(2)}, u32[]{:S(2)}) async-start(s16[32,16,1920]{2,1,0:T(8,128)(2,1)} %bitcast.24), calls=%async_computation | async-start | bytes 3932160 | tf_op jit(solution)/shard_map/all_to_all | solution.py:381
  26.7 4.7 %collective-permute-start = (s16[16,4736]{1,0:T(8,128)(2,1)S(1)}, s16[16,4736]{1,0:T(8,128)(2,1)S(1)}, u32[]{:S(2)}, u32[]{:S(2)}) collective-permute-start(s16[16,4736]{1,0:T(8,128)(2,1)S(1)} %copy-done.30), channel_id=1, source_target_pairs={{0,3},{1,4},{2,5},{3,6},{4,7},{5,0},{6,1},{7,2},{8,11},{9,12},{10,... | collective-permute-start | bytes 454664 | tf_op jit(solution)/shard_map/ppermute | solution.py:386
  31.4 2.2 %collective-permute-start.1 = (s16[16,4736]{1,0:T(8,128)(2,1)S(1)}, s16[16,4736]{1,0:T(8,128)(2,1)S(1)}, u32[]{:S(2)}, u32[]{:S(2)}) collective-permute-start(s16[16,4736]{1,0:T(8,128)(2,1)S(1)} %copy-done.29), channel_id=1, source_target_pairs={{0,5},{1,6},{2,7},{3,0},{4,1},{5,2},{6,3},{7,4},{8,13},{9,14},{10,... | collective-permute-start | bytes 454664 | tf_op jit(solution)/shard_map/ppermute | solution.py:386
  35.1 3.0 %collective-permute-start.3 = (s16[16,4736]{1,0:T(8,128)(2,1)}, s16[16,4736]{1,0:T(8,128)(2,1)S(1)}, u32[]{:S(2)}, u32[]{:S(2)}) collective-permute-start(s16[16,4736]{1,0:T(8,128)(2,1)} %get-tuple-element.42), channel_id=1, source_target_pairs={{0,6},{1,7},{2,0},{3,1},{4,2},{5,3},{6,4},{7,5},{8,14},{9,15},{10,... | collective-permute-start | bytes 454664 | tf_op jit(solution)/shard_map/ppermute | solution.py:386
  38.1 5.0 %collective-permute-start.4 = (s16[16,4736]{1,0:T(8,128)(2,1)}, s16[16,4736]{1,0:T(8,128)(2,1)S(1)}, u32[]{:S(2)}, u32[]{:S(2)}) collective-permute-start(s16[16,4736]{1,0:T(8,128)(2,1)} %get-tuple-element.43), channel_id=1, source_target_pairs={{0,4},{1,5},{2,6},{3,7},{4,0},{5,1},{6,2},{7,3},{8,12},{9,13},{10,... | collective-permute-start | bytes 454664 | tf_op jit(solution)/shard_map/ppermute | solution.py:386
  43.2 4.5 %collective-permute-start.5 = (s16[16,4736]{1,0:T(8,128)(2,1)S(1)}, s16[16,4736]{1,0:T(8,128)(2,1)S(1)}, u32[]{:S(2)}, u32[]{:S(2)}) collective-permute-start(s16[16,4736]{1,0:T(8,128)(2,1)S(1)} %copy-done.28), channel_id=1, source_target_pairs={{0,1},{1,2},{2,3},{3,4},{4,5},{5,6},{6,7},{7,0},{8,9},{9,10},{10,1... | collective-permute-start | bytes 454664 | tf_op jit(solution)/shard_map/ppermute | solution.py:386
  47.7 3.6 %collective-permute-start.6 = (s16[16,4736]{1,0:T(8,128)(2,1)S(1)}, s16[16,4736]{1,0:T(8,128)(2,1)S(1)}, u32[]{:S(2)}, u32[]{:S(2)}) collective-permute-start(s16[16,4736]{1,0:T(8,128)(2,1)S(1)} %copy-done.27), channel_id=1, source_target_pairs={{0,7},{1,0},{2,1},{3,2},{4,3},{5,4},{6,5},{7,6},{8,15},{9,8},{10,9... | collective-permute-start | bytes 454664 | tf_op jit(solution)/shard_map/ppermute | solution.py:386
  51.3 1.8 all-to-all-done
  54.3 6.2 %place.1 = f32[1024,896]{1,0:T(8,128)} custom-call(s32[2]{0:T(128)} %pad_add_fusion.me_ref, s16[512,1920]{1,0:T(8,128)(2,1)} %bitcast.15), custom_call_target="tpu_custom_call" | custom-call | flops 1879048192 | bytes 5505024 | tf_op jit(solution)/shard_map/place/pallas_call | solution.py:430
  61.7 4.2 %route.1 = s16[512,2432]{1,0:T(8,128)(2,1)S(1)} custom-call(s32[2]{0:T(128)S(1)} %copy-done.22, s16[16,4736]{1,0:T(8,128)(2,1)S(1)} %copy-done.9, s16[16,4736]{1,0:T(8,128)(2,1)S(1)} %collective-permute-done.5.refs_1_, s16[16,4736]{1,0:T(8,128)(2,1)S(1)} %collective-permute-done.2.refs_2_, s16[16,4736]{1,0:T(8,128)(2,1)S(1)} %collective-permute-done.refs_3_, ...), custom_call_target="tpu_custom_call" | custom-call | flops 1207959552 | bytes 3538944 | tf_op jit(solution)/shard_map/route/pallas_call | solution.py:449
  66.7 39.0 %all_to_all.20 = s16[32,16,2432]{2,1,0:T(8,128)(2,1)S(1)} all-to-all(s16[32,16,2432]{2,1,0:T(8,128)(2,1)S(1)} %bitcast.19), channel_id=1, replica_groups=mesh['vocab'=32,'rep'=8] {'vocab'}, dimensions={0} | all-to-all | bytes 4980736 | tf_op jit(solution)/shard_map/all_to_all | solution.py:381
  105.7 6.1 %adam_a.1 = (f32[128,2048]{1,0:T(8,128)}, f32[128,2048]{1,0:T(8,128)}, f32[128,2048]{1,0:T(8,128)}, bf16[512,2304]{1,0:T(8,128)(2,1)S(1)}) custom-call(s32[2]{0:T(128)S(1)} %copy-done.22, s16[512,2432]{1,0:T(8,128)(2,1)S(1)} %bitcast.12, s16[512,2432]{1,0:T(8,128)(2,1)S(1)} %bitcast.13, f32[128,2048]{1,0:T(8,128)S(1)} %copy-done.3, ...), custom_call_target="tpu_custom_call" | custom-call | flops 905969664 | bytes 8257536 | tf_op jit(solution)/shard_map/adam_a/pallas_call | solution.py:464
  113.3 3.6 %adam_b.1 = (f32[128,2048]{1,0:T(8,128)}, f32[128,2048]{1,0:T(8,128)}, f32[128,2048]{1,0:T(8,128)}, bf16[128,896]{1,0:T(8,128)(2,1)}) custom-call(s32[2]{0:T(128)} %pad_add_fusion.me_ref, f32[128,896]{1,0:T(8,128)} %reduce-scatter.2.cloned.1.call-done.grad_ref, f32[128,2048]{1,0:T(8,128)} %refs_0_.3, ...), custom_call_target="tpu_custom_call", output_to_operand_aliasing={{0}: (5, {}), {1}: (6, {}), {2}: (7, {})} | custom-call | flops 2293760 | bytes 3440640 | tf_op jit(solution)/shard_map/adam_b/pallas_call | solution.py:477
  117.0 36.5 %all_to_all.21 = bf16[32,16,2304]{2,1,0:T(8,128)(2,1)S(1)} all-to-all(bf16[32,16,2304]{2,1,0:T(8,128)(2,1)S(1)} %bitcast.20), channel_id=1, replica_groups=mesh['vocab'=32,'rep'=8] {'vocab'}, dimensions={0} | all-to-all | bytes 4718592 | tf_op jit(solution)/shard_map/all_to_all | solution.py:381
  153.6 2.5 %unpad.1 = (bf16[64,1152]{1,0:T(8,128)(2,1)S(1)}, bf16[64,1152]{1,0:T(8,128)(2,1)S(1)}, bf16[64,1152]{1,0:T(8,128)(2,1)}, bf16[64,1152]{1,0:T(8,128)(2,1)}, bf16...) custom-call(s32[2]{0:T(128)S(1)} %copy-done.23, ...), custom_call_target="tpu_custom_call" | custom-call | flops 603979776 | bytes 3538944 | tf_op jit(solution)/shard_map/unpad/pallas_call | solution.py:493
  156.7 1.9 collective-permute-start.7
  158.7 4.2 %collective-permute-done.7.refs_5_ = bf16[64,1152]{1,0:T(8,128)(2,1)S(1)} collective-permute-done((bf16[64,1152]{1,0:T(8,128)(2,1)S(1)}, bf16[64,1152]{1,0:T(8,128)(2,1)S(1)}, u32[]{:S(2)}, u32[]{:S(2)}) %collective-permute-start.7) | collective-permute-done | bytes 147488 | tf_op jit(solution)/shard_map/ppermute | solution.py:386
  162.9 2.8 %collective-permute-done.8.refs_6_ = bf16[64,1152]{1,0:T(8,128)(2,1)S(1)} collective-permute-done((bf16[64,1152]{1,0:T(8,128)(2,1)S(1)}, bf16[64,1152]{1,0:T(8,128)(2,1)S(1)}, u32[]{:S(2)}, u32[]{:S(2)}) %collective-permute-start.8) | collective-permute-done | bytes 147488 | tf_op jit(solution)/shard_map/ppermute | solution.py:386
  165.7 1.5 copy-done.8
  167.2 2.2 %pick.1 = bf16[512,1792]{1,0:T(8,128)(2,1)S(1)} custom-call(s32[2]{0:T(128)S(1)} %copy-done.23, s16[512,1920]{1,0:T(8,128)(2,1)S(1)} %bitcast.16, bf16[1024,896]{1,0:T(8,128)(2,1)S(1)} %copy-done.8), custom_call_target="tpu_custom_call" | custom-call | flops 939524096 | bytes 3670016 | tf_op jit(solution)/shard_map/pick/pallas_call | solution.py:510
  170.6 5.1 %all-to-all-start.3 = ((bf16[32,16,1792]{2,1,0:T(8,128)(2,1)}), bf16[32,16,1792]{2,1,0:T(8,128)(2,1)S(1)}, u32[]{:S(2)}, u32[]{:S(2)}) async-start(bf16[32,16,1792]{2,1,0:T(8,128)(2,1)} %bitcast.18), calls=%async_computation.4 | async-start | bytes 3670016 | tf_op jit(solution)/shard_map/all_to_all | solution.py:381
  175.7 1.5 collective-permute-start.9
  177.2 2.4 %collective-permute-start.10 = (bf16[64,1152]{1,0:T(8,128)(2,1)}, bf16[64,1152]{1,0:T(8,128)(2,1)S(1)}, u32[]{:S(2)}, u32[]{:S(2)}) collective-permute-start(bf16[64,1152]{1,0:T(8,128)(2,1)} %get-tuple-element.67), channel_id=1, source_target_pairs={{0,3},{1,4},{2,5},{3,6},{4,7},{5,0},{6,1},{7,2},{8,11},{9,12},{10,... | collective-permute-start | bytes 442376 | tf_op jit(solution)/shard_map/ppermute | solution.py:386
  179.6 1.7 collective-permute-start.11
  182.6 3.8 %collective-permute-start.13 = (bf16[64,1152]{1,0:T(8,128)(2,1)S(1)}, bf16[64,1152]{1,0:T(8,128)(2,1)S(1)}, u32[]{:S(2)}, u32[]{:S(2)}) collective-permute-start(bf16[64,1152]{1,0:T(8,128)(2,1)S(1)} %copy-done.26), channel_id=1, source_target_pairs={{0,4},{1,5},{2,6},{3,7},{4,0},{5,1},{6,2},{7,3},{8,12},{9,13},{10,... | collective-permute-start | bytes 442376 | tf_op jit(solution)/shard_map/ppermute | solution.py:386
  186.4 3.5 %collective-permute-done.9.refs_0_ = bf16[64,1152]{1,0:T(8,128)(2,1)S(1)} collective-permute-done((bf16[64,1152]{1,0:T(8,128)(2,1)}, bf16[64,1152]{1,0:T(8,128)(2,1)S(1)}, u32[]{:S(2)}, u32[]{:S(2)}) %collective-permute-start.9) | collective-permute-done | bytes 147488 | tf_op jit(solution)/shard_map/ppermute | solution.py:386
  189.8 6.6 %collective-permute-done.10.refs_1_ = bf16[64,1152]{1,0:T(8,128)(2,1)S(1)} collective-permute-done((bf16[64,1152]{1,0:T(8,128)(2,1)}, bf16[64,1152]{1,0:T(8,128)(2,1)S(1)}, u32[]{:S(2)}, u32[]{:S(2)}) %collective-permute-start.10) | collective-permute-done | bytes 147488 | tf_op jit(solution)/shard_map/ppermute | solution.py:386
  196.4 2.2 %collective-permute-done.11.refs_2_ = bf16[64,1152]{1,0:T(8,128)(2,1)S(1)} collective-permute-done((bf16[64,1152]{1,0:T(8,128)(2,1)}, bf16[64,1152]{1,0:T(8,128)(2,1)S(1)}, u32[]{:S(2)}, u32[]{:S(2)}) %collective-permute-start.11) | collective-permute-done | bytes 147488 | tf_op jit(solution)/shard_map/ppermute | solution.py:386
  198.7 7.0 %collective-permute-done.13.refs_4_ = bf16[64,1152]{1,0:T(8,128)(2,1)S(1)} collective-permute-done((bf16[64,1152]{1,0:T(8,128)(2,1)S(1)}, bf16[64,1152]{1,0:T(8,128)(2,1)S(1)}, u32[]{:S(2)}, u32[]{:S(2)}) %collective-permute-start.13) | collective-permute-done | bytes 147488 | tf_op jit(solution)/shard_map/ppermute | solution.py:386
  205.7 2.3 %final.1 = bf16[64,16384]{1,0:T(8,128)(2,1)} custom-call(s32[2]{0:T(128)S(1)} %copy-done.23, s32[1,64]{1,0:T(1,128)S(1)} %bitcast.23, bf16[512,1792]{1,0:T(8,128)(2,1)S(1)} %bitcast.17, bf16[64,1152]{1,0:T(8,128)(2,1)S(1)} %collective-permute-done.9.refs_0_, bf16[64,1152]{1,0:T(8,128)(2,1)S(1)} %collective-permute-done.10.refs_1_, ...), custom_call_target="tpu_custom_call" | custom-call | flops 469762048 | bytes 4194304 | tf_op jit(solution)/shard_map/final/pallas_call | solution.py:523
  (80 shorter events, 10.0 us)
Async XLA Ops:
  18.9 12.6 %copy-start.29 = (s16[16,4736]{1,0:T(8,128)(2,1)S(1)}, s16[16,4736]{1,0:T(8,128)(2,1)}, u32[]{:S(2)}) copy-start(s16[16,4736]{1,0:T(8,128)(2,1)} %get-tuple-element.40) | copy-start | bytes 454660
  18.9 24.3 %copy-start.28 = (s16[16,4736]{1,0:T(8,128)(2,1)S(1)}, s16[16,4736]{1,0:T(8,128)(2,1)}, u32[]{:S(2)}) copy-start(s16[16,4736]{1,0:T(8,128)(2,1)} %get-tuple-element.44) | copy-start | bytes 454660
  18.9 28.8 %copy-start.27 = (s16[16,4736]{1,0:T(8,128)(2,1)S(1)}, s16[16,4736]{1,0:T(8,128)(2,1)}, u32[]{:S(2)}) copy-start(s16[16,4736]{1,0:T(8,128)(2,1)} %get-tuple-element.45) | copy-start | bytes 454660
  18.9 34.2 %all-to-all-start = ((s16[32,16,1920]{2,1,0:T(8,128)(2,1)}), s16[32,16,1920]{2,1,0:T(8,128)(2,1)S(1)}, u32[]{:S(2)}, u32[]{:S(2)}) async-start(s16[32,16,1920]{2,1,0:T(8,128)(2,1)} %bitcast.24), calls=%async_computation | async-start | bytes 3932160 | tf_op jit(solution)/shard_map/all_to_all | solution.py:381
  26.7 86.6 %reduce-scatter.2.cloned.1.call-start = ((), (), s32[]{:S(2)}) async-start(), calls=%async_computation.5 | async-start | bytes 4128768 | tf_op jit(solution)/shard_map/reduce_scatter | solution.py:445
  26.7 16.4 %collective-permute-start = (s16[16,4736]{1,0:T(8,128)(2,1)S(1)}, s16[16,4736]{1,0:T(8,128)(2,1)S(1)}, u32[]{:S(2)}, u32[]{:S(2)}) collective-permute-start(s16[16,4736]{1,0:T(8,128)(2,1)S(1)} %copy-done.30), channel_id=1, source_target_pairs={{0,3},{1,4},{2,5},{3,6},{4,7},{5,0},{6,1},{7,2},{8,11},{9,12},{10,... | collective-permute-start | bytes 454664 | tf_op jit(solution)/shard_map/ppermute | solution.py:386
  31.4 16.2 %collective-permute-start.1 = (s16[16,4736]{1,0:T(8,128)(2,1)S(1)}, s16[16,4736]{1,0:T(8,128)(2,1)S(1)}, u32[]{:S(2)}, u32[]{:S(2)}) collective-permute-start(s16[16,4736]{1,0:T(8,128)(2,1)S(1)} %copy-done.29), channel_id=1, source_target_pairs={{0,5},{1,6},{2,7},{3,0},{4,1},{5,2},{6,3},{7,4},{8,13},{9,14},{10,... | collective-permute-start | bytes 454664 | tf_op jit(solution)/shard_map/ppermute | solution.py:386
  33.6 26.9 %collective-permute-start.2 = (s16[16,4736]{1,0:T(8,128)(2,1)}, s16[16,4736]{1,0:T(8,128)(2,1)S(1)}, u32[]{:S(2)}, u32[]{:S(2)}) collective-permute-start(s16[16,4736]{1,0:T(8,128)(2,1)} %get-tuple-element.41), channel_id=1, source_target_pairs={{0,2},{1,3},{2,4},{3,5},{4,6},{5,7},{6,0},{7,1},{8,10},{9,11},{10,... | collective-permute-start | bytes 454664 | tf_op jit(solution)/shard_map/ppermute | solution.py:386
  35.1 25.4 %collective-permute-start.3 = (s16[16,4736]{1,0:T(8,128)(2,1)}, s16[16,4736]{1,0:T(8,128)(2,1)S(1)}, u32[]{:S(2)}, u32[]{:S(2)}) collective-permute-start(s16[16,4736]{1,0:T(8,128)(2,1)} %get-tuple-element.42), channel_id=1, source_target_pairs={{0,6},{1,7},{2,0},{3,1},{4,2},{5,3},{6,4},{7,5},{8,14},{9,15},{10,... | collective-permute-start | bytes 454664 | tf_op jit(solution)/shard_map/ppermute | solution.py:386
  38.1 22.4 %collective-permute-start.4 = (s16[16,4736]{1,0:T(8,128)(2,1)}, s16[16,4736]{1,0:T(8,128)(2,1)S(1)}, u32[]{:S(2)}, u32[]{:S(2)}) collective-permute-start(s16[16,4736]{1,0:T(8,128)(2,1)} %get-tuple-element.43), channel_id=1, source_target_pairs={{0,4},{1,5},{2,6},{3,7},{4,0},{5,1},{6,2},{7,3},{8,12},{9,13},{10,... | collective-permute-start | bytes 454664 | tf_op jit(solution)/shard_map/ppermute | solution.py:386
  43.2 17.4 %collective-permute-start.5 = (s16[16,4736]{1,0:T(8,128)(2,1)S(1)}, s16[16,4736]{1,0:T(8,128)(2,1)S(1)}, u32[]{:S(2)}, u32[]{:S(2)}) collective-permute-start(s16[16,4736]{1,0:T(8,128)(2,1)S(1)} %copy-done.28), channel_id=1, source_target_pairs={{0,1},{1,2},{2,3},{3,4},{4,5},{5,6},{6,7},{7,0},{8,9},{9,10},{10,1... | collective-permute-start | bytes 454664 | tf_op jit(solution)/shard_map/ppermute | solution.py:386
  47.7 13.8 %collective-permute-start.6 = (s16[16,4736]{1,0:T(8,128)(2,1)S(1)}, s16[16,4736]{1,0:T(8,128)(2,1)S(1)}, u32[]{:S(2)}, u32[]{:S(2)}) collective-permute-start(s16[16,4736]{1,0:T(8,128)(2,1)S(1)} %copy-done.27), channel_id=1, source_target_pairs={{0,7},{1,0},{2,1},{3,2},{4,3},{5,4},{6,5},{7,6},{8,15},{9,8},{10,9... | collective-permute-start | bytes 454664 | tf_op jit(solution)/shard_map/ppermute | solution.py:386
  61.5 104.2 %all-gather.2.cloned.1.call-start = ((), (), s32[]{:S(2)}) async-start(), calls=%async_computation.6 | async-start | bytes 2064384 | tf_op jit(solution)/shard_map/all_gather | solution.py:489
  66.7 39.0 %copy-start.3 = (f32[128,2048]{1,0:T(8,128)S(1)}, f32[128,2048]{1,0:T(8,128)}, u32[]{:S(2)}) copy-start(f32[128,2048]{1,0:T(8,128)} %refs_0_.3) | copy-start | bytes 3145732
  66.7 39.0 %copy-start.4 = (f32[128,2048]{1,0:T(8,128)S(1)}, f32[128,2048]{1,0:T(8,128)}, u32[]{:S(2)}) copy-start(f32[128,2048]{1,0:T(8,128)} %refs_1_.3) | copy-start | bytes 3145732
  66.7 39.0 %copy-start.5 = (f32[128,2048]{1,0:T(8,128)S(1)}, f32[128,2048]{1,0:T(8,128)}, u32[]{:S(2)}) copy-start(f32[128,2048]{1,0:T(8,128)} %refs_2_.3) | copy-start | bytes 3145732
  116.9 36.6 %copy-start.11 = (s16[16,4736]{1,0:T(8,128)(2,1)S(1)}, s16[16,4736]{1,0:T(8,128)(2,1)}, u32[]{:S(2)}) copy-start(s16[16,4736]{1,0:T(8,128)(2,1)} %copy-done.10) | copy-start | bytes 454660
  116.9 36.6 %copy-start.13 = (s16[16,4736]{1,0:T(8,128)(2,1)S(1)}, s16[16,4736]{1,0:T(8,128)(2,1)}, u32[]{:S(2)}) copy-start(s16[16,4736]{1,0:T(8,128)(2,1)} %copy-done.12) | copy-start | bytes 454660
  116.9 36.6 %copy-start.15 = (s16[16,4736]{1,0:T(8,128)(2,1)S(1)}, s16[16,4736]{1,0:T(8,128)(2,1)}, u32[]{:S(2)}) copy-start(s16[16,4736]{1,0:T(8,128)(2,1)} %copy-done.14) | copy-start | bytes 454660
  116.9 36.6 %copy-start.17 = (s16[16,4736]{1,0:T(8,128)(2,1)S(1)}, s16[16,4736]{1,0:T(8,128)(2,1)}, u32[]{:S(2)}) copy-start(s16[16,4736]{1,0:T(8,128)(2,1)} %copy-done.16) | copy-start | bytes 454660
  116.9 36.6 %copy-start.19 = (s16[16,4736]{1,0:T(8,128)(2,1)S(1)}, s16[16,4736]{1,0:T(8,128)(2,1)}, u32[]{:S(2)}) copy-start(s16[16,4736]{1,0:T(8,128)(2,1)} %copy-done.18) | copy-start | bytes 454660
  116.9 36.6 %copy-start.21 = (s16[16,4736]{1,0:T(8,128)(2,1)S(1)}, s16[16,4736]{1,0:T(8,128)(2,1)}, u32[]{:S(2)}) copy-start(s16[16,4736]{1,0:T(8,128)(2,1)} %copy-done.20) | copy-start | bytes 454660
  117.0 36.6 %copy-start.23 = (s32[2]{0:T(128)S(1)}, s32[2]{0:T(128)}, u32[]{:S(2)}) copy-start(s32[2]{0:T(128)} %pad_add_fusion.me_ref) | copy-start | bytes 28
  156.7 6.2 %collective-permute-start.7 = (bf16[64,1152]{1,0:T(8,128)(2,1)S(1)}, bf16[64,1152]{1,0:T(8,128)(2,1)S(1)}, u32[]{:S(2)}, u32[]{:S(2)}) collective-permute-start(bf16[64,1152]{1,0:T(8,128)(2,1)S(1)} %get-tuple-element.62), channel_id=1, source_target_pairs={{0,7},{1,0},{2,1},{3,2},{4,3},{5,4},{6,5},{7,6},{8,15},{9,8},{10,9... | collective-permute-start | bytes 442376 | tf_op jit(solution)/shard_map/ppermute | solution.py:386
  158.5 7.2 %collective-permute-start.8 = (bf16[64,1152]{1,0:T(8,128)(2,1)S(1)}, bf16[64,1152]{1,0:T(8,128)(2,1)S(1)}, u32[]{:S(2)}, u32[]{:S(2)}) collective-permute-start(bf16[64,1152]{1,0:T(8,128)(2,1)S(1)} %get-tuple-element.63), channel_id=1, source_target_pairs={{0,1},{1,2},{2,3},{3,4},{4,5},{5,6},{6,7},{7,0},{8,9},{9,10},{10,1... | collective-permute-start | bytes 442376 | tf_op jit(solution)/shard_map/ppermute | solution.py:386
  170.6 35.0 %copy-start.24 = (s32[64]{0:T(128)S(1)}, s32[64]{0:T(128)}, u32[]{:S(2)}) copy-start(s32[64]{0:T(128)} %param.8) | copy-start | bytes 772
  170.6 35.0 %all-to-all-start.3 = ((bf16[32,16,1792]{2,1,0:T(8,128)(2,1)}), bf16[32,16,1792]{2,1,0:T(8,128)(2,1)S(1)}, u32[]{:S(2)}, u32[]{:S(2)}) async-start(bf16[32,16,1792]{2,1,0:T(8,128)(2,1)} %bitcast.18), calls=%async_computation.4 | async-start | bytes 3670016 | tf_op jit(solution)/shard_map/all_to_all | solution.py:381
  175.7 14.1 %collective-permute-start.9 = (bf16[64,1152]{1,0:T(8,128)(2,1)}, bf16[64,1152]{1,0:T(8,128)(2,1)S(1)}, u32[]{:S(2)}, u32[]{:S(2)}) collective-permute-start(bf16[64,1152]{1,0:T(8,128)(2,1)} %get-tuple-element.66), channel_id=1, source_target_pairs={{0,5},{1,6},{2,7},{3,0},{4,1},{5,2},{6,3},{7,4},{8,13},{9,14},{10,... | collective-permute-start | bytes 442376 | tf_op jit(solution)/shard_map/ppermute | solution.py:386
  177.2 19.2 %collective-permute-start.10 = (bf16[64,1152]{1,0:T(8,128)(2,1)}, bf16[64,1152]{1,0:T(8,128)(2,1)S(1)}, u32[]{:S(2)}, u32[]{:S(2)}) collective-permute-start(bf16[64,1152]{1,0:T(8,128)(2,1)} %get-tuple-element.67), channel_id=1, source_target_pairs={{0,3},{1,4},{2,5},{3,6},{4,7},{5,0},{6,1},{7,2},{8,11},{9,12},{10,... | collective-permute-start | bytes 442376 | tf_op jit(solution)/shard_map/ppermute | solution.py:386
  179.6 19.0 %collective-permute-start.11 = (bf16[64,1152]{1,0:T(8,128)(2,1)}, bf16[64,1152]{1,0:T(8,128)(2,1)S(1)}, u32[]{:S(2)}, u32[]{:S(2)}) collective-permute-start(bf16[64,1152]{1,0:T(8,128)(2,1)} %get-tuple-element.68), channel_id=1, source_target_pairs={{0,6},{1,7},{2,0},{3,1},{4,2},{5,3},{6,4},{7,5},{8,14},{9,15},{10,... | collective-permute-start | bytes 442376 | tf_op jit(solution)/shard_map/ppermute | solution.py:386
  181.3 17.3 %collective-permute-start.12 = (bf16[64,1152]{1,0:T(8,128)(2,1)}, bf16[64,1152]{1,0:T(8,128)(2,1)S(1)}, u32[]{:S(2)}, u32[]{:S(2)}) collective-permute-start(bf16[64,1152]{1,0:T(8,128)(2,1)} %get-tuple-element.69), channel_id=1, source_target_pairs={{0,2},{1,3},{2,4},{3,5},{4,6},{5,7},{6,0},{7,1},{8,10},{9,11},{10,... | collective-permute-start | bytes 442376 | tf_op jit(solution)/shard_map/ppermute | solution.py:386
  182.6 23.1 %collective-permute-start.13 = (bf16[64,1152]{1,0:T(8,128)(2,1)S(1)}, bf16[64,1152]{1,0:T(8,128)(2,1)S(1)}, u32[]{:S(2)}, u32[]{:S(2)}) collective-permute-start(bf16[64,1152]{1,0:T(8,128)(2,1)S(1)} %copy-done.26), channel_id=1, source_target_pairs={{0,4},{1,5},{2,6},{3,7},{4,0},{5,1},{6,2},{7,3},{8,12},{9,13},{10,... | collective-permute-start | bytes 442376 | tf_op jit(solution)/shard_map/ppermute | solution.py:386
  (17 other events, 71.0 us)
Sparse Core Ops, SparseCore 0:
  61.6 50.6 reduce-scatter.1
  117.0 38.1 all-gather.1

commit v4 on v3

--- a/solution.py
+++ b/solution.py
@@ -17,7 +17,7 @@
 QUAD = 4
 SUB, LANES = 16, 128
 PART_A, COLS = 1152, 384
-ORDER = (3, 5, 2, 6, 4, 1, 7)
+ORDER = (4, 3, 5, 2, 6, 1, 7)
 SOON = (1, 7)
 TOP = 32000.0
 PER_OCTAVE = 64.0 / math.log(2.0)

time: 216 us -> 213 us (0.986)
  starting transfers between devices: 50.3 us -> 42.9 us
  waiting for transfers between devices: 29 us -> 34.2 us
    ppermute x14, starting transfers between devices: 37.2 us -> 29.8 us  [shift(): return lax.ppermute(x, 'rep', [(i, (i + s) % reps) for i in range(reps)])]
    ppermute x14, waiting for transfers between devices: 27.1 us -> 34.2 us  [shift(): return lax.ppermute(x, 'rep', [(i, (i + s) % reps) for i in range(reps)])]
  transfers between devices with their start and end apart: 18 -> 18, of which waited for: 8 -> 9; matrix products, arithmetic and copies ran while one was open for 0% -> 0% of each run, Pallas kernels for 9% -> 9%
where the time goes in v4:
time: 213 us; the launch traced here: 212 us
  blocking collectives  74.2 us (35%)
  starting transfers between devices  42.9 us (20%)
  Pallas kernels  38.1 us (18%)
  waiting for transfers between devices  34.2 us (16%)
  between operations  14.4 us (7%)
  local copies, waits for them, and re-layouts  7.36 us (3%)
    all_to_all x2, blocking collectives, over_vocab(): lax.all_to_all(x, 'vocab', split_axis=0, concat_axis=0, tiled=True)  74.2 us
    ppermute x14, waiting for transfers between devices, shift(): return lax.ppermute(x, 'rep', [(i, (i + s) % reps) for i in range(reps)])  34.2 us
    ppermute x14, starting transfers between devices, shift(): return lax.ppermute(x, 'rep', [(i, (i + s) % reps) for i in range(reps)])  29.8 us
    all_to_all x2, starting transfers between devices, over_vocab(): lax.all_to_all(x, 'vocab', split_axis=0, concat_axis=0, tiled=True)  12.9 us
    unnamed x62, local copies, waits for them, and re-layouts  7.36 us
    pallas_call x1, Pallas kernels, shards(): call(functools.partial(place_kernel, owned, wb), 'place', sds((reps * own...  6.15 us
    pallas_call x1, Pallas kernels, shards(): call(adam_a_kernel, 'adam_a', [*(sds((owned, width), f32) for _ in range(...  6.15 us
    pallas_call x1, Pallas kernels, shards(): call(functools.partial(sums_kernel, width), 'sums', [sds((SUB, wide), i16...  5.55 us
  transfers between devices with their start and end apart: 18, of which 9 were waited for; matrix products, arithmetic and copies ran while one was open for 0% of the time, Pallas kernels for 9%

profile of v4, /device:TPU:2, one launch (start us, length us, event | category | flops | bytes accessed | tf_op | source)
XLA Modules:
  0.0 211.7 jit_solution(11589000224817507201)
XLA Ops:
  7.8 5.5 %sums.1 = (s16[16,4736]{1,0:T(8,128)(2,1)}, s16[16,4736]{1,0:T(8,128)(2,1)}, s16[16,4736]{1,0:T(8,128)(2,1)}, s16[16,4736]{1,0:T(8,128)(2,1)}, s16[16,4736]{1,0:...) custom-call(s32[2]{0:T(128)} %pad_add_fusion.me_ref, s32[1,128]{1,0:T(1,128)} %bitcast.25, ...), custom_call_target="tpu_custom_call" | custom-call | flops 150994944 | bytes 3538944 | tf_op jit(solution)/shard_map/sums/pallas_call | solution.py:394
  13.3 5.5 %send.1 = s16[512,1920]{1,0:T(8,128)(2,1)} custom-call(s32[2]{0:T(128)} %pad_add_fusion.me_ref, s32[1,128]{1,0:T(1,128)} %bitcast.26, s32[1,64]{1,0:T(1,128)} %bitcast.22, s16[16,4736]{1,0:T(8,128)(2,1)} %get-tuple-element.46.after_ref.refs_0_, bf16[128,16384]{1,0:T(8,128)(2,1)} %grads_ref.3), custom_call_target="tpu_custom_call" | custom-call | flops 939524096 | bytes 3670016 | tf_op jit(solution)/shard_map/send/pallas_call | solution.py:410
  18.9 7.8 %all-to-all-start = ((s16[32,16,1920]{2,1,0:T(8,128)(2,1)}), s16[32,16,1920]{2,1,0:T(8,128)(2,1)S(1)}, u32[]{:S(2)}, u32[]{:S(2)}) async-start(s16[32,16,1920]{2,1,0:T(8,128)(2,1)} %bitcast.24), calls=%async_computation | async-start | bytes 3932160 | tf_op jit(solution)/shard_map/all_to_all | solution.py:381
  26.7 7.3 %collective-permute-start = (s16[16,4736]{1,0:T(8,128)(2,1)S(1)}, s16[16,4736]{1,0:T(8,128)(2,1)S(1)}, u32[]{:S(2)}, u32[]{:S(2)}) collective-permute-start(s16[16,4736]{1,0:T(8,128)(2,1)S(1)} %copy-done.30), channel_id=1, source_target_pairs={{0,4},{1,5},{2,6},{3,7},{4,0},{5,1},{6,2},{7,3},{8,12},{9,13},{10,... | collective-permute-start | bytes 454664 | tf_op jit(solution)/shard_map/ppermute | solution.py:386
  34.0 1.9 collective-permute-start.1
  35.9 3.1 %collective-permute-start.2 = (s16[16,4736]{1,0:T(8,128)(2,1)}, s16[16,4736]{1,0:T(8,128)(2,1)S(1)}, u32[]{:S(2)}, u32[]{:S(2)}) collective-permute-start(s16[16,4736]{1,0:T(8,128)(2,1)} %get-tuple-element.41), channel_id=1, source_target_pairs={{0,5},{1,6},{2,7},{3,0},{4,1},{5,2},{6,3},{7,4},{8,13},{9,14},{10,... | collective-permute-start | bytes 454664 | tf_op jit(solution)/shard_map/ppermute | solution.py:386
  39.0 1.5 collective-permute-start.3
  40.5 2.7 %collective-permute-start.4 = (s16[16,4736]{1,0:T(8,128)(2,1)}, s16[16,4736]{1,0:T(8,128)(2,1)S(1)}, u32[]{:S(2)}, u32[]{:S(2)}) collective-permute-start(s16[16,4736]{1,0:T(8,128)(2,1)} %get-tuple-element.43), channel_id=1, source_target_pairs={{0,6},{1,7},{2,0},{3,1},{4,2},{5,3},{6,4},{7,5},{8,14},{9,15},{10,... | collective-permute-start | bytes 454664 | tf_op jit(solution)/shard_map/ppermute | solution.py:386
  43.2 2.0 collective-permute-done.refs_4_
  45.2 8.9 %collective-permute-done.1.refs_3_ = s16[16,4736]{1,0:T(8,128)(2,1)S(1)} collective-permute-done((s16[16,4736]{1,0:T(8,128)(2,1)S(1)}, s16[16,4736]{1,0:T(8,128)(2,1)S(1)}, u32[]{:S(2)}, u32[]{:S(2)}) %collective-permute-start.1) | collective-permute-done | bytes 151584 | tf_op jit(solution)/shard_map/ppermute | solution.py:386
  54.1 1.3 copy-done
  55.4 6.2 %place.1 = f32[1024,896]{1,0:T(8,128)} custom-call(s32[2]{0:T(128)} %pad_add_fusion.me_ref, s16[512,1920]{1,0:T(8,128)(2,1)} %bitcast.15), custom_call_target="tpu_custom_call" | custom-call | flops 1879048192 | bytes 5505024 | tf_op jit(solution)/shard_map/place/pallas_call | solution.py:430
  62.5 4.2 %route.1 = s16[512,2432]{1,0:T(8,128)(2,1)S(1)} custom-call(s32[2]{0:T(128)S(1)} %copy-done.22, s16[16,4736]{1,0:T(8,128)(2,1)S(1)} %copy-done.9, s16[16,4736]{1,0:T(8,128)(2,1)S(1)} %collective-permute-done.5.refs_1_, s16[16,4736]{1,0:T(8,128)(2,1)S(1)} %collective-permute-done.3.refs_2_, s16[16,4736]{1,0:T(8,128)(2,1)S(1)} %collective-permute-done.1.refs_3_, ...), custom_call_target="tpu_custom_call" | custom-call | flops 1207959552 | bytes 3538944 | tf_op jit(solution)/shard_map/route/pallas_call | solution.py:449
  67.5 39.0 %all_to_all.20 = s16[32,16,2432]{2,1,0:T(8,128)(2,1)S(1)} all-to-all(s16[32,16,2432]{2,1,0:T(8,128)(2,1)S(1)} %bitcast.19), channel_id=1, replica_groups=mesh['vocab'=32,'rep'=8] {'vocab'}, dimensions={0} | all-to-all | bytes 4980736 | tf_op jit(solution)/shard_map/all_to_all | solution.py:381
  106.5 6.1 %adam_a.1 = (f32[128,2048]{1,0:T(8,128)}, f32[128,2048]{1,0:T(8,128)}, f32[128,2048]{1,0:T(8,128)}, bf16[512,2304]{1,0:T(8,128)(2,1)S(1)}) custom-call(s32[2]{0:T(128)S(1)} %copy-done.22, s16[512,2432]{1,0:T(8,128)(2,1)S(1)} %bitcast.12, s16[512,2432]{1,0:T(8,128)(2,1)S(1)} %bitcast.13, f32[128,2048]{1,0:T(8,128)S(1)} %copy-done.3, ...), custom_call_target="tpu_custom_call" | custom-call | flops 905969664 | bytes 8257536 | tf_op jit(solution)/shard_map/adam_a/pallas_call | solution.py:464
  112.6 1.5 copy-done.6
  114.1 3.6 %adam_b.1 = (f32[128,2048]{1,0:T(8,128)}, f32[128,2048]{1,0:T(8,128)}, f32[128,2048]{1,0:T(8,128)}, bf16[128,896]{1,0:T(8,128)(2,1)}) custom-call(s32[2]{0:T(128)} %pad_add_fusion.me_ref, f32[128,896]{1,0:T(8,128)} %reduce-scatter.2.cloned.1.call-done.grad_ref, f32[128,2048]{1,0:T(8,128)} %refs_0_.3, ...), custom_call_target="tpu_custom_call", output_to_operand_aliasing={{0}: (5, {}), {1}: (6, {}), {2}: (7, {})} | custom-call | flops 2293760 | bytes 3440640 | tf_op jit(solution)/shard_map/adam_b/pallas_call | solution.py:477
  117.8 35.2 %all_to_all.21 = bf16[32,16,2304]{2,1,0:T(8,128)(2,1)S(1)} all-to-all(bf16[32,16,2304]{2,1,0:T(8,128)(2,1)S(1)} %bitcast.20), channel_id=1, replica_groups=mesh['vocab'=32,'rep'=8] {'vocab'}, dimensions={0} | all-to-all | bytes 4718592 | tf_op jit(solution)/shard_map/all_to_all | solution.py:381
  153.0 2.5 %unpad.1 = (bf16[64,1152]{1,0:T(8,128)(2,1)S(1)}, bf16[64,1152]{1,0:T(8,128)(2,1)S(1)}, bf16[64,1152]{1,0:T(8,128)(2,1)}, bf16[64,1152]{1,0:T(8,128)(2,1)}, bf16...) custom-call(s32[2]{0:T(128)S(1)} %copy-done.23, ...), custom_call_target="tpu_custom_call" | custom-call | flops 603979776 | bytes 3538944 | tf_op jit(solution)/shard_map/unpad/pallas_call | solution.py:493
  156.1 2.6 %collective-permute-start.7 = (bf16[64,1152]{1,0:T(8,128)(2,1)S(1)}, bf16[64,1152]{1,0:T(8,128)(2,1)S(1)}, u32[]{:S(2)}, u32[]{:S(2)}) collective-permute-start(bf16[64,1152]{1,0:T(8,128)(2,1)S(1)} %get-tuple-element.62), channel_id=1, source_target_pairs={{0,7},{1,0},{2,1},{3,2},{4,3},{5,4},{6,5},{7,6},{8,15},{9,8},{10,9... | collective-permute-start | bytes 442376 | tf_op jit(solution)/shard_map/ppermute | solution.py:386
  158.7 3.7 %collective-permute-done.7.refs_5_ = bf16[64,1152]{1,0:T(8,128)(2,1)S(1)} collective-permute-done((bf16[64,1152]{1,0:T(8,128)(2,1)S(1)}, bf16[64,1152]{1,0:T(8,128)(2,1)S(1)}, u32[]{:S(2)}, u32[]{:S(2)}) %collective-permute-start.7) | collective-permute-done | bytes 147488 | tf_op jit(solution)/shard_map/ppermute | solution.py:386
  162.4 3.4 %collective-permute-done.8.refs_6_ = bf16[64,1152]{1,0:T(8,128)(2,1)S(1)} collective-permute-done((bf16[64,1152]{1,0:T(8,128)(2,1)S(1)}, bf16[64,1152]{1,0:T(8,128)(2,1)S(1)}, u32[]{:S(2)}, u32[]{:S(2)}) %collective-permute-start.8) | collective-permute-done | bytes 147488 | tf_op jit(solution)/shard_map/ppermute | solution.py:386
  165.8 1.5 copy-done.8
  167.3 2.2 %pick.1 = bf16[512,1792]{1,0:T(8,128)(2,1)S(1)} custom-call(s32[2]{0:T(128)S(1)} %copy-done.23, s16[512,1920]{1,0:T(8,128)(2,1)S(1)} %bitcast.16, bf16[1024,896]{1,0:T(8,128)(2,1)S(1)} %copy-done.8), custom_call_target="tpu_custom_call" | custom-call | flops 939524096 | bytes 3670016 | tf_op jit(solution)/shard_map/pick/pallas_call | solution.py:510
  170.8 5.1 %all-to-all-start.3 = ((bf16[32,16,1792]{2,1,0:T(8,128)(2,1)}), bf16[32,16,1792]{2,1,0:T(8,128)(2,1)S(1)}, u32[]{:S(2)}, u32[]{:S(2)}) async-start(bf16[32,16,1792]{2,1,0:T(8,128)(2,1)} %bitcast.18), calls=%async_computation.4 | async-start | bytes 3670016 | tf_op jit(solution)/shard_map/all_to_all | solution.py:381
  175.9 4.0 %collective-permute-start.9 = (bf16[64,1152]{1,0:T(8,128)(2,1)}, bf16[64,1152]{1,0:T(8,128)(2,1)S(1)}, u32[]{:S(2)}, u32[]{:S(2)}) collective-permute-start(bf16[64,1152]{1,0:T(8,128)(2,1)} %get-tuple-element.66), channel_id=1, source_target_pairs={{0,4},{1,5},{2,6},{3,7},{4,0},{5,1},{6,2},{7,3},{8,12},{9,13},{10,... | collective-permute-start | bytes 442376 | tf_op jit(solution)/shard_map/ppermute | solution.py:386
  179.9 3.8 %collective-permute-start.11 = (bf16[64,1152]{1,0:T(8,128)(2,1)}, bf16[64,1152]{1,0:T(8,128)(2,1)S(1)}, u32[]{:S(2)}, u32[]{:S(2)}) collective-permute-start(bf16[64,1152]{1,0:T(8,128)(2,1)} %get-tuple-element.68), channel_id=1, source_target_pairs={{0,3},{1,4},{2,5},{3,6},{4,7},{5,0},{6,1},{7,2},{8,11},{9,12},{10,... | collective-permute-start | bytes 442376 | tf_op jit(solution)/shard_map/ppermute | solution.py:386
  184.1 2.6 %collective-permute-start.13 = (bf16[64,1152]{1,0:T(8,128)(2,1)S(1)}, bf16[64,1152]{1,0:T(8,128)(2,1)S(1)}, u32[]{:S(2)}, u32[]{:S(2)}) collective-permute-start(bf16[64,1152]{1,0:T(8,128)(2,1)S(1)} %copy-done.26), channel_id=1, source_target_pairs={{0,2},{1,3},{2,4},{3,5},{4,6},{5,7},{6,0},{7,1},{8,10},{9,11},{10,... | collective-permute-start | bytes 442376 | tf_op jit(solution)/shard_map/ppermute | solution.py:386
  186.6 3.5 %collective-permute-done.9.refs_0_ = bf16[64,1152]{1,0:T(8,128)(2,1)S(1)} collective-permute-done((bf16[64,1152]{1,0:T(8,128)(2,1)}, bf16[64,1152]{1,0:T(8,128)(2,1)S(1)}, u32[]{:S(2)}, u32[]{:S(2)}) %collective-permute-start.9) | collective-permute-done | bytes 147488 | tf_op jit(solution)/shard_map/ppermute | solution.py:386
  190.1 6.7 %collective-permute-done.10.refs_1_ = bf16[64,1152]{1,0:T(8,128)(2,1)S(1)} collective-permute-done((bf16[64,1152]{1,0:T(8,128)(2,1)}, bf16[64,1152]{1,0:T(8,128)(2,1)S(1)}, u32[]{:S(2)}, u32[]{:S(2)}) %collective-permute-start.10) | collective-permute-done | bytes 147488 | tf_op jit(solution)/shard_map/ppermute | solution.py:386
  196.8 4.6 %collective-permute-done.11.refs_2_ = bf16[64,1152]{1,0:T(8,128)(2,1)S(1)} collective-permute-done((bf16[64,1152]{1,0:T(8,128)(2,1)}, bf16[64,1152]{1,0:T(8,128)(2,1)S(1)}, u32[]{:S(2)}, u32[]{:S(2)}) %collective-permute-start.11) | collective-permute-done | bytes 147488 | tf_op jit(solution)/shard_map/ppermute | solution.py:386
  202.6 2.3 %final.1 = bf16[64,16384]{1,0:T(8,128)(2,1)} custom-call(s32[2]{0:T(128)S(1)} %copy-done.23, s32[1,64]{1,0:T(1,128)S(1)} %bitcast.23, bf16[512,1792]{1,0:T(8,128)(2,1)S(1)} %bitcast.17, bf16[64,1152]{1,0:T(8,128)(2,1)S(1)} %collective-permute-done.9.refs_0_, bf16[64,1152]{1,0:T(8,128)(2,1)S(1)} %collective-permute-done.10.refs_1_, ...), custom_call_target="tpu_custom_call" | custom-call | flops 469762048 | bytes 4194304 | tf_op jit(solution)/shard_map/final/pallas_call | solution.py:523
  (80 shorter events, 5.8 us)
Async XLA Ops:
  18.9 15.1 %copy-start.29 = (s16[16,4736]{1,0:T(8,128)(2,1)S(1)}, s16[16,4736]{1,0:T(8,128)(2,1)}, u32[]{:S(2)}) copy-start(s16[16,4736]{1,0:T(8,128)(2,1)} %get-tuple-element.40) | copy-start | bytes 454660
  18.9 26.3 %copy-start.28 = (s16[16,4736]{1,0:T(8,128)(2,1)S(1)}, s16[16,4736]{1,0:T(8,128)(2,1)}, u32[]{:S(2)}) copy-start(s16[16,4736]{1,0:T(8,128)(2,1)} %get-tuple-element.44) | copy-start | bytes 454660
  18.9 35.2 %copy-start.27 = (s16[16,4736]{1,0:T(8,128)(2,1)S(1)}, s16[16,4736]{1,0:T(8,128)(2,1)}, u32[]{:S(2)}) copy-start(s16[16,4736]{1,0:T(8,128)(2,1)} %get-tuple-element.45) | copy-start | bytes 454660
  18.9 35.2 %all-to-all-start = ((s16[32,16,1920]{2,1,0:T(8,128)(2,1)}), s16[32,16,1920]{2,1,0:T(8,128)(2,1)S(1)}, u32[]{:S(2)}, u32[]{:S(2)}) async-start(s16[32,16,1920]{2,1,0:T(8,128)(2,1)} %bitcast.24), calls=%async_computation | async-start | bytes 3932160 | tf_op jit(solution)/shard_map/all_to_all | solution.py:381
  26.7 87.4 %reduce-scatter.2.cloned.1.call-start = ((), (), s32[]{:S(2)}) async-start(), calls=%async_computation.5 | async-start | bytes 4128768 | tf_op jit(solution)/shard_map/reduce_scatter | solution.py:445
  26.7 18.5 %collective-permute-start = (s16[16,4736]{1,0:T(8,128)(2,1)S(1)}, s16[16,4736]{1,0:T(8,128)(2,1)S(1)}, u32[]{:S(2)}, u32[]{:S(2)}) collective-permute-start(s16[16,4736]{1,0:T(8,128)(2,1)S(1)} %copy-done.30), channel_id=1, source_target_pairs={{0,4},{1,5},{2,6},{3,7},{4,0},{5,1},{6,2},{7,3},{8,12},{9,13},{10,... | collective-permute-start | bytes 454664 | tf_op jit(solution)/shard_map/ppermute | solution.py:386
  34.0 20.1 %collective-permute-start.1 = (s16[16,4736]{1,0:T(8,128)(2,1)S(1)}, s16[16,4736]{1,0:T(8,128)(2,1)S(1)}, u32[]{:S(2)}, u32[]{:S(2)}) collective-permute-start(s16[16,4736]{1,0:T(8,128)(2,1)S(1)} %copy-done.29), channel_id=1, source_target_pairs={{0,3},{1,4},{2,5},{3,6},{4,7},{5,0},{6,1},{7,2},{8,11},{9,12},{10,... | collective-permute-start | bytes 454664 | tf_op jit(solution)/shard_map/ppermute | solution.py:386
  35.9 25.6 %collective-permute-start.2 = (s16[16,4736]{1,0:T(8,128)(2,1)}, s16[16,4736]{1,0:T(8,128)(2,1)S(1)}, u32[]{:S(2)}, u32[]{:S(2)}) collective-permute-start(s16[16,4736]{1,0:T(8,128)(2,1)} %get-tuple-element.41), channel_id=1, source_target_pairs={{0,5},{1,6},{2,7},{3,0},{4,1},{5,2},{6,3},{7,4},{8,13},{9,14},{10,... | collective-permute-start | bytes 454664 | tf_op jit(solution)/shard_map/ppermute | solution.py:386
  39.0 22.6 %collective-permute-start.3 = (s16[16,4736]{1,0:T(8,128)(2,1)}, s16[16,4736]{1,0:T(8,128)(2,1)S(1)}, u32[]{:S(2)}, u32[]{:S(2)}) collective-permute-start(s16[16,4736]{1,0:T(8,128)(2,1)} %get-tuple-element.42), channel_id=1, source_target_pairs={{0,2},{1,3},{2,4},{3,5},{4,6},{5,7},{6,0},{7,1},{8,10},{9,11},{10,... | collective-permute-start | bytes 454664 | tf_op jit(solution)/shard_map/ppermute | solution.py:386
  40.5 21.1 %collective-permute-start.4 = (s16[16,4736]{1,0:T(8,128)(2,1)}, s16[16,4736]{1,0:T(8,128)(2,1)S(1)}, u32[]{:S(2)}, u32[]{:S(2)}) collective-permute-start(s16[16,4736]{1,0:T(8,128)(2,1)} %get-tuple-element.43), channel_id=1, source_target_pairs={{0,6},{1,7},{2,0},{3,1},{4,2},{5,3},{6,4},{7,5},{8,14},{9,15},{10,... | collective-permute-start | bytes 454664 | tf_op jit(solution)/shard_map/ppermute | solution.py:386
  45.2 16.4 %collective-permute-start.5 = (s16[16,4736]{1,0:T(8,128)(2,1)S(1)}, s16[16,4736]{1,0:T(8,128)(2,1)S(1)}, u32[]{:S(2)}, u32[]{:S(2)}) collective-permute-start(s16[16,4736]{1,0:T(8,128)(2,1)S(1)} %copy-done.28), channel_id=1, source_target_pairs={{0,1},{1,2},{2,3},{3,4},{4,5},{5,6},{6,7},{7,0},{8,9},{9,10},{10,1... | collective-permute-start | bytes 454664 | tf_op jit(solution)/shard_map/ppermute | solution.py:386
  54.1 7.7 %collective-permute-start.6 = (s16[16,4736]{1,0:T(8,128)(2,1)S(1)}, s16[16,4736]{1,0:T(8,128)(2,1)S(1)}, u32[]{:S(2)}, u32[]{:S(2)}) collective-permute-start(s16[16,4736]{1,0:T(8,128)(2,1)S(1)} %copy-done.27), channel_id=1, source_target_pairs={{0,7},{1,0},{2,1},{3,2},{4,3},{5,4},{6,5},{7,6},{8,15},{9,8},{10,9... | collective-permute-start | bytes 454664 | tf_op jit(solution)/shard_map/ppermute | solution.py:386
  61.8 104.0 %all-gather.2.cloned.1.call-start = ((), (), s32[]{:S(2)}) async-start(), calls=%async_computation.6 | async-start | bytes 2064384 | tf_op jit(solution)/shard_map/all_gather | solution.py:489
  67.5 39.0 %copy-start.3 = (f32[128,2048]{1,0:T(8,128)S(1)}, f32[128,2048]{1,0:T(8,128)}, u32[]{:S(2)}) copy-start(f32[128,2048]{1,0:T(8,128)} %refs_0_.3) | copy-start | bytes 3145732
  67.5 39.0 %copy-start.4 = (f32[128,2048]{1,0:T(8,128)S(1)}, f32[128,2048]{1,0:T(8,128)}, u32[]{:S(2)}) copy-start(f32[128,2048]{1,0:T(8,128)} %refs_1_.3) | copy-start | bytes 3145732
  67.5 39.0 %copy-start.5 = (f32[128,2048]{1,0:T(8,128)S(1)}, f32[128,2048]{1,0:T(8,128)}, u32[]{:S(2)}) copy-start(f32[128,2048]{1,0:T(8,128)} %refs_2_.3) | copy-start | bytes 3145732
  117.7 35.2 %copy-start.11 = (s16[16,4736]{1,0:T(8,128)(2,1)S(1)}, s16[16,4736]{1,0:T(8,128)(2,1)}, u32[]{:S(2)}) copy-start(s16[16,4736]{1,0:T(8,128)(2,1)} %copy-done.10) | copy-start | bytes 454660
  117.7 35.2 %copy-start.13 = (s16[16,4736]{1,0:T(8,128)(2,1)S(1)}, s16[16,4736]{1,0:T(8,128)(2,1)}, u32[]{:S(2)}) copy-start(s16[16,4736]{1,0:T(8,128)(2,1)} %copy-done.12) | copy-start | bytes 454660
  117.7 35.2 %copy-start.15 = (s16[16,4736]{1,0:T(8,128)(2,1)S(1)}, s16[16,4736]{1,0:T(8,128)(2,1)}, u32[]{:S(2)}) copy-start(s16[16,4736]{1,0:T(8,128)(2,1)} %copy-done.14) | copy-start | bytes 454660
  117.8 35.2 %copy-start.17 = (s16[16,4736]{1,0:T(8,128)(2,1)S(1)}, s16[16,4736]{1,0:T(8,128)(2,1)}, u32[]{:S(2)}) copy-start(s16[16,4736]{1,0:T(8,128)(2,1)} %copy-done.16) | copy-start | bytes 454660
  117.8 35.2 %copy-start.19 = (s16[16,4736]{1,0:T(8,128)(2,1)S(1)}, s16[16,4736]{1,0:T(8,128)(2,1)}, u32[]{:S(2)}) copy-start(s16[16,4736]{1,0:T(8,128)(2,1)} %copy-done.18) | copy-start | bytes 454660
  117.8 35.2 %copy-start.21 = (s16[16,4736]{1,0:T(8,128)(2,1)S(1)}, s16[16,4736]{1,0:T(8,128)(2,1)}, u32[]{:S(2)}) copy-start(s16[16,4736]{1,0:T(8,128)(2,1)} %copy-done.20) | copy-start | bytes 454660
  117.8 35.2 %copy-start.23 = (s32[2]{0:T(128)S(1)}, s32[2]{0:T(128)}, u32[]{:S(2)}) copy-start(s32[2]{0:T(128)} %pad_add_fusion.me_ref) | copy-start | bytes 28
  156.1 6.3 %collective-permute-start.7 = (bf16[64,1152]{1,0:T(8,128)(2,1)S(1)}, bf16[64,1152]{1,0:T(8,128)(2,1)S(1)}, u32[]{:S(2)}, u32[]{:S(2)}) collective-permute-start(bf16[64,1152]{1,0:T(8,128)(2,1)S(1)} %get-tuple-element.62), channel_id=1, source_target_pairs={{0,7},{1,0},{2,1},{3,2},{4,3},{5,4},{6,5},{7,6},{8,15},{9,8},{10,9... | collective-permute-start | bytes 442376 | tf_op jit(solution)/shard_map/ppermute | solution.py:386
  158.7 7.1 %collective-permute-start.8 = (bf16[64,1152]{1,0:T(8,128)(2,1)S(1)}, bf16[64,1152]{1,0:T(8,128)(2,1)S(1)}, u32[]{:S(2)}, u32[]{:S(2)}) collective-permute-start(bf16[64,1152]{1,0:T(8,128)(2,1)S(1)} %get-tuple-element.63), channel_id=1, source_target_pairs={{0,1},{1,2},{2,3},{3,4},{4,5},{5,6},{6,7},{7,0},{8,9},{9,10},{10,1... | collective-permute-start | bytes 442376 | tf_op jit(solution)/shard_map/ppermute | solution.py:386
  170.8 31.9 %copy-start.24 = (s32[64]{0:T(128)S(1)}, s32[64]{0:T(128)}, u32[]{:S(2)}) copy-start(s32[64]{0:T(128)} %param.8) | copy-start | bytes 772
  170.8 31.9 %all-to-all-start.3 = ((bf16[32,16,1792]{2,1,0:T(8,128)(2,1)}), bf16[32,16,1792]{2,1,0:T(8,128)(2,1)S(1)}, u32[]{:S(2)}, u32[]{:S(2)}) async-start(bf16[32,16,1792]{2,1,0:T(8,128)(2,1)} %bitcast.18), calls=%async_computation.4 | async-start | bytes 3670016 | tf_op jit(solution)/shard_map/all_to_all | solution.py:381
  175.9 14.2 %collective-permute-start.9 = (bf16[64,1152]{1,0:T(8,128)(2,1)}, bf16[64,1152]{1,0:T(8,128)(2,1)S(1)}, u32[]{:S(2)}, u32[]{:S(2)}) collective-permute-start(bf16[64,1152]{1,0:T(8,128)(2,1)} %get-tuple-element.66), channel_id=1, source_target_pairs={{0,4},{1,5},{2,6},{3,7},{4,0},{5,1},{6,2},{7,3},{8,12},{9,13},{10,... | collective-permute-start | bytes 442376 | tf_op jit(solution)/shard_map/ppermute | solution.py:386
  179.9 16.9 %collective-permute-start.10 = (bf16[64,1152]{1,0:T(8,128)(2,1)}, bf16[64,1152]{1,0:T(8,128)(2,1)S(1)}, u32[]{:S(2)}, u32[]{:S(2)}) collective-permute-start(bf16[64,1152]{1,0:T(8,128)(2,1)} %get-tuple-element.67), channel_id=1, source_target_pairs={{0,5},{1,6},{2,7},{3,0},{4,1},{5,2},{6,3},{7,4},{8,13},{9,14},{10,... | collective-permute-start | bytes 442376 | tf_op jit(solution)/shard_map/ppermute | solution.py:386
  179.9 21.5 %collective-permute-start.11 = (bf16[64,1152]{1,0:T(8,128)(2,1)}, bf16[64,1152]{1,0:T(8,128)(2,1)S(1)}, u32[]{:S(2)}, u32[]{:S(2)}) collective-permute-start(bf16[64,1152]{1,0:T(8,128)(2,1)} %get-tuple-element.68), channel_id=1, source_target_pairs={{0,3},{1,4},{2,5},{3,6},{4,7},{5,0},{6,1},{7,2},{8,11},{9,12},{10,... | collective-permute-start | bytes 442376 | tf_op jit(solution)/shard_map/ppermute | solution.py:386
  183.7 18.9 %collective-permute-start.12 = (bf16[64,1152]{1,0:T(8,128)(2,1)}, bf16[64,1152]{1,0:T(8,128)(2,1)S(1)}, u32[]{:S(2)}, u32[]{:S(2)}) collective-permute-start(bf16[64,1152]{1,0:T(8,128)(2,1)} %get-tuple-element.69), channel_id=1, source_target_pairs={{0,6},{1,7},{2,0},{3,1},{4,2},{5,3},{6,4},{7,5},{8,14},{9,15},{10,... | collective-permute-start | bytes 442376 | tf_op jit(solution)/shard_map/ppermute | solution.py:386
  184.1 18.6 %collective-permute-start.13 = (bf16[64,1152]{1,0:T(8,128)(2,1)S(1)}, bf16[64,1152]{1,0:T(8,128)(2,1)S(1)}, u32[]{:S(2)}, u32[]{:S(2)}) collective-permute-start(bf16[64,1152]{1,0:T(8,128)(2,1)S(1)} %copy-done.26), channel_id=1, source_target_pairs={{0,2},{1,3},{2,4},{3,5},{4,6},{5,7},{6,0},{7,1},{8,10},{9,11},{10,... | collective-permute-start | bytes 442376 | tf_op jit(solution)/shard_map/ppermute | solution.py:386
  (17 other events, 72.0 us)
Sparse Core Ops, SparseCore 0:
  61.9 49.7 reduce-scatter.1
  117.8 37.1 all-gather.1
